TPU v7x, 512 devices: a whole 4x4x16 slice. The times are simulated.
512 devices in a mesh: dp: 16 (over z_lo, x), panel: 32 (over y, z_hi, core).
Axes of the slice: x: 4, y: 4, z: 16 (z_hi: 4, z_lo: 4; z = z_hi * 4 + z_lo), core: 2. Of those that a mesh axis runs over, the one named last changes fastest.
Arguments:
- features: bfloat16 [12288, 4096], P('dp', 'panel'), may hold values from -48 to 48
- sketch: float32 [32, 128, 256], P('panel', 'dp'), may hold values from -6 to 6
- counts: int32 [16], replicated, may hold values from 384 to 768, as said below
Outputs:
- covariance: float32 [4096, 16, 256], P('panel', 'dp')
- basis: float32 [32, 128, 256], P('panel', 'dp')
Inputs may be any that keep to these rules, and one draw needn't show every extreme that they name: `counts`: some dp index has all 768 rows live.
All inputs are finite; a program needn't handle non-finite values.
Results may differ from a plain program's by a relative error of at most 0.0003.
Values may be sent and summed in bfloat16 or wider, within the bound.
No kernel may reach another device: no remote copies, remote signals or barrier semaphores. Data moves between devices by JAX's collectives and lax.ppermute only.
A program may use at most 64 MiB of HBM per device.

v0:
```python
import math

import jax
import jax.numpy as jnp
from jax import lax
from jax.sharding import PartitionSpec as P

ITERS = 2


def local(features, sketch, counts):
    dp_count = lax.axis_size("dp")
    panel_count = lax.axis_size("panel")
    tok_rows, feat_width = features.shape
    sub_rows = sketch.shape[1]
    rank_cols = sketch.shape[2]
    total_width = feat_width * panel_count
    limit = counts[lax.axis_index("dp")]
    live_rows = (lax.iota(jnp.int32, tok_rows) < limit).astype(jnp.bfloat16)
    masked = features * live_rows[:, None]
    token_total = jnp.sum(counts).astype(jnp.float32)
    contract = (((0,), (0,)), ((), ()))
    partial_value = lax.dot_general(
        masked,
        lax.all_gather(features, "panel", axis=1, tiled=True),
        contract,
        preferred_element_type=jnp.float32,
    )
    partial_value = partial_value.reshape(feat_width, panel_count, dp_count, sub_rows)
    partial_value = jnp.transpose(partial_value, (0, 2, 1, 3)).reshape(
        feat_width, dp_count, panel_count * sub_rows
    )
    summed = lax.psum_scatter(partial_value, "dp", scatter_dimension=1, tiled=True)
    covariance = summed / token_total
    cov_flat = covariance.reshape(feat_width, panel_count * sub_rows)
    basis_now = sketch[0]
    for sweep in range(ITERS):
        shaped = jnp.dot(
            cov_flat,
            lax.all_gather(basis_now, "panel", axis=0, tiled=True),
            precision=lax.Precision.HIGHEST,
            preferred_element_type=jnp.float32,
        ).reshape(dp_count, sub_rows, rank_cols)
        basis_block = lax.psum_scatter(shaped, "dp", scatter_dimension=0, tiled=True)[0]
        inner_gram = jnp.dot(
            basis_block.T,
            basis_block,
            precision=lax.Precision.HIGHEST,
            preferred_element_type=jnp.float32,
        )
        summed_gram = lax.psum(inner_gram, ("dp", "panel"))
        factor_low = jnp.linalg.cholesky(summed_gram)
        basis_now = jax.scipy.linalg.solve_triangular(factor_low, basis_block.T, lower=True).T
    scaled = (math.sqrt(total_width) * basis_now)[None]
    return (covariance, scaled)


def solution(mesh):
    in_specs = (P("dp", "panel"), P("panel", "dp", None), P())
    out_specs = (P("panel", "dp", None), P("panel", "dp", None))
    return jax.shard_map(local, mesh=mesh, in_specs=in_specs, out_specs=out_specs, check_vma=False)
```

profile of v0, /device:TPU:1, one launch (start us, length us, event | category | flops | bytes accessed | tf_op | source)
XLA Modules:
  0.0 1508.6 jit_solution(8885281473320648278)
XLA Ops:
  7.2 0.0 all-gather.3.cloned.1.call-start
  7.2 0.7 all-gather.3.cloned.1.call-update
  7.9 0.0 reduce-scatter.4.cloned.1.call-start
  7.9 1.2 dynamic_slice.3
  9.2 0.6 fusion.34
  9.9 130.1 %all-gather.3.cloned.1.call-done = bf16[768,4096]{1,0:T(8,128)(2,1)} async-done(((bf16[768,128]{1,0:T(8,128)(2,1)}), bf16[768,4096]{1,0:T(8,128)(2,1)}) %all-gather.3.cloned.1.call-update) | async-done | bytes 6291472 | tf_op jit(solution)/shard_map/all_gather | solution.py:25
  140.0 5.6 fusion.6
  145.6 1.6 copy.31
  147.2 0.0 reduce-scatter.6.cloned.1.call-start
  147.3 0.6 reduce_sum.9
  148.6 50.2 %all-gather = f32[1,256,256]{2,1,0:T(8,128)S(1)} all-gather(f32[1,8,256]{2,1,0:T(8,128)S(1)} %copy-done), channel_id=2, replica_groups=mesh['dp'=16,'panel'=32] {'panel'}, dimensions={1}, use_global_device_ids=true | all-gather | bytes 270336 | tf_op jit(solution)/shard_map/all_gather | solution.py:40
  198.8 24.6 %reduce-scatter.4.cloned.1.call-done = f32[128,1,256]{0,2,1:T(8,128)} async-done(((f32[128,16,256]{0,2,1:T(8,128)}), f32[128,1,256]{0,2,1:T(8,128)}) %reduce-scatter.4.cloned.1.call-update) | async-done | bytes 131088 | tf_op jit(solution)/shard_map/reduce_scatter | solution.py:33
  223.4 0.9 broadcast_divide_fusion
  224.3 0.1 copy.21
  224.4 0.9 fusion.4
  225.4 0.0 all-reduce.4.cloned.1.call-start
  225.4 85.0 %reduce-scatter.6.cloned.1.call-done = f32[1,8,256]{2,1,0:T(8,128)} async-done(((f32[16,8,256]{2,1,0:T(8,128)}), f32[1,8,256]{2,1,0:T(8,128)}) %reduce-scatter.6.cloned.1.call-update) | async-done | bytes 8208 | tf_op jit(solution)/shard_map/reduce_scatter | solution.py:44
  310.4 1.9 fusion.30
  312.3 0.2 reduce-scatter.8.cloned.1.call-start
  312.5 468.1 %all-reduce.4.cloned.1.call-done = f32[256,256]{0,1:T(8,128)} async-done(((f32[256,256]{0,1:T(8,128)}), f32[256,256]{0,1:T(8,128)}) %all-reduce.4.cloned.1.call-update) | async-done | bytes 262160 | tf_op jit(solution)/shard_map/psum | solution.py:51
  780.6 1.1 copy.23
  781.7 1.0 fusion.3
  782.7 11.7 cholesky.130
  794.5 9.8 custom-call.13
  804.3 0.2 constant_dynamic-update-slice_fusion.3
  804.5 0.3 convolution_subtract_fusion.1
  804.8 11.7 cholesky.147
  816.5 0.7 compare_reduce_fusion.2
  818.5 0.1 triangular_solve.75
  818.6 4.1 while.4
  818.7 0.7 fusion.48
  819.3 1.3 bitcast_dynamic-update-slice_fusion.4
  820.7 0.7 fusion.48
  821.4 1.3 bitcast_dynamic-update-slice_fusion.4
  822.7 19.7 %custom-call.14 = f32[2,128,128]{1,2,0:T(8,128)S(1)} custom-call(f32[2,128,128]{2,1,0:T(8,128)S(1)} %get-tuple-element.18), custom_call_target="InvertDiagBlocksLowerTriangular" | custom-call | tf_op jit(solution)/shard_map/jit(_solve_triangular)/triangular_solve | solution.py:53
  842.4 0.8 fusion.18
  843.2 0.9 convolution_subtract_fusion.3
  844.1 0.2 fusion.17
  844.3 54.8 %all_gather.11 = f32[256,256]{1,0:T(8,128)S(1)} all-gather(f32[8,256]{1,0:T(8,128)S(1)} %maximum_bitcast_fusion), channel_id=1, replica_groups=mesh['dp'=16,'panel'=32] {'panel'}, dimensions={0}, use_global_device_ids=true | all-gather | bytes 270336 | tf_op jit(solution)/shard_map/all_gather | solution.py:40
  899.1 0.9 fusion.1
  900.1 0.3 all-reduce.6.cloned.1.call-start
  900.3 66.2 %reduce-scatter.8.cloned.1.call-done = f32[1,8,256]{2,1,0:T(8,128)} async-done(((f32[16,8,256]{2,1,0:T(8,128)}), f32[1,8,256]{2,1,0:T(8,128)}) %reduce-scatter.8.cloned.1.call-update) | async-done | bytes 8208 | tf_op jit(solution)/shard_map/reduce_scatter | solution.py:44
  966.6 1.9 fusion.28
  968.5 0.8 copy.26
  969.3 467.4 %all-reduce.6.cloned.1.call-done = f32[256,256]{0,1:T(8,128)} async-done(((f32[256,256]{0,1:T(8,128)}), f32[256,256]{0,1:T(8,128)}) %all-reduce.6.cloned.1.call-update) | async-done | bytes 262160 | tf_op jit(solution)/shard_map/psum | solution.py:51
  1436.6 1.1 copy.25
  1437.7 1.0 fusion
  1438.7 11.7 cholesky.164
  1450.5 9.8 custom-call.15
  1460.3 0.2 constant_dynamic-update-slice_fusion.1
  1460.5 0.3 convolution_subtract_fusion
  1460.8 11.7 cholesky.181
  1472.6 0.6 compare_reduce_fusion
  1473.2 0.7 compare_reduce_fusion.1
  1475.2 4.3 while.5
  1475.5 0.7 fusion.49
  1476.2 1.3 bitcast_dynamic-update-slice_fusion.5
  1477.5 0.7 fusion.49
  1478.2 1.3 bitcast_dynamic-update-slice_fusion.5
  1479.5 19.7 %custom-call.16 = f32[2,128,128]{1,2,0:T(8,128)S(1)} custom-call(f32[2,128,128]{2,1,0:T(8,128)S(1)} %get-tuple-element.19), custom_call_target="InvertDiagBlocksLowerTriangular" | custom-call | tf_op jit(solution)/shard_map/jit(_solve_triangular)/triangular_solve | solution.py:53
  1499.2 0.8 fusion.13
  1500.1 0.9 convolution_subtract_fusion.2
  1500.9 0.2 fusion.12
  1501.1 0.6 fusion.27
  (27 shorter events, 0.4 us)
Async XLA Ops:
  7.2 132.8 %all-gather.3.cloned.1.call-start = ((), (), s32[]{:S(2)}) async-start(), calls=%async_computation.3 | async-start | bytes 6488064 | tf_op jit(solution)/shard_map/all_gather | solution.py:25
  7.9 215.5 %reduce-scatter.4.cloned.1.call-start = ((), (), s32[]{:S(2)}) async-start(), calls=%async_computation.4 | async-start | bytes 2228224 | tf_op jit(solution)/shard_map/reduce_scatter | solution.py:33
  9.8 137.4 %copy-start.1 = (s32[16]{0:T(128)S(1)}, s32[16]{0:T(128)}, u32[]{:S(2)}) copy-start(s32[16]{0:T(128)} %param.8) | copy-start | bytes 196
  9.9 138.7 %copy-start = (f32[1,8,256]{2,1,0:T(8,128)S(1)}, f32[1,8,256]{2,1,0:T(8,128)}, u32[]{:S(2)}) copy-start(f32[1,8,256]{2,1,0:T(8,128)} %param.7) | copy-start | bytes 24580
  147.2 163.2 %reduce-scatter.6.cloned.1.call-start = ((), (), s32[]{:S(2)}) async-start(), calls=%async_computation.5 | async-start | bytes 139264 | tf_op jit(solution)/shard_map/reduce_scatter | solution.py:44
  225.4 555.3 %all-reduce.4.cloned.1.call-start = ((), (), s32[]{:S(2)}) async-start(), calls=%async_computation.6 | async-start | bytes 524288 | tf_op jit(solution)/shard_map/psum | solution.py:51
  312.3 654.3 %reduce-scatter.8.cloned.1.call-start = ((), (), s32[]{:S(2)}) async-start(), calls=%async_computation.7 | async-start | bytes 139264 | tf_op jit(solution)/shard_map/reduce_scatter | solution.py:44
  900.1 536.6 %all-reduce.6.cloned.1.call-start = ((), (), s32[]{:S(2)}) async-start(), calls=%async_computation.8 | async-start | bytes 524288 | tf_op jit(solution)/shard_map/psum | solution.py:51
Sparse Core Ops, SparseCore 0:
  11.1 128.8 all-gather.2
  147.3 75.9 reduce-scatter.3
  226.7 83.5 reduce-scatter.5
  316.6 464.0 all-reduce.3
  900.2 66.3 reduce-scatter.7
  972.8 463.8 all-reduce.5
where the time goes:
time: 1510 us
  waiting for transfers between devices  1240 us (82%)
  other arithmetic  113 us (7%)
  blocking collectives  105 us (7%)
  between operations  17.5 us (1%)
  matrix products  16.1 us (1%)
    psum x2, waiting for transfers between devices, local(): summed_gram = lax.psum(inner_gram, ('dp', 'panel'))  935 us
    reduce_scatter x2, waiting for transfers between devices, local(): lax.psum_scatter(shaped, 'dp', scatter_dimension=0, tiled=True)[0]  151 us
    all_gather x1, waiting for transfers between devices, local(): lax.all_gather(features, 'panel', axis=1, tiled=True)  130 us
    all_gather x2, blocking collectives, local(): lax.all_gather(basis_now, 'panel', axis=0, tiled=True)  105 us
    another operation x13, other arithmetic, local(): factor_low = jnp.linalg.cholesky(summed_gram)  68.7 us
    another operation x5, other arithmetic, local(): jax.scipy.linalg.solve_triangular(factor_low, basis_block.T, lower=True)  39.4 us
  transfers between devices with their start and end apart: 6, of which 6 were waited for; matrix products, arithmetic and copies ran while one was open for 0% of the time, Pallas kernels for 0%

commit v1 on v0

v1 whole, which is shorter than its diff:
```python
import math

import jax
import jax.numpy as jnp
from jax import lax
from jax.experimental import pallas as pl
from jax.experimental.pallas import tpu as pltpu
from jax.sharding import Mesh, PartitionSpec as P

F32 = jnp.float32
BF16 = jnp.bfloat16
HIGH = lax.Precision.HIGHEST
DP = ("zl", "x")
PANEL = ("y", "zh", "c")
YC = ("y", "c")
STEP = 32


def exchange(blocks, axes):
    return lax.all_to_all(blocks, axes, 0, 0, tiled=True)


def gather(block, axes):
    size = lax.axis_size(axes)
    return exchange(jnp.broadcast_to(block[None], (size,) + block.shape), axes)


def solve_kernel(gram_ref, rows_ref, out_ref, held_ref):
    rank = gram_ref.shape[0]
    width = held_ref.shape[1]
    held_ref[:, 0:rank] = gram_ref[...]
    held_ref[:, rank:width] = rows_ref[...]
    index = lax.broadcasted_iota(jnp.int32, (STEP, 1), 0)
    for first in range(0, rank, STEP):
        left = first // 128 * 128
        panel = held_ref[first : first + STEP, left:width]
        if first > 0:
            panel = panel - lax.dot_general(
                held_ref[0:first, first : first + STEP],
                held_ref[0:first, left:width],
                (((0,), (0,)), ((), ())),
                precision=HIGH,
                preferred_element_type=F32,
            )
        pivots = jnp.ones((STEP, 1), F32)
        for step in range(STEP):
            at = first + step - left
            column = panel[:, at : at + 1]
            pivot = column[step : step + 1, :]
            factor = jnp.where(index > step, column / pivot, 0.0)
            pivots = jnp.where(index == step, pivot, pivots)
            panel = panel - factor * panel[step : step + 1, :]
        held_ref[first : first + STEP, left:width] = panel * (1.0 / jnp.sqrt(pivots))
    out_ref[...] = held_ref[:, rank:width]


def solve(gram, rows):
    count, rank = rows.shape
    padded = jnp.pad(rows.T, ((0, 0), (0, 128 - count)))
    solved = pl.pallas_call(
        solve_kernel,
        out_shape=jax.ShapeDtypeStruct((rank, 128), F32),
        scratch_shapes=[pltpu.VMEM((rank, rank + 128), F32)],
        name="solve",
    )(gram, padded)
    return solved[:, 0:count].T


def local(features, sketch, counts):
    tok_rows, width = features.shape
    sub_rows, rank = sketch.shape[1:]
    n_dp, n_panel = lax.axis_size(DP), lax.axis_size(PANEL)
    n_y, n_zh, n_c = lax.axis_size("y"), lax.axis_size("zh"), lax.axis_size("c")
    limit = counts[lax.axis_index(DP)]
    masked = jnp.where(lax.iota(jnp.int32, tok_rows)[:, None] < limit, features, 0)
    token_total = jnp.sum(counts).astype(F32)

    high = lax.reduce_precision(sketch[0], 8, 7)
    rest = sketch[0] - high
    middle = lax.reduce_precision(rest, 8, 7)
    extra = jnp.stack([high, middle, rest - middle]).astype(BF16).reshape(-1, width)
    extra_rows = extra.shape[0]

    along_z = gather(jnp.concatenate([masked, extra]), ("zh",))
    along_y = gather(
        jnp.concatenate([masked, along_z[:, tok_rows:].reshape(-1, width)]), ("y",)
    )
    along_c = gather(along_y, ("c",))

    thirds = along_c[:, :, tok_rows:].astype(F32)
    thirds = thirds.reshape(n_c, n_y, n_zh, 3, sub_rows, rank)
    start = (thirds[:, :, :, 0] + thirds[:, :, :, 1]) + thirds[:, :, :, 2]
    start = start.transpose(1, 2, 0, 3, 4).reshape(n_panel * sub_rows, rank)

    partial_sums = jnp.einsum(
        "ztf,cyta->zfcya",
        along_z[:, :tok_rows],
        along_c[:, :, :tok_rows],
        preferred_element_type=F32,
    )
    partial_sums = partial_sums.reshape(n_zh, n_dp, sub_rows, n_c, n_y, width)
    partial_sums = partial_sums.transpose(1, 4, 3, 0, 2, 5)
    partial_sums = partial_sums.reshape(n_dp * n_y * n_c, n_zh, sub_rows, width)
    received = exchange(partial_sums, DP + YC)
    received = received.reshape(n_dp, n_y, n_c, n_zh, sub_rows, width)
    columns = jnp.sum(received, axis=0).transpose(0, 2, 1, 3, 4)
    columns = columns.reshape(n_panel * sub_rows, width) / token_total
    covariance = columns.T.reshape(width, 1, n_panel * sub_rows)

    product = lax.dot_general(
        columns, start, (((0,), (0,)), ((), ())), precision=HIGH, preferred_element_type=F32
    )
    product = jnp.sum(exchange(product.reshape(n_dp, sub_rows, rank), DP), axis=0)
    product = gather(product, DP).reshape(width, rank)
    product = jnp.dot(columns, product, precision=HIGH, preferred_element_type=F32)
    rows = jnp.sum(exchange(product.reshape(n_panel, sub_rows, rank), PANEL), axis=0)

    group = gather(rows, PANEL).reshape(n_panel * sub_rows, rank)
    gram = lax.dot_general(
        group, group, (((0,), (0,)), ((), ())), precision=HIGH, preferred_element_type=F32
    )
    gram = jnp.sum(exchange(gram.reshape(n_dp, -1, rank), DP), axis=0)
    gram = gather(gram, DP).reshape(rank, rank)
    basis = math.sqrt(width * n_panel) * solve(gram, rows)
    return covariance, basis[None]


def solution(mesh):
    inner = Mesh(mesh.devices.reshape(4, 4, 4, 4, 2), DP + PANEL)
    return jax.shard_map(
        local,
        mesh=inner,
        in_specs=(P(DP, PANEL), P(PANEL, DP, None), P()),
        out_specs=(P(PANEL, DP, None), P(PANEL, DP, None)),
        check_vma=False,
    )
```

time: 1510 us -> 288 us (0.19)
  waiting for transfers between devices: 1240 us -> 54.6 us
  other arithmetic: 113 us -> 6.51 us
  blocking collectives: 105 us -> 171 us
  Pallas kernels: 0 us -> 25.7 us
  between operations: 17.5 us -> 1.49 us
  starting transfers between devices: 0.64 us -> 15.9 us
    psum x2 -> x0, waiting for transfers between devices: 935 us -> none  [local(): summed_gram = lax.psum(inner_gram, ('dp', 'panel'))]
    reduce_scatter x3 -> x0, waiting for transfers between devices: 176 us -> none  [the longest x2 151 us: local(): lax.psum_scatter(shaped, 'dp', scatter_dimension=0, tiled=True)[0]]
    all_to_all x0 -> x8, blocking collectives: none -> 171 us  [exchange(): return lax.all_to_all(blocks, axes, 0, 0, tiled=True)]
    all_gather x1 -> x0, waiting for transfers between devices: 130 us -> none  [local(): lax.all_gather(features, 'panel', axis=1, tiled=True)]
    another operation x18 -> x2, other arithmetic: 108 us -> 0.71 us  [the longest x13 68.7 us: local(): factor_low = jnp.linalg.cholesky(summed_gram)]
    all_gather x2 -> x0, blocking collectives: 105 us -> none  [local(): lax.all_gather(basis_now, 'panel', axis=0, tiled=True)]
    all_to_all x0 -> x2, waiting for transfers between devices: none -> 54.6 us  [exchange(): return lax.all_to_all(blocks, axes, 0, 0, tiled=True)]
    pallas_call x0 -> x1, Pallas kernels: none -> 25.7 us  [solve(): pl.pallas_call(solve_kernel, out_shape=jax.ShapeDtypeStruct((rank, 128),...]
  transfers between devices with their start and end apart: 6 -> 2, of which waited for: 6 -> 2; matrix products, arithmetic and copies ran while one was open for 0% -> 2% of each run, Pallas kernels for 0% -> 0%
where the time goes in v1:
time: 288 us; the launch traced here: 286 us
  blocking collectives  171 us (59%)
  waiting for transfers between devices  54.6 us (19%)
  Pallas kernels  25.7 us (9%)
  starting transfers between devices  15.9 us (6%)
  local copies, waits for them, and re-layouts  8.69 us (3%)
  other arithmetic  6.51 us (2%)
    all_to_all x8, blocking collectives, exchange(): return lax.all_to_all(blocks, axes, 0, 0, tiled=True)  171 us
    all_to_all x2, waiting for transfers between devices, exchange(): return lax.all_to_all(blocks, axes, 0, 0, tiled=True)  54.6 us
    pallas_call x1, Pallas kernels, solve(): pl.pallas_call(solve_kernel, out_shape=jax.ShapeDtypeStruct((rank, 128),...  25.7 us
    all_to_all x2, starting transfers between devices, exchange(): return lax.all_to_all(blocks, axes, 0, 0, tiled=True)  15.9 us
  transfers between devices with their start and end apart: 2, of which 2 were waited for; matrix products, arithmetic and copies ran while one was open for 2% of the time, Pallas kernels for 0%

profile of v1, /device:TPU:1, one launch (start us, length us, event | category | flops | bytes accessed | tf_op | source)
XLA Modules:
  0.0 286.1 jit_solution(18365984220443220674)
XLA Ops:
  0.6 1.2 dynamic_slice.3
  1.9 0.6 iota_compare_fusion
  2.5 0.7 reduce-precision_convert_fusion.1
  3.3 1.1 broadcast_select_fusion
  4.4 0.1 broadcast_in_dim.28
  4.5 55.5 %all_to_all.50 = bf16[4,816,128]{2,1,0:T(8,128)(2,1)S(1)} all-to-all(bf16[4,816,128]{2,1,0:T(8,128)(2,1)S(1)} %broadcast_in_dim.28), channel_id=1, replica_groups=mesh['zl'=4,'x'=4,'y'=4,'zh'=4,'c'=2] {'zh'}, dimensions={0} | all-to-all | bytes 1671168 | tf_op jit(solution)/shard_map/all_to_all | solution.py:20
  60.1 0.1 broadcast_in_dim.29
  60.2 16.5 %all_to_all.51 = bf16[4,960,128]{2,1,0:T(8,128)(2,1)S(1)} all-to-all(bf16[4,960,128]{2,1,0:T(8,128)(2,1)S(1)} %broadcast_in_dim.29), channel_id=1, replica_groups=mesh['zl'=4,'x'=4,'y'=4,'zh'=4,'c'=2] {'y'}, dimensions={0} | all-to-all | bytes 1966080 | tf_op jit(solution)/shard_map/all_to_all | solution.py:20
  76.7 0.3 broadcast_in_dim.30
  76.9 7.8 %all_to_all.52 = bf16[2,4,960,128]{3,2,1,0:T(8,128)(2,1)S(1)} all-to-all(bf16[2,4,960,128]{3,2,1,0:T(8,128)(2,1)S(1)} %broadcast_in_dim.30), channel_id=1, replica_groups=mesh['zl'=4,'x'=4,'y'=4,'zh'=4,'c'=2] {'c'}, dimensions={0} | all-to-all | bytes 3932160 | tf_op jit(solution)/shard_map/all_to_all | solution.py:20
  84.7 0.0 copy-start
  84.7 1.0 convolution_bitcast_fusion
  85.8 0.2 copy-done
  86.0 1.6 copy.39
  87.6 0.0 copy-start.2
  87.6 11.8 %all-to-all-start.3 = ((f32[128,4,8,128]{3,2,1,0:T(8,128)}), f32[128,4,8,128]{3,2,1,0:T(8,128)S(1)}, u32[]{:S(2)}, u32[]{:S(2)}) async-start(f32[128,4,8,128]{3,2,1,0:T(8,128)} %bitcast.60), calls=%async_computation.3 | async-start | bytes 4194304 | tf_op jit(solution)/shard_map/all_to_all | solution.py:20
  99.5 0.0 copy-done.2
  99.5 0.6 reduce_sum.46
  100.8 1.1 slice_convert_fusion
  101.8 1.1 reshape.76
  103.0 1.2 fusion
  104.2 47.3 %all-to-all-done.3 = f32[128,4,8,128]{3,2,1,0:T(8,128)S(1)} async-done(((f32[128,4,8,128]{3,2,1,0:T(8,128)}), f32[128,4,8,128]{3,2,1,0:T(8,128)S(1)}, u32[]{:S(2)}, u32[]{:S(2)}) %all-to-all-start.3) | async-done | bytes 2097184 | tf_op jit(solution)/shard_map/all_to_all | solution.py:20
  151.5 0.2 reduce_sum.45
  151.7 0.1 copy.42
  151.8 0.3 fusion.6
  152.1 10.4 %all_to_all.53 = f32[16,8,256]{2,1,0:T(8,128)S(1)} all-to-all(f32[16,8,256]{2,1,0:T(8,128)S(1)} %fusion.6), channel_id=1, replica_groups=mesh['zl'=4,'x'=4,'y'=4,'zh'=4,'c'=2] {'zl','x'}, dimensions={0} | all-to-all | bytes 262144 | tf_op jit(solution)/shard_map/all_to_all | solution.py:20
  162.6 10.5 %all_to_all.54 = f32[16,8,256]{2,1,0:T(8,128)S(1)} all-to-all(f32[16,8,256]{2,1,0:T(8,128)S(1)} %broadcast_in_dim.31), channel_id=1, replica_groups=mesh['zl'=4,'x'=4,'y'=4,'zh'=4,'c'=2] {'zl','x'}, dimensions={0} | all-to-all | bytes 262144 | tf_op jit(solution)/shard_map/all_to_all | solution.py:20
  173.1 0.4 fusion.4
  173.4 28.1 %all_to_all.55 = f32[32,8,256]{2,1,0:T(8,128)S(1)} all-to-all(f32[32,8,256]{2,1,0:T(8,128)S(1)} %fusion.4), channel_id=1, replica_groups=mesh['zl'=4,'x'=4,'y'=4,'zh'=4,'c'=2] {'y','zh','c'}, dimensions={0} | all-to-all | bytes 524288 | tf_op jit(solution)/shard_map/all_to_all | solution.py:20
  201.6 26.1 %all_to_all.56 = f32[32,8,256]{2,1,0:T(8,128)S(1)} all-to-all(f32[32,8,256]{2,1,0:T(8,128)S(1)} %broadcast_in_dim.32), channel_id=1, replica_groups=mesh['zl'=4,'x'=4,'y'=4,'zh'=4,'c'=2] {'y','zh','c'}, dimensions={0} | all-to-all | bytes 524288 | tf_op jit(solution)/shard_map/all_to_all | solution.py:20
  227.7 0.1 copy.44
  227.8 0.4 fusion.1
  228.2 16.3 %all_to_all.57 = f32[16,16,256]{2,1,0:T(8,128)S(1)} all-to-all(f32[16,16,256]{2,1,0:T(8,128)S(1)} %fusion.1), channel_id=1, replica_groups=mesh['zl'=4,'x'=4,'y'=4,'zh'=4,'c'=2] {'zl','x'}, dimensions={0} | all-to-all | bytes 524288 | tf_op jit(solution)/shard_map/all_to_all | solution.py:20
  244.5 0.7 broadcast_in_dim.33
  245.3 4.0 %all-to-all-start.9 = ((f32[16,16,256]{2,1,0:T(8,128)}), f32[16,16,256]{2,1,0:T(8,128)S(1)}, u32[]{:S(2)}, u32[]{:S(2)}) async-start(f32[16,16,256]{2,1,0:T(8,128)} %broadcast_in_dim.33), calls=%async_computation.9 | async-start | bytes 524288 | tf_op jit(solution)/shard_map/all_to_all | solution.py:20
  249.3 0.8 copy.46
  250.0 0.1 copy.45
  250.2 0.7 pad.4.rows_ref
  250.8 7.3 %all-to-all-done.9 = f32[16,16,256]{2,1,0:T(8,128)S(1)} async-done(((f32[16,16,256]{2,1,0:T(8,128)}), f32[16,16,256]{2,1,0:T(8,128)S(1)}, u32[]{:S(2)}, u32[]{:S(2)}) %all-to-all-start.9) | async-done | bytes 262176 | tf_op jit(solution)/shard_map/all_to_all | solution.py:20
  258.1 0.0 copy-start.1
  258.1 0.7 copy-done.1
  258.8 25.7 %solve.1 = f32[256,128]{1,0:T(8,128)} custom-call(f32[256,256]{1,0:T(8,128)} %bitcast.66, f32[256,128]{1,0:T(8,128)} %pad.4.rows_ref), custom_call_target="tpu_custom_call" | custom-call | tf_op jit(solution)/shard_map/solve/pallas_call | solution.py:60
  284.5 0.9 fusion.3
  285.5 0.7 copy.47
  (13 shorter events, 0.2 us)
Async XLA Ops:
  84.7 1.3 copy-start
  87.6 11.9 %copy-start.2 = (s32[16]{0:T(128)S(1)}, s32[16]{0:T(128)}, u32[]{:S(2)}) copy-start(s32[16]{0:T(128)} %param.5) | copy-start | bytes 196
  87.6 63.9 %all-to-all-start.3 = ((f32[128,4,8,128]{3,2,1,0:T(8,128)}), f32[128,4,8,128]{3,2,1,0:T(8,128)S(1)}, u32[]{:S(2)}, u32[]{:S(2)}) async-start(f32[128,4,8,128]{3,2,1,0:T(8,128)} %bitcast.60), calls=%async_computation.3 | async-start | bytes 4194304 | tf_op jit(solution)/shard_map/all_to_all | solution.py:20
  245.3 12.9 %all-to-all-start.9 = ((f32[16,16,256]{2,1,0:T(8,128)}), f32[16,16,256]{2,1,0:T(8,128)S(1)}, u32[]{:S(2)}, u32[]{:S(2)}) async-start(f32[16,16,256]{2,1,0:T(8,128)} %broadcast_in_dim.33), calls=%async_computation.9 | async-start | bytes 524288 | tf_op jit(solution)/shard_map/all_to_all | solution.py:20
  258.1 0.7 copy-start.1

commit v2 on v1

--- a/solution.py
+++ b/solution.py
@@ -8,12 +8,13 @@
 from jax.sharding import Mesh, PartitionSpec as P
 
 F32 = jnp.float32
-BF16 = jnp.bfloat16
 HIGH = lax.Precision.HIGHEST
 DP = ("zl", "x")
 PANEL = ("y", "zh", "c")
 YC = ("y", "c")
+XYC = ("x", "y", "c")
 STEP = 32
+PAD_ROWS = 24
 
 
 def exchange(blocks, axes):
@@ -70,40 +71,24 @@
     tok_rows, width = features.shape
     sub_rows, rank = sketch.shape[1:]
     n_dp, n_panel = lax.axis_size(DP), lax.axis_size(PANEL)
-    n_y, n_zh, n_c = lax.axis_size("y"), lax.axis_size("zh"), lax.axis_size("c")
+    n_zl, n_x, n_y, n_zh, n_c = (lax.axis_size(name) for name in DP + PANEL)
     limit = counts[lax.axis_index(DP)]
     masked = jnp.where(lax.iota(jnp.int32, tok_rows)[:, None] < limit, features, 0)
     token_total = jnp.sum(counts).astype(F32)
 
-    high = lax.reduce_precision(sketch[0], 8, 7)
-    rest = sketch[0] - high
-    middle = lax.reduce_precision(rest, 8, 7)
-    extra = jnp.stack([high, middle, rest - middle]).astype(BF16).reshape(-1, width)
-    extra_rows = extra.shape[0]
+    along_z = gather(features, ("zh",))
+    across = lax.all_gather(masked, YC)
+    wide = jnp.pad(sketch[0], ((0, PAD_ROWS), (0, 0)))
+    start = lax.all_gather(wide, PANEL)[:, 0:sub_rows].reshape(n_panel * sub_rows, rank)
 
-    along_z = gather(jnp.concatenate([masked, extra]), ("zh",))
-    along_y = gather(
-        jnp.concatenate([masked, along_z[:, tok_rows:].reshape(-1, width)]), ("y",)
-    )
-    along_c = gather(along_y, ("c",))
-
-    thirds = along_c[:, :, tok_rows:].astype(F32)
-    thirds = thirds.reshape(n_c, n_y, n_zh, 3, sub_rows, rank)
-    start = (thirds[:, :, :, 0] + thirds[:, :, :, 1]) + thirds[:, :, :, 2]
-    start = start.transpose(1, 2, 0, 3, 4).reshape(n_panel * sub_rows, rank)
-
-    partial_sums = jnp.einsum(
-        "ztf,cyta->zfcya",
-        along_z[:, :tok_rows],
-        along_c[:, :, :tok_rows],
-        preferred_element_type=F32,
-    )
-    partial_sums = partial_sums.reshape(n_zh, n_dp, sub_rows, n_c, n_y, width)
-    partial_sums = partial_sums.transpose(1, 4, 3, 0, 2, 5)
-    partial_sums = partial_sums.reshape(n_dp * n_y * n_c, n_zh, sub_rows, width)
-    received = exchange(partial_sums, DP + YC)
-    received = received.reshape(n_dp, n_y, n_c, n_zh, sub_rows, width)
-    columns = jnp.sum(received, axis=0).transpose(0, 2, 1, 3, 4)
+    sums = jnp.einsum("ztf,pta->zfpa", along_z, across, preferred_element_type=F32)
+    sums = sums.reshape(n_zh, n_zl, n_x, sub_rows, n_y * n_c, width)
+    sums = sums.transpose(2, 4, 1, 0, 3, 5)
+    sums = sums.reshape(n_x * n_y * n_c, n_zl, n_zh, sub_rows, width)
+    sums = exchange(sums, XYC).reshape(n_x, n_y * n_c, n_zl, n_zh, sub_rows, width)
+    sums = jnp.sum(sums, axis=0).transpose(1, 0, 2, 3, 4)
+    sums = jnp.sum(exchange(sums, ("zl",)), axis=0)
+    columns = sums.reshape(n_y, n_c, n_zh, sub_rows, width).transpose(0, 2, 1, 3, 4)
     columns = columns.reshape(n_panel * sub_rows, width) / token_total
     covariance = columns.T.reshape(width, 1, n_panel * sub_rows)
 

time: 288 us -> 307 us (1.066)
  blocking collectives: 171 us -> 151 us
  waiting for transfers between devices: 54.6 us -> 74.3 us
  between operations: 1.49 us -> 16.3 us
  starting transfers between devices: 15.9 us -> 20.6 us
    all_gather x0 -> x2, waiting for transfers between devices: none -> 26.7 us  [the longest x1 26.7 us: local(): lax.all_gather(wide, PANEL)[:, 0:sub_rows].reshape(n_panel * sub_rows, rank)]
    all_to_all x8 -> x6, blocking collectives: 171 us -> 151 us  [exchange(): return lax.all_to_all(blocks, axes, 0, 0, tiled=True)]
    all_to_all x2 -> x3, waiting for transfers between devices: 54.6 us -> 47.6 us  [exchange(): return lax.all_to_all(blocks, axes, 0, 0, tiled=True)]
    all_to_all x2 -> x3, starting transfers between devices: 15.9 us -> 20.5 us  [exchange(): return lax.all_to_all(blocks, axes, 0, 0, tiled=True)]
  transfers between devices with their start and end apart: 2 -> 5, of which waited for: 2 -> 4; matrix products, arithmetic and copies ran while one was open for 2% -> 2% of each run, Pallas kernels for 0% -> 0%
where the time goes in v2:
time: 307 us; the launch traced here: 306 us
  blocking collectives  151 us (49%)
  waiting for transfers between devices  74.3 us (24%)
  Pallas kernels  25.7 us (8%)
  starting transfers between devices  20.6 us (7%)
  between operations  16.3 us (5%)
  local copies, waits for them, and re-layouts  9.34 us (3%)
  matrix products  4.35 us (1%)
  other arithmetic  4.34 us (1%)
    all_to_all x6, blocking collectives, exchange(): return lax.all_to_all(blocks, axes, 0, 0, tiled=True)  151 us
    all_to_all x3, waiting for transfers between devices, exchange(): return lax.all_to_all(blocks, axes, 0, 0, tiled=True)  47.6 us
    all_gather x1, waiting for transfers between devices, local(): lax.all_gather(wide, PANEL)[:, 0:sub_rows].reshape(n_panel * sub_rows, rank)  26.7 us
    pallas_call x1, Pallas kernels, solve(): pl.pallas_call(solve_kernel, out_shape=jax.ShapeDtypeStruct((rank, 128),...  25.7 us
    all_to_all x3, starting transfers between devices, exchange(): return lax.all_to_all(blocks, axes, 0, 0, tiled=True)  20.5 us
  transfers between devices with their start and end apart: 5, of which 4 were waited for; matrix products, arithmetic and copies ran while one was open for 2% of the time, Pallas kernels for 0%

profile of v2, /device:TPU:1, one launch (start us, length us, event | category | flops | bytes accessed | tf_op | source)
XLA Modules:
  0.0 305.7 jit_solution(13121621782462995514)
XLA Ops:
  8.0 0.0 all-gather.5.cloned.1.call-start
  8.0 1.2 dynamic_slice.3
  9.3 0.6 iota_compare_fusion
  9.9 1.8 broadcast_select_fusion
  11.7 0.0 all-gather.5.cloned.1.call-update
  11.7 1.1 copy.36
  12.8 0.1 broadcast_in_dim.24
  12.9 53.4 %all_to_all.45 = bf16[4,768,128]{1,2,0:T(8,128)(2,1)S(1)} all-to-all(bf16[4,768,128]{1,2,0:T(8,128)(2,1)S(1)} %broadcast_in_dim.24), channel_id=1, replica_groups=mesh['zl'=4,'x'=4,'y'=4,'zh'=4,'c'=2] {'zh'}, dimensions={0} | all-to-all | bytes 1572864 | tf_op jit(solution)/shard_map/all_to_all | solution.py:21
  66.3 0.0 all-gather.5.cloned.1.call-done
  66.3 2.4 fusion
  68.7 1.6 copy.37
  70.3 0.0 copy-start.1
  70.3 8.4 %all-to-all-start.1 = ((f32[32,4,4,8,128]{4,3,2,1,0:T(8,128)}), f32[32,4,4,8,128]{4,3,2,1,0:T(8,128)S(1)}, u32[]{:S(2)}, u32[]{:S(2)}) async-start(f32[32,4,4,8,128]{4,3,2,1,0:T(8,128)} %bitcast.59), calls=%async_computation.1 | async-start | bytes 4194304 | tf_op jit(solution)/shard_map/all_to_all | solution.py:21
  78.7 0.0 all-gather.7.cloned.1.call-start
  78.8 0.0 copy-done.1
  78.8 0.6 pad.8
  79.4 0.0 all-gather.7.cloned.1.call-update
  79.4 27.6 %all-to-all-done.1 = f32[32,4,4,8,128]{4,3,2,1,0:T(8,128)S(1)} async-done(((f32[32,4,4,8,128]{4,3,2,1,0:T(8,128)}), f32[32,4,4,8,128]{4,3,2,1,0:T(8,128)S(1)}, u32[]{:S(2)}, u32[]{:S(2)}) %all-to-all-start.1) | async-done | bytes 2097184 | tf_op jit(solution)/shard_map/all_to_all | solution.py:21
  107.0 0.0 copy-start.2
  107.0 0.2 reduce_sum.54
  107.3 0.8 copy.38
  108.1 8.1 %all-to-all-start.2 = ((f32[4,8,4,8,128]{4,3,2,1,0:T(8,128)}), f32[4,8,4,8,128]{4,3,2,1,0:T(8,128)S(1)}, u32[]{:S(2)}, u32[]{:S(2)}) async-start(f32[4,8,4,8,128]{4,3,2,1,0:T(8,128)} %copy.38), calls=%async_computation.2 | async-start | bytes 1048576 | tf_op jit(solution)/shard_map/all_to_all | solution.py:21
  116.2 0.0 copy-done.2
  116.2 0.6 reduce_sum.56
  117.5 12.7 %all-to-all-done.2 = f32[4,8,4,8,128]{4,3,2,1,0:T(8,128)S(1)} async-done(((f32[4,8,4,8,128]{4,3,2,1,0:T(8,128)}), f32[4,8,4,8,128]{4,3,2,1,0:T(8,128)S(1)}, u32[]{:S(2)}, u32[]{:S(2)}) %all-to-all-start.2) | async-done | bytes 524320 | tf_op jit(solution)/shard_map/all_to_all | solution.py:21
  130.3 0.1 copy.41
  130.4 26.7 %all-gather.7.cloned.1.call-done = f32[1024,256]{1,0:T(8,128)} async-done(((f32[32,256]{1,0:T(8,128)}), f32[1024,256]{1,0:T(8,128)}) %all-gather.7.cloned.1.call-update) | async-done | bytes 1048592 | tf_op jit(solution)/shard_map/all_gather | solution.py:82
  157.1 1.2 fusion.2
  158.3 12.2 %all_to_all.46 = f32[16,8,256]{2,1,0:T(8,128)S(1)} all-to-all(f32[16,8,256]{2,1,0:T(8,128)S(1)} %fusion.2), channel_id=1, replica_groups=mesh['zl'=4,'x'=4,'y'=4,'zh'=4,'c'=2] {'zl','x'}, dimensions={0} | all-to-all | bytes 262144 | tf_op jit(solution)/shard_map/all_to_all | solution.py:21
  170.5 11.2 %all_to_all.47 = f32[16,8,256]{2,1,0:T(8,128)S(1)} all-to-all(f32[16,8,256]{2,1,0:T(8,128)S(1)} %broadcast_in_dim.25), channel_id=1, replica_groups=mesh['zl'=4,'x'=4,'y'=4,'zh'=4,'c'=2] {'zl','x'}, dimensions={0} | all-to-all | bytes 262144 | tf_op jit(solution)/shard_map/all_to_all | solution.py:21
  181.8 0.4 fusion.6
  182.1 31.5 %all_to_all.48 = f32[32,8,256]{2,1,0:T(8,128)S(1)} all-to-all(f32[32,8,256]{2,1,0:T(8,128)S(1)} %fusion.6), channel_id=1, replica_groups=mesh['zl'=4,'x'=4,'y'=4,'zh'=4,'c'=2] {'y','zh','c'}, dimensions={0} | all-to-all | bytes 524288 | tf_op jit(solution)/shard_map/all_to_all | solution.py:21
  213.7 26.1 %all_to_all.49 = f32[32,8,256]{2,1,0:T(8,128)S(1)} all-to-all(f32[32,8,256]{2,1,0:T(8,128)S(1)} %broadcast_in_dim.44), channel_id=1, replica_groups=mesh['zl'=4,'x'=4,'y'=4,'zh'=4,'c'=2] {'y','zh','c'}, dimensions={0} | all-to-all | bytes 524288 | tf_op jit(solution)/shard_map/all_to_all | solution.py:21
  239.8 0.1 copy.42
  240.0 0.4 fusion.3
  240.3 16.3 %all_to_all.50 = f32[16,16,256]{2,1,0:T(8,128)S(1)} all-to-all(f32[16,16,256]{2,1,0:T(8,128)S(1)} %fusion.3), channel_id=1, replica_groups=mesh['zl'=4,'x'=4,'y'=4,'zh'=4,'c'=2] {'zl','x'}, dimensions={0} | all-to-all | bytes 524288 | tf_op jit(solution)/shard_map/all_to_all | solution.py:21
  256.7 0.7 broadcast_in_dim.45
  257.4 4.0 %all-to-all-start.8 = ((f32[16,16,256]{2,1,0:T(8,128)}), f32[16,16,256]{2,1,0:T(8,128)S(1)}, u32[]{:S(2)}, u32[]{:S(2)}) async-start(f32[16,16,256]{2,1,0:T(8,128)} %broadcast_in_dim.45), calls=%async_computation.8 | async-start | bytes 524288 | tf_op jit(solution)/shard_map/all_to_all | solution.py:21
  261.4 0.8 copy.44
  262.2 0.1 copy.43
  262.3 0.7 pad.9.rows_ref
  263.0 7.3 %all-to-all-done.8 = f32[16,16,256]{2,1,0:T(8,128)S(1)} async-done(((f32[16,16,256]{2,1,0:T(8,128)}), f32[16,16,256]{2,1,0:T(8,128)S(1)}, u32[]{:S(2)}, u32[]{:S(2)}) %all-to-all-start.8) | async-done | bytes 262176 | tf_op jit(solution)/shard_map/all_to_all | solution.py:21
  270.2 0.0 copy-start
  270.2 0.7 copy-done
  270.9 25.7 %solve.1 = f32[256,128]{1,0:T(8,128)} custom-call(f32[256,256]{1,0:T(8,128)} %bitcast.67, f32[256,128]{1,0:T(8,128)} %pad.9.rows_ref), custom_call_target="tpu_custom_call" | custom-call | tf_op jit(solution)/shard_map/solve/pallas_call | solution.py:61
  296.7 0.9 fusion.5
  297.6 0.7 copy.45
  (8 shorter events, 0.2 us)
Async XLA Ops:
  8.0 58.3 %all-gather.5.cloned.1.call-start = ((), (), s32[]{:S(2)}) async-start(), calls=%async_computation.9 | async-start | bytes 1769472 | tf_op jit(solution)/shard_map/all_gather | solution.py:80
  70.3 8.5 %copy-start.1 = (f32[1,8,256]{2,1,0:T(8,128)S(1)}, f32[1,8,256]{2,1,0:T(8,128)}, u32[]{:S(2)}) copy-start(f32[1,8,256]{2,1,0:T(8,128)} %param.4) | copy-start | bytes 24580
  70.3 36.7 %all-to-all-start.1 = ((f32[32,4,4,8,128]{4,3,2,1,0:T(8,128)}), f32[32,4,4,8,128]{4,3,2,1,0:T(8,128)S(1)}, u32[]{:S(2)}, u32[]{:S(2)}) async-start(f32[32,4,4,8,128]{4,3,2,1,0:T(8,128)} %bitcast.59), calls=%async_computation.1 | async-start | bytes 4194304 | tf_op jit(solution)/shard_map/all_to_all | solution.py:21
  78.7 78.3 %all-gather.7.cloned.1.call-start = ((), (), s32[]{:S(2)}) async-start(), calls=%async_computation.10 | async-start | bytes 1081344 | tf_op jit(solution)/shard_map/all_gather | solution.py:82
  107.0 9.2 %copy-start.2 = (s32[16]{0:T(128)S(1)}, s32[16]{0:T(128)}, u32[]{:S(2)}) copy-start(s32[16]{0:T(128)} %param.5) | copy-start | bytes 196
  108.1 22.1 %all-to-all-start.2 = ((f32[4,8,4,8,128]{4,3,2,1,0:T(8,128)}), f32[4,8,4,8,128]{4,3,2,1,0:T(8,128)S(1)}, u32[]{:S(2)}, u32[]{:S(2)}) async-start(f32[4,8,4,8,128]{4,3,2,1,0:T(8,128)} %copy.38), calls=%async_computation.2 | async-start | bytes 1048576 | tf_op jit(solution)/shard_map/all_to_all | solution.py:21
  257.4 12.9 %all-to-all-start.8 = ((f32[16,16,256]{2,1,0:T(8,128)}), f32[16,16,256]{2,1,0:T(8,128)S(1)}, u32[]{:S(2)}, u32[]{:S(2)}) async-start(f32[16,16,256]{2,1,0:T(8,128)} %broadcast_in_dim.45), calls=%async_computation.8 | async-start | bytes 524288 | tf_op jit(solution)/shard_map/all_to_all | solution.py:21
  270.2 0.7 copy-start
Sparse Core Ops, SparseCore 0:
  11.9 37.9 all-gather.4
Sparse Core Ops, SparseCore 1:
  82.9 74.1 all-gather.6

commit v3 on v2

v3 whole, which is shorter than its diff:
```python
import math

import jax
import jax.numpy as jnp
from jax import lax
from jax.experimental import pallas as pl
from jax.experimental.pallas import tpu as pltpu
from jax.sharding import Mesh, PartitionSpec as P

F32 = jnp.float32
BF16 = jnp.bfloat16
HIGH = lax.Precision.HIGHEST
DP = ("zl", "x")
PANEL = ("y", "zh", "c")
YC = ("y", "c")
XYC = ("x", "y", "c")
PANEL_STEP = 64
BLOCK = 8
PAD_ROWS = 512


def exchange(blocks, axes):
    return lax.all_to_all(blocks, axes, 0, 0, tiled=True)


def gather(block, axes):
    size = lax.axis_size(axes)
    return exchange(jnp.broadcast_to(block[None], (size,) + block.shape), axes)


def solve_kernel(gram_ref, rows_ref, out_ref, held_ref):
    rank, lanes = rows_ref.shape
    width = held_ref.shape[1]
    held_ref[:, 0:rank] = gram_ref[...]
    held_ref[:, rank:width] = rows_ref[...]
    for first in range(0, rank, PANEL_STEP):
        last = first + PANEL_STEP
        parts = {}
        for at in range(first // lanes * lanes, width, lanes):
            parts[at] = held_ref[first:last, at : at + lanes]
            if first > 0:
                parts[at] = parts[at] - lax.dot_general(
                    held_ref[0:first, first:last],
                    held_ref[0:first, at : at + lanes],
                    (((0,), (0,)), ((), ())),
                    precision=HIGH,
                    preferred_element_type=F32,
                )
        for pivot in range(first, last, BLOCK):
            base = pivot // lanes * lanes
            parts = {at: part for at, part in parts.items() if at >= base}
            source, lane = parts[base], pivot - base
            columns = [
                jnp.broadcast_to(source[:, lane + j : lane + j + 1], source.shape)
                for j in range(BLOCK)
            ]
            square = [[columns[j][i : i + 1] for j in range(i + 1)] for i in range(BLOCK)]
            rows = [{at: part[j : j + 1] for at, part in parts.items()} for j in range(BLOCK)]
            inverse = []
            for j in range(BLOCK):
                inverse.append(1.0 / square[j][j])
                for i in range(j + 1, BLOCK):
                    factor = square[i][j] * inverse[j]
                    for m in range(j + 1, i + 1):
                        square[i][m] = square[i][m] - factor * square[m][j]
                    for at in parts:
                        rows[i][at] = rows[i][at] - factor * rows[j][at]
                    if pivot + BLOCK < last:
                        columns[i] = columns[i] - columns[j] * factor
            for j in range(BLOCK):
                scale = 1.0 / jnp.sqrt(square[j][j])
                for at in parts:
                    held_ref[pivot + j : pivot + j + 1, at : at + lanes] = rows[j][at] * scale
            if pivot + BLOCK < last:
                for at in parts:
                    rest = parts[at][BLOCK:]
                    for j in range(BLOCK):
                        rest = rest - columns[j][BLOCK:] * (rows[j][at] * inverse[j])
                    parts[at] = rest
    out_ref[...] = held_ref[:, rank:width]


def solve(gram, rows):
    count, rank = rows.shape
    padded = jnp.pad(rows.T, ((0, 0), (0, 128 - count)))
    solved = pl.pallas_call(
        solve_kernel,
        out_shape=jax.ShapeDtypeStruct((rank, 128), F32),
        scratch_shapes=[pltpu.VMEM((rank, rank + 128), F32)],
        name="solve",
    )(gram, padded)
    return solved[:, 0:count].T


def local(features, sketch, counts):
    tok_rows, width = features.shape
    sub_rows, rank = sketch.shape[1:]
    n_dp, n_panel = lax.axis_size(DP), lax.axis_size(PANEL)
    n_zl, n_x, n_y, n_zh, n_c = (lax.axis_size(name) for name in DP + PANEL)
    limit = counts[lax.axis_index(DP)]
    live = lax.iota(jnp.int32, tok_rows)[:, None] < limit
    token_total = jnp.sum(counts).astype(F32)

    high = lax.reduce_precision(sketch[0], 8, 7)
    rest = sketch[0] - high
    middle = lax.reduce_precision(rest, 8, 7)
    extra = jnp.stack([high, middle, rest - middle]).astype(BF16).reshape(-1, width)

    across = lax.all_gather(features, YC)
    along_z = lax.all_gather(jnp.concatenate([features, extra]), "zh")
    thirds = along_z[:, tok_rows:].reshape(-1, width)
    thirds = lax.all_gather(jnp.pad(thirds, ((0, PAD_ROWS - thirds.shape[0]), (0, 0))), YC)
    thirds = thirds[:, 0 : n_zh * extra.shape[0]].astype(F32)
    thirds = thirds.reshape(n_y * n_c, n_zh, 3, sub_rows, rank)
    start = (thirds[:, :, 0] + thirds[:, :, 1]) + thirds[:, :, 2]
    start = start.reshape(n_panel * sub_rows, rank)

    near = jnp.where(live, along_z[:, :tok_rows], 0)
    sums = jnp.einsum("ztf,pta->zfpa", near, across, preferred_element_type=F32)
    sums = sums.reshape(n_zh, n_zl, n_x, sub_rows, n_y * n_c, width)
    sums = sums.transpose(2, 4, 1, 0, 3, 5)
    sums = sums.reshape(n_x * n_y * n_c, n_zl, n_zh, sub_rows, width)
    sums = exchange(sums, XYC).reshape(n_x, n_y * n_c, n_zl, n_zh, sub_rows, width)
    sums = jnp.sum(sums, axis=0).transpose(1, 0, 2, 3, 4)
    sums = jnp.sum(exchange(sums, ("zl",)), axis=0) / token_total

    columns = sums.reshape(n_panel * sub_rows, width)
    covariance = sums.reshape(n_y, n_c, n_zh, sub_rows, width)
    covariance = covariance.transpose(4, 0, 2, 1, 3).reshape(width, 1, n_panel * sub_rows)

    product = lax.dot_general(
        columns, start, (((0,), (0,)), ((), ())), precision=HIGH, preferred_element_type=F32
    )
    product = jnp.sum(exchange(product.reshape(n_dp, sub_rows, rank), DP), axis=0)
    product = gather(product, DP).reshape(width, rank)
    product = jnp.dot(columns, product, precision=HIGH, preferred_element_type=F32)
    rows = jnp.sum(exchange(product.reshape(n_y * n_c, n_zh * sub_rows, rank), YC), axis=0)
    rows = jnp.sum(gather(rows, ("zh",)), axis=0)

    gram = lax.dot_general(
        rows, rows, (((0,), (0,)), ((), ())), precision=HIGH, preferred_element_type=F32
    )
    gram = jnp.sum(exchange(gram.reshape(n_x * n_y * n_c, -1, rank), XYC), axis=0)
    gram = jnp.sum(gather(gram, ("zl",)), axis=0)
    gram = gather(gram, XYC).reshape(rank, rank)
    own = lax.dynamic_slice_in_dim(rows, lax.axis_index("zh") * sub_rows, sub_rows)
    basis = math.sqrt(width * n_panel) * solve(gram, own)
    return covariance, basis[None]


def solution(mesh):
    inner = Mesh(mesh.devices.reshape(4, 4, 4, 4, 2), DP + PANEL)
    return jax.shard_map(
        local,
        mesh=inner,
        in_specs=(P(DP, PANEL), P(PANEL, DP, None), P()),
        out_specs=(P(PANEL, DP, None), P(PANEL, DP, None)),
        check_vma=False,
    )
```

time: 307 us -> 228 us (0.74)
  blocking collectives: 151 us -> 120 us
  waiting for transfers between devices: 74.3 us -> 47.1 us
  Pallas kernels: 25.7 us -> 9.2 us
    all_to_all x6, blocking collectives: 151 us -> 75.7 us  [exchange(): return lax.all_to_all(blocks, axes, 0, 0, tiled=True)]
    all_gather x0 -> x1, blocking collectives: none -> 44.2 us  [local(): along_z = lax.all_gather(jnp.concatenate([features, extra]), 'zh')]
    all_gather x2, waiting for transfers between devices: 26.7 us -> 1.28 us  [the longest x1 1.26 us: local(): lax.all_gather(jnp.pad(thirds, ((0, PAD_ROWS - thirds.shape[0]), (0, 0)))...]
    pallas_call x1, Pallas kernels: 25.7 us -> 9.2 us  [solve(): pl.pallas_call(solve_kernel, out_shape=jax.ShapeDtypeStruct((rank, 128),...]
  transfers between devices with their start and end apart: 5 -> 5, of which waited for: 4 -> 4; matrix products, arithmetic and copies ran while one was open for 2% -> 4% of each run, Pallas kernels for 0% -> 0%
where the time goes in v3:
time: 228 us; the launch traced here: 227 us
  blocking collectives  120 us (53%)
  waiting for transfers between devices  47.1 us (21%)
  starting transfers between devices  18.8 us (8%)
  between operations  14.9 us (7%)
  Pallas kernels  9.2 us (4%)
  local copies, waits for them, and re-layouts  8.16 us (4%)
  other arithmetic  5.34 us (2%)
  matrix products  3.37 us (1%)
    all_to_all x6, blocking collectives, exchange(): return lax.all_to_all(blocks, axes, 0, 0, tiled=True)  75.7 us
    all_to_all x3, waiting for transfers between devices, exchange(): return lax.all_to_all(blocks, axes, 0, 0, tiled=True)  45.1 us
    all_gather x1, blocking collectives, local(): along_z = lax.all_gather(jnp.concatenate([features, extra]), 'zh')  44.2 us
    all_to_all x3, starting transfers between devices, exchange(): return lax.all_to_all(blocks, axes, 0, 0, tiled=True)  18.7 us
    pallas_call x1, Pallas kernels, solve(): pl.pallas_call(solve_kernel, out_shape=jax.ShapeDtypeStruct((rank, 128),...  9.2 us
  transfers between devices with their start and end apart: 5, of which 4 were waited for; matrix products, arithmetic and copies ran while one was open for 4% of the time, Pallas kernels for 0%

profile of v3, /device:TPU:1, one launch (start us, length us, event | category | flops | bytes accessed | tf_op | source)
XLA Modules:
  0.0 226.8 jit_solution(8316500098313820993)
XLA Ops:
  7.2 0.0 all-gather.6.cloned.1.call-start
  7.2 0.7 all-gather.6.cloned.1.call-update
  7.9 0.7 reduce-precision_convert_fusion.1
  8.6 0.9 pad_maximum_fusion
  9.6 0.0 copy-start.1
  9.6 44.2 %all-gather = bf16[3264,128]{1,0:T(8,128)(2,1)S(1)} all-gather(bf16[816,128]{1,0:T(8,128)(2,1)S(1)} %pad_maximum_fusion), channel_id=2, replica_groups=mesh['zl'=4,'x'=4,'y'=4,'zh'=4,'c'=2] {'zh'}, dimensions={0}, use_global_device_ids=true | all-gather | bytes 1044480 | tf_op jit(solution)/shard_map/all_gather | solution.py:110
  53.8 0.1 slice.28
  53.9 0.3 copy.50
  54.2 0.0 copy-done.1
  54.2 0.6 dynamic_slice.6
  54.8 0.6 iota_compare_fusion
  55.4 0.0 all-gather.6.cloned.1.call-done
  55.4 2.4 %fusion = f32[4,128,8,128]{3,1,2,0:T(8,128)S(1)} fusion(bf16[8,768,128,1]{2,1,0,3:T(8,128)(2,1)} %bitcast.69, bf16[4,768,128]{1,2,0:T(8,128)(2,1)S(1)} %copy.50, pred[768]{0:T(1024)(128)(4,1)S(1)} %iota_compare_fusion), kind=kOutput, calls=%fused_computation | convolution fusion | flops 805699584 | bytes 4457216 | tf_op jit(solution)/shard_map/ztf,pta->zfpa/dot_general | solution.py:119
  57.8 1.6 copy.41
  59.5 10.1 %all-to-all-start = ((f32[32,4,4,8,128]{4,3,2,1,0:T(8,128)}), f32[32,4,4,8,128]{4,3,2,1,0:T(8,128)S(1)}, u32[]{:S(2)}, u32[]{:S(2)}) async-start(f32[32,4,4,8,128]{4,3,2,1,0:T(8,128)} %bitcast.55), calls=%async_computation | async-start | bytes 4194304 | tf_op jit(solution)/shard_map/all_to_all | solution.py:23
  69.6 0.0 all-gather.8.cloned.1.call-start
  69.6 0.7 pad.8
  70.3 0.0 all-gather.8.cloned.1.call-update
  70.3 27.6 %all-to-all-done = f32[32,4,4,8,128]{4,3,2,1,0:T(8,128)S(1)} async-done(((f32[32,4,4,8,128]{4,3,2,1,0:T(8,128)}), f32[32,4,4,8,128]{4,3,2,1,0:T(8,128)S(1)}, u32[]{:S(2)}, u32[]{:S(2)}) %all-to-all-start) | async-done | bytes 2097184 | tf_op jit(solution)/shard_map/all_to_all | solution.py:23
  97.9 0.2 reduce_sum.72
  98.1 0.8 copy.42
  99.0 3.5 %all-to-all-start.1 = ((f32[4,8,4,8,128]{4,3,2,1,0:T(8,128)}), f32[4,8,4,8,128]{4,3,2,1,0:T(8,128)S(1)}, u32[]{:S(2)}, u32[]{:S(2)}) async-start(f32[4,8,4,8,128]{4,3,2,1,0:T(8,128)} %copy.42), calls=%async_computation.1 | async-start | bytes 1048576 | tf_op jit(solution)/shard_map/all_to_all | solution.py:23
  102.4 0.6 reduce_sum.74
  103.7 1.3 all-gather.8.cloned.1.call-done
  105.0 1.0 slice_convert_fusion
  106.0 0.2 reshape.79
  106.3 0.1 slice_add_fusion
  106.3 10.1 %all-to-all-done.1 = f32[4,8,4,8,128]{4,3,2,1,0:T(8,128)S(1)} async-done(((f32[4,8,4,8,128]{4,3,2,1,0:T(8,128)}), f32[4,8,4,8,128]{4,3,2,1,0:T(8,128)S(1)}, u32[]{:S(2)}, u32[]{:S(2)}) %all-to-all-start.1) | async-done | bytes 524320 | tf_op jit(solution)/shard_map/all_to_all | solution.py:23
  116.5 0.1 copy.44
  116.6 0.3 fusion.10
  116.9 12.9 %all_to_all.45 = f32[16,8,256]{2,1,0:T(8,128)S(1)} all-to-all(f32[16,8,256]{2,1,0:T(8,128)S(1)} %fusion.10), channel_id=1, replica_groups=mesh['zl'=4,'x'=4,'y'=4,'zh'=4,'c'=2] {'zl','x'}, dimensions={0} | all-to-all | bytes 262144 | tf_op jit(solution)/shard_map/all_to_all | solution.py:23
  129.8 11.3 %all_to_all.46 = f32[16,8,256]{2,1,0:T(8,128)S(1)} all-to-all(f32[16,8,256]{2,1,0:T(8,128)S(1)} %broadcast_in_dim.24), channel_id=1, replica_groups=mesh['zl'=4,'x'=4,'y'=4,'zh'=4,'c'=2] {'zl','x'}, dimensions={0} | all-to-all | bytes 262144 | tf_op jit(solution)/shard_map/all_to_all | solution.py:23
  141.1 0.4 fusion.6
  141.5 11.3 %all_to_all.47 = f32[8,32,256]{2,1,0:T(8,128)S(1)} all-to-all(f32[8,32,256]{2,1,0:T(8,128)S(1)} %fusion.6), channel_id=1, replica_groups=mesh['zl'=4,'x'=4,'y'=4,'zh'=4,'c'=2] {'y','c'}, dimensions={0} | all-to-all | bytes 524288 | tf_op jit(solution)/shard_map/all_to_all | solution.py:23
  152.9 17.3 %all_to_all.48 = f32[4,32,256]{2,1,0:T(8,128)S(1)} all-to-all(f32[4,32,256]{2,1,0:T(8,128)S(1)} %broadcast_in_dim.25), channel_id=1, replica_groups=mesh['zl'=4,'x'=4,'y'=4,'zh'=4,'c'=2] {'zh'}, dimensions={0} | all-to-all | bytes 262144 | tf_op jit(solution)/shard_map/all_to_all | solution.py:23
  170.2 0.1 copy.45
  170.3 0.3 fusion.8
  170.6 15.5 %all_to_all.49 = f32[32,8,256]{2,1,0:T(8,128)S(1)} all-to-all(f32[32,8,256]{2,1,0:T(8,128)S(1)} %fusion.8), channel_id=1, replica_groups=mesh['zl'=4,'x'=4,'y'=4,'zh'=4,'c'=2] {'x','y','c'}, dimensions={0} | all-to-all | bytes 524288 | tf_op jit(solution)/shard_map/all_to_all | solution.py:23
  186.2 7.3 %all_to_all.50 = f32[4,8,256]{2,1,0:T(8,128)S(1)} all-to-all(f32[4,8,256]{2,1,0:T(8,128)S(1)} %broadcast_in_dim.44), channel_id=1, replica_groups=mesh['zl'=4,'x'=4,'y'=4,'zh'=4,'c'=2] {'zl'}, dimensions={0} | all-to-all | bytes 65536 | tf_op jit(solution)/shard_map/all_to_all | solution.py:23
  193.5 0.7 broadcast_in_dim.45
  194.2 5.1 %all-to-all-start.8 = ((f32[32,8,256]{2,1,0:T(8,128)}), f32[32,8,256]{2,1,0:T(8,128)S(1)}, u32[]{:S(2)}, u32[]{:S(2)}) async-start(f32[32,8,256]{2,1,0:T(8,128)} %broadcast_in_dim.45), calls=%async_computation.8 | async-start | bytes 524288 | tf_op jit(solution)/shard_map/all_to_all | solution.py:23
  199.4 0.8 copy.47
  200.2 0.1 copy.51
  200.3 0.7 pad.9.rows_ref
  201.0 7.5 %all-to-all-done.8 = f32[32,8,256]{2,1,0:T(8,128)S(1)} async-done(((f32[32,8,256]{2,1,0:T(8,128)}), f32[32,8,256]{2,1,0:T(8,128)S(1)}, u32[]{:S(2)}, u32[]{:S(2)}) %all-to-all-start.8) | async-done | bytes 262176 | tf_op jit(solution)/shard_map/all_to_all | solution.py:23
  208.5 0.0 copy-start
  208.5 0.7 copy-done
  209.2 9.2 %solve.1 = f32[256,128]{1,0:T(8,128)} custom-call(f32[256,256]{1,0:T(8,128)} %bitcast.62, f32[256,128]{1,0:T(8,128)} %pad.9.rows_ref), custom_call_target="tpu_custom_call" | custom-call | tf_op jit(solution)/shard_map/solve/pallas_call | solution.py:86
  218.4 0.9 fusion.5
  219.3 0.7 copy.48
  (15 shorter events, 0.2 us)
Async XLA Ops:
  7.2 48.3 %all-gather.6.cloned.1.call-start = ((), (), s32[]{:S(2)}) async-start(), calls=%async_computation.9 | async-start | bytes 1769472 | tf_op jit(solution)/shard_map/all_gather | solution.py:109
  9.6 44.6 %copy-start.1 = (s32[16]{0:T(128)S(1)}, s32[16]{0:T(128)}, u32[]{:S(2)}) copy-start(s32[16]{0:T(128)} %param.5) | copy-start | bytes 196
  59.5 38.4 %all-to-all-start = ((f32[32,4,4,8,128]{4,3,2,1,0:T(8,128)}), f32[32,4,4,8,128]{4,3,2,1,0:T(8,128)S(1)}, u32[]{:S(2)}, u32[]{:S(2)}) async-start(f32[32,4,4,8,128]{4,3,2,1,0:T(8,128)} %bitcast.55), calls=%async_computation | async-start | bytes 4194304 | tf_op jit(solution)/shard_map/all_to_all | solution.py:23
  69.6 35.4 %all-gather.8.cloned.1.call-start = ((), (), s32[]{:S(2)}) async-start(), calls=%async_computation.10 | async-start | bytes 1179648 | tf_op jit(solution)/shard_map/all_gather | solution.py:112
  99.0 17.4 %all-to-all-start.1 = ((f32[4,8,4,8,128]{4,3,2,1,0:T(8,128)}), f32[4,8,4,8,128]{4,3,2,1,0:T(8,128)S(1)}, u32[]{:S(2)}, u32[]{:S(2)}) async-start(f32[4,8,4,8,128]{4,3,2,1,0:T(8,128)} %copy.42), calls=%async_computation.1 | async-start | bytes 1048576 | tf_op jit(solution)/shard_map/all_to_all | solution.py:23
  194.2 14.2 %all-to-all-start.8 = ((f32[32,8,256]{2,1,0:T(8,128)}), f32[32,8,256]{2,1,0:T(8,128)S(1)}, u32[]{:S(2)}, u32[]{:S(2)}) async-start(f32[32,8,256]{2,1,0:T(8,128)} %broadcast_in_dim.45), calls=%async_computation.8 | async-start | bytes 524288 | tf_op jit(solution)/shard_map/all_to_all | solution.py:23
  208.5 0.7 copy-start
Sparse Core Ops, SparseCore 0:
  10.1 37.9 all-gather.5
  73.1 31.7 all-gather.7

commit v4 on v3

--- a/solution.py
+++ b/solution.py
@@ -14,9 +14,9 @@
 PANEL = ("y", "zh", "c")
 YC = ("y", "c")
 XYC = ("x", "y", "c")
+ZYC = ("zl", "y", "c")
 PANEL_STEP = 64
 BLOCK = 8
-PAD_ROWS = 512
 
 
 def exchange(blocks, axes):
@@ -109,11 +109,10 @@
     across = lax.all_gather(features, YC)
     along_z = lax.all_gather(jnp.concatenate([features, extra]), "zh")
     thirds = along_z[:, tok_rows:].reshape(-1, width)
-    thirds = lax.all_gather(jnp.pad(thirds, ((0, PAD_ROWS - thirds.shape[0]), (0, 0))), YC)
-    thirds = thirds[:, 0 : n_zh * extra.shape[0]].astype(F32)
-    thirds = thirds.reshape(n_y * n_c, n_zh, 3, sub_rows, rank)
+    thirds = lax.all_gather(thirds, ZYC).astype(F32)
+    thirds = thirds.reshape(n_zl * n_y * n_c, n_zh, 3, sub_rows, rank)
     start = (thirds[:, :, 0] + thirds[:, :, 1]) + thirds[:, :, 2]
-    start = start.reshape(n_panel * sub_rows, rank)
+    start = start.reshape(n_zl * n_panel * sub_rows, rank)
 
     near = jnp.where(live, along_z[:, :tok_rows], 0)
     sums = jnp.einsum("ztf,pta->zfpa", near, across, preferred_element_type=F32)
@@ -122,17 +121,22 @@
     sums = sums.reshape(n_x * n_y * n_c, n_zl, n_zh, sub_rows, width)
     sums = exchange(sums, XYC).reshape(n_x, n_y * n_c, n_zl, n_zh, sub_rows, width)
     sums = jnp.sum(sums, axis=0).transpose(1, 0, 2, 3, 4)
-    sums = jnp.sum(exchange(sums, ("zl",)), axis=0) / token_total
-
-    columns = sums.reshape(n_panel * sub_rows, width)
-    covariance = sums.reshape(n_y, n_c, n_zh, sub_rows, width)
-    covariance = covariance.transpose(4, 0, 2, 1, 3).reshape(width, 1, n_panel * sub_rows)
 
     product = lax.dot_general(
-        columns, start, (((0,), (0,)), ((), ())), precision=HIGH, preferred_element_type=F32
+        sums.reshape(-1, width), start, (((0,), (0,)), ((), ())), precision=HIGH, preferred_element_type=F32
     )
-    product = jnp.sum(exchange(product.reshape(n_dp, sub_rows, rank), DP), axis=0)
-    product = gather(product, DP).reshape(width, rank)
+    product = product.reshape(n_zl, width // n_zl, rank // width, width).transpose(0, 2, 1, 3)
+    group_rows = n_panel * sub_rows
+    both = [sums.reshape(n_zl, group_rows, width), product.reshape(n_zl, -1, width)]
+    both = jnp.sum(exchange(jnp.concatenate(both, axis=1), ("zl",)), axis=0) / token_total
+    product = jnp.sum(gather(both[group_rows:], ("x",)), axis=0)
+    product = gather(product, ("zl",)).reshape(n_zl, rank // width, width // n_zl, width)
+    product = product.transpose(0, 2, 1, 3).reshape(width, rank)
+
+    columns = both[:group_rows]
+    covariance = columns.reshape(n_y, n_c, n_zh, sub_rows, width)
+    covariance = covariance.transpose(4, 0, 2, 1, 3).reshape(width, 1, group_rows)
+
     product = jnp.dot(columns, product, precision=HIGH, preferred_element_type=F32)
     rows = jnp.sum(exchange(product.reshape(n_y * n_c, n_zh * sub_rows, rank), YC), axis=0)
     rows = jnp.sum(gather(rows, ("zh",)), axis=0)

time: 228 us -> 273 us (1.20)
  waiting for transfers between devices: 47.1 us -> 91.7 us
  blocking collectives: 120 us -> 110 us
  local copies, waits for them, and re-layouts: 8.16 us -> 12 us
  starting transfers between devices: 18.8 us -> 22.2 us
    all_gather x1, waiting for transfers between devices: 1.26 us -> 62.9 us  [local(): thirds = lax.all_gather(thirds, ZYC).astype(F32)]
    all_to_all x3 -> x4, waiting for transfers between devices: 45.1 us -> 28.1 us  [exchange(): return lax.all_to_all(blocks, axes, 0, 0, tiled=True)]
    all_to_all x6 -> x5, blocking collectives: 75.7 us -> 65.5 us  [exchange(): return lax.all_to_all(blocks, axes, 0, 0, tiled=True)]
    all_to_all x3 -> x4, starting transfers between devices: 18.7 us -> 22.1 us  [exchange(): return lax.all_to_all(blocks, axes, 0, 0, tiled=True)]
  transfers between devices with their start and end apart: 5 -> 6, of which waited for: 4 -> 4; matrix products, arithmetic and copies ran while one was open for 4% -> 6% of each run, Pallas kernels for 0% -> 0%
where the time goes in v4:
time: 273 us; the launch traced here: 272 us
  blocking collectives  110 us (40%)
  waiting for transfers between devices  91.7 us (34%)
  starting transfers between devices  22.2 us (8%)
  between operations  15 us (5%)
  local copies, waits for them, and re-layouts  12 us (4%)
  Pallas kernels  9.2 us (3%)
  other arithmetic  7.93 us (3%)
  matrix products  4.28 us (2%)
    all_to_all x5, blocking collectives, exchange(): return lax.all_to_all(blocks, axes, 0, 0, tiled=True)  65.5 us
    all_gather x1, waiting for transfers between devices, local(): thirds = lax.all_gather(thirds, ZYC).astype(F32)  62.9 us
    all_gather x1, blocking collectives, local(): along_z = lax.all_gather(jnp.concatenate([features, extra]), 'zh')  44.2 us
    all_to_all x4, waiting for transfers between devices, exchange(): return lax.all_to_all(blocks, axes, 0, 0, tiled=True)  28.1 us
    all_to_all x4, starting transfers between devices, exchange(): return lax.all_to_all(blocks, axes, 0, 0, tiled=True)  22.1 us
    pallas_call x1, Pallas kernels, solve(): pl.pallas_call(solve_kernel, out_shape=jax.ShapeDtypeStruct((rank, 128),...  9.2 us
  transfers between devices with their start and end apart: 6, of which 4 were waited for; matrix products, arithmetic and copies ran while one was open for 6% of the time, Pallas kernels for 0%

profile of v4, /device:TPU:1, one launch (start us, length us, event | category | flops | bytes accessed | tf_op | source)
XLA Modules:
  0.0 272.0 jit_solution(2357474260136430413)
XLA Ops:
  7.2 0.0 all-gather.7.cloned.1.call-start
  7.2 0.7 all-gather.7.cloned.1.call-update
  7.9 0.0 all-gather.5.cloned.1.call-start
  7.9 0.7 reduce-precision_convert_fusion.1
  8.7 0.9 pad_maximum_fusion.1
  9.6 0.0 copy-start.1
  9.6 44.2 %all-gather = bf16[3264,128]{1,0:T(8,128)(2,1)S(1)} all-gather(bf16[816,128]{1,0:T(8,128)(2,1)S(1)} %pad_maximum_fusion.1), channel_id=2, replica_groups=mesh['zl'=4,'x'=4,'y'=4,'zh'=4,'c'=2] {'zh'}, dimensions={0}, use_global_device_ids=true | all-gather | bytes 1044480 | tf_op jit(solution)/shard_map/all_gather | solution.py:110
  53.9 0.6 slice.33
  54.5 0.0 all-gather.5.cloned.1.call-update
  54.5 0.1 slice.32
  54.6 0.3 copy.68
  54.9 0.0 copy-done.1
  54.9 0.6 dynamic_slice.6
  55.5 0.6 iota_compare_fusion
  56.1 0.0 all-gather.7.cloned.1.call-done
  56.1 2.4 fusion
  58.5 1.6 copy.54
  60.1 10.1 %all-to-all-start = ((f32[32,4,4,8,128]{4,3,2,1,0:T(8,128)}), f32[32,4,4,8,128]{4,3,2,1,0:T(8,128)}, u32[]{:S(2)}, u32[]{:S(2)}) async-start(f32[32,4,4,8,128]{4,3,2,1,0:T(8,128)} %bitcast.8), calls=%async_computation | async-start | bytes 4194304 | tf_op jit(solution)/shard_map/all_to_all | solution.py:23
  70.3 62.9 %all-gather.5.cloned.1.call-done = bf16[32,192,128]{2,1,0:T(8,128)(2,1)} async-done(((bf16[1,192,128]{2,1,0:T(8,128)(2,1)}), bf16[32,192,128]{2,1,0:T(8,128)(2,1)}) %all-gather.5.cloned.1.call-update) | async-done | bytes 1572880 | tf_op jit(solution)/shard_map/all_gather | solution.py:112
  133.2 2.4 reshape.82
  135.6 1.2 slice_add_fusion
  136.8 1.6 copy.67
  138.3 0.0 all-to-all-done
  138.4 1.9 reduce_sum.72
  140.3 0.2 copy.57
  140.5 1.2 fusion.11
  141.7 0.9 pad_maximum_fusion
  142.5 3.5 %all-to-all-start.1 = ((f32[4,320,128]{2,1,0:T(8,128)}), f32[4,320,128]{2,1,0:T(8,128)S(1)}, u32[]{:S(2)}, u32[]{:S(2)}) async-start(f32[4,320,128]{2,1,0:T(8,128)} %pad_maximum_fusion), calls=%async_computation.1 | async-start | bytes 1310720 | tf_op jit(solution)/shard_map/all_to_all | solution.py:23
  146.0 0.6 reduce_sum.74
  147.3 15.8 %all-to-all-done.1 = f32[4,320,128]{2,1,0:T(8,128)S(1)} async-done(((f32[4,320,128]{2,1,0:T(8,128)}), f32[4,320,128]{2,1,0:T(8,128)S(1)}, u32[]{:S(2)}, u32[]{:S(2)}) %all-to-all-start.1) | async-done | bytes 655392 | tf_op jit(solution)/shard_map/all_to_all | solution.py:23
  163.2 7.2 %all_to_all.45 = f32[4,64,128]{2,1,0:T(8,128)S(1)} all-to-all(f32[4,64,128]{2,1,0:T(8,128)S(1)} %broadcast_in_dim.26), channel_id=1, replica_groups=mesh['zl'=4,'x'=4,'y'=4,'zh'=4,'c'=2] {'x'}, dimensions={0} | all-to-all | bytes 262144 | tf_op jit(solution)/shard_map/all_to_all | solution.py:23
  170.5 0.7 broadcast_in_dim.27
  171.1 3.3 %all-to-all-start.3 = ((f32[4,64,128]{2,1,0:T(8,128)}), f32[4,64,128]{2,1,0:T(8,128)S(1)}, u32[]{:S(2)}, u32[]{:S(2)}) async-start(f32[4,64,128]{2,1,0:T(8,128)} %broadcast_in_dim.27), calls=%async_computation.3 | async-start | bytes 262144 | tf_op jit(solution)/shard_map/all_to_all | solution.py:23
  174.5 4.7 %all-to-all-done.3 = f32[4,64,128]{2,1,0:T(8,128)S(1)} async-done(((f32[4,64,128]{2,1,0:T(8,128)}), f32[4,64,128]{2,1,0:T(8,128)S(1)}, u32[]{:S(2)}, u32[]{:S(2)}) %all-to-all-start.3) | async-done | bytes 131104 | tf_op jit(solution)/shard_map/all_to_all | solution.py:23
  179.2 0.1 copy.60
  179.3 0.1 reshape.89
  179.4 0.4 fusion.12
  179.8 13.2 %all_to_all.46 = f32[8,32,256]{2,1,0:T(8,128)S(1)} all-to-all(f32[8,32,256]{2,1,0:T(8,128)S(1)} %fusion.12), channel_id=1, replica_groups=mesh['zl'=4,'x'=4,'y'=4,'zh'=4,'c'=2] {'y','c'}, dimensions={0} | all-to-all | bytes 524288 | tf_op jit(solution)/shard_map/all_to_all | solution.py:23
  193.1 21.7 %all_to_all.47 = f32[4,32,256]{2,1,0:T(8,128)S(1)} all-to-all(f32[4,32,256]{2,1,0:T(8,128)S(1)} %broadcast_in_dim.28), channel_id=1, replica_groups=mesh['zl'=4,'x'=4,'y'=4,'zh'=4,'c'=2] {'zh'}, dimensions={0} | all-to-all | bytes 262144 | tf_op jit(solution)/shard_map/all_to_all | solution.py:23
  214.8 0.1 copy.61
  214.9 0.3 fusion.6
  215.2 15.5 %all_to_all.48 = f32[32,8,256]{2,1,0:T(8,128)S(1)} all-to-all(f32[32,8,256]{2,1,0:T(8,128)S(1)} %fusion.6), channel_id=1, replica_groups=mesh['zl'=4,'x'=4,'y'=4,'zh'=4,'c'=2] {'x','y','c'}, dimensions={0} | all-to-all | bytes 524288 | tf_op jit(solution)/shard_map/all_to_all | solution.py:23
  230.8 7.9 %all_to_all.49 = f32[4,8,256]{2,1,0:T(8,128)S(1)} all-to-all(f32[4,8,256]{2,1,0:T(8,128)S(1)} %broadcast_in_dim.29), channel_id=1, replica_groups=mesh['zl'=4,'x'=4,'y'=4,'zh'=4,'c'=2] {'zl'}, dimensions={0} | all-to-all | bytes 65536 | tf_op jit(solution)/shard_map/all_to_all | solution.py:23
  238.7 0.7 broadcast_in_dim.52
  239.4 5.1 %all-to-all-start.8 = ((f32[32,8,256]{2,1,0:T(8,128)}), f32[32,8,256]{2,1,0:T(8,128)S(1)}, u32[]{:S(2)}, u32[]{:S(2)}) async-start(f32[32,8,256]{2,1,0:T(8,128)} %broadcast_in_dim.52), calls=%async_computation.8 | async-start | bytes 524288 | tf_op jit(solution)/shard_map/all_to_all | solution.py:23
  244.6 0.8 copy.63
  245.3 0.1 copy.69
  245.5 0.7 pad.4.rows_ref
  246.1 7.5 %all-to-all-done.8 = f32[32,8,256]{2,1,0:T(8,128)S(1)} async-done(((f32[32,8,256]{2,1,0:T(8,128)}), f32[32,8,256]{2,1,0:T(8,128)S(1)}, u32[]{:S(2)}, u32[]{:S(2)}) %all-to-all-start.8) | async-done | bytes 262176 | tf_op jit(solution)/shard_map/all_to_all | solution.py:23
  253.6 0.0 copy-start
  253.6 0.7 copy-done
  254.3 9.2 %solve.1 = f32[256,128]{1,0:T(8,128)} custom-call(f32[256,256]{1,0:T(8,128)} %bitcast.72, f32[256,128]{1,0:T(8,128)} %pad.4.rows_ref), custom_call_target="tpu_custom_call" | custom-call | tf_op jit(solution)/shard_map/solve/pallas_call | solution.py:86
  263.5 0.9 fusion.5
  264.5 0.7 copy.64
  (17 shorter events, 0.2 us)
Async XLA Ops:
  7.2 49.0 %all-gather.7.cloned.1.call-start = ((), (), s32[]{:S(2)}) async-start(), calls=%async_computation.10 | async-start | bytes 1769472 | tf_op jit(solution)/shard_map/all_gather | solution.py:109
  7.9 125.3 %all-gather.5.cloned.1.call-start = ((), (), s32[]{:S(2)}) async-start(), calls=%async_computation.9 | async-start | bytes 1622016 | tf_op jit(solution)/shard_map/all_gather | solution.py:112
  9.6 45.2 %copy-start.1 = (s32[16]{0:T(128)S(1)}, s32[16]{0:T(128)}, u32[]{:S(2)}) copy-start(s32[16]{0:T(128)} %param.5) | copy-start | bytes 196
  60.1 78.2 %all-to-all-start = ((f32[32,4,4,8,128]{4,3,2,1,0:T(8,128)}), f32[32,4,4,8,128]{4,3,2,1,0:T(8,128)}, u32[]{:S(2)}, u32[]{:S(2)}) async-start(f32[32,4,4,8,128]{4,3,2,1,0:T(8,128)} %bitcast.8), calls=%async_computation | async-start | bytes 4194304 | tf_op jit(solution)/shard_map/all_to_all | solution.py:23
  142.5 20.6 %all-to-all-start.1 = ((f32[4,320,128]{2,1,0:T(8,128)}), f32[4,320,128]{2,1,0:T(8,128)S(1)}, u32[]{:S(2)}, u32[]{:S(2)}) async-start(f32[4,320,128]{2,1,0:T(8,128)} %pad_maximum_fusion), calls=%async_computation.1 | async-start | bytes 1310720 | tf_op jit(solution)/shard_map/all_to_all | solution.py:23
  171.1 8.1 %all-to-all-start.3 = ((f32[4,64,128]{2,1,0:T(8,128)}), f32[4,64,128]{2,1,0:T(8,128)S(1)}, u32[]{:S(2)}, u32[]{:S(2)}) async-start(f32[4,64,128]{2,1,0:T(8,128)} %broadcast_in_dim.27), calls=%async_computation.3 | async-start | bytes 262144 | tf_op jit(solution)/shard_map/all_to_all | solution.py:23
  239.4 14.2 %all-to-all-start.8 = ((f32[32,8,256]{2,1,0:T(8,128)}), f32[32,8,256]{2,1,0:T(8,128)S(1)}, u32[]{:S(2)}, u32[]{:S(2)}) async-start(f32[32,8,256]{2,1,0:T(8,128)} %broadcast_in_dim.52), calls=%async_computation.8 | async-start | bytes 524288 | tf_op jit(solution)/shard_map/all_to_all | solution.py:23
  253.6 0.7 copy-start
Sparse Core Ops, SparseCore 0:
  10.1 37.9 all-gather.6
  54.6 78.5 all-gather.4

commit v5 on v3

--- a/solution.py
+++ b/solution.py
@@ -1,3 +1,4 @@
+import functools
 import math
 
 import jax
@@ -28,11 +29,14 @@
     return exchange(jnp.broadcast_to(block[None], (size,) + block.shape), axes)
 
 
-def solve_kernel(gram_ref, rows_ref, out_ref, held_ref):
-    rank, lanes = rows_ref.shape
+def solve_kernel(place_ref, gram_ref, rows_ref, out_ref, held_ref, *, scale_by):
+    count, rank = out_ref.shape
     width = held_ref.shape[1]
+    lanes = width - rank
+    own = rows_ref[pl.ds(pl.multiple_of(place_ref[0] * count, count), count), :]
+    padded = jnp.concatenate([own, jnp.zeros((lanes - count, rank), F32)], axis=0)
     held_ref[:, 0:rank] = gram_ref[...]
-    held_ref[:, rank:width] = rows_ref[...]
+    held_ref[:, rank:width] = padded.T
     for first in range(0, rank, PANEL_STEP):
         last = first + PANEL_STEP
         parts = {}
@@ -77,19 +81,63 @@
                     for j in range(BLOCK):
                         rest = rest - columns[j][BLOCK:] * (rows[j][at] * inverse[j])
                     parts[at] = rest
-    out_ref[...] = held_ref[:, rank:width]
-
-
-def solve(gram, rows):
-    count, rank = rows.shape
-    padded = jnp.pad(rows.T, ((0, 0), (0, 128 - count)))
-    solved = pl.pallas_call(
-        solve_kernel,
-        out_shape=jax.ShapeDtypeStruct((rank, 128), F32),
+    out_ref[...] = held_ref[:, rank:width].T[0:count] * scale_by
+
+
+def solve(gram, rows, place, count, scale_by):
+    rank = rows.shape[1]
+    vmem = pl.BlockSpec(memory_space=pltpu.VMEM)
+    return pl.pallas_call(
+        functools.partial(solve_kernel, scale_by=scale_by),
+        out_shape=jax.ShapeDtypeStruct((count, rank), F32),
+        in_specs=[pl.BlockSpec(memory_space=pltpu.SMEM), vmem, vmem],
+        out_specs=vmem,
         scratch_shapes=[pltpu.VMEM((rank, rank + 128), F32)],
         name="solve",
-    )(gram, padded)
-    return solved[:, 0:count].T
+    )(place, gram, rows)
+
+
+def tile_kernel(limit_ref, near_ref, across_ref, out_ref, turned_ref):
+    n_zh, width = near_ref.shape[0], near_ref.shape[2]
+    tok_rows = across_ref.shape[1]
+    n_x, pair, n_zl, _, sub_rows, _ = out_ref.shape
+
+    @pl.when(pl.program_id(0) == 0)
+    def turn():
+        token = lax.broadcasted_iota(jnp.int32, (tok_rows, width), 0)
+        live = jnp.where(token < limit_ref[0], 1.0, 0.0)
+        for z in range(n_zh):
+            kept = near_ref[z, 0:tok_rows, :].astype(F32) * live
+            turned_ref[z * width : (z + 1) * width, :] = kept.astype(BF16).T
+
+    both = jnp.concatenate([across_ref[p] for p in range(pair)], axis=1)
+    for z in range(n_zh):
+        product = jnp.dot(
+            turned_ref[z * width : (z + 1) * width, :], both, preferred_element_type=F32
+        )
+        for low in range(n_zl):
+            for x in range(n_x):
+                row = (low * n_x + x) * sub_rows
+                for p in range(pair):
+                    out_ref[x, p, low, z] = product[row : row + sub_rows, p * width : (p + 1) * width]
+
+
+def tile(limit, near, across, n_zl, n_x, sub_rows):
+    n_zh, near_rows, width = near.shape
+    panels, tok_rows = across.shape[:2]
+    return pl.pallas_call(
+        tile_kernel,
+        grid=(panels // 2,),
+        out_shape=jax.ShapeDtypeStruct((n_x, panels, n_zl, n_zh, sub_rows, width), F32),
+        in_specs=[
+            pl.BlockSpec(memory_space=pltpu.SMEM),
+            pl.BlockSpec((n_zh, near_rows, width), lambda q: (0, 0, 0)),
+            pl.BlockSpec((2, tok_rows, width), lambda q: (q, 0, 0)),
+        ],
+        out_specs=pl.BlockSpec((n_x, 2, n_zl, n_zh, sub_rows, width), lambda q: (0, q, 0, 0, 0, 0)),
+        scratch_shapes=[pltpu.VMEM((n_zh * width, tok_rows), BF16)],
+        name="tile",
+    )(limit, near, across)
 
 
 def local(features, sketch, counts):
@@ -97,8 +145,7 @@
     sub_rows, rank = sketch.shape[1:]
     n_dp, n_panel = lax.axis_size(DP), lax.axis_size(PANEL)
     n_zl, n_x, n_y, n_zh, n_c = (lax.axis_size(name) for name in DP + PANEL)
-    limit = counts[lax.axis_index(DP)]
-    live = lax.iota(jnp.int32, tok_rows)[:, None] < limit
+    limit = lax.dynamic_slice_in_dim(counts, lax.axis_index(DP), 1)
     token_total = jnp.sum(counts).astype(F32)
 
     high = lax.reduce_precision(sketch[0], 8, 7)
@@ -115,10 +162,7 @@
     start = (thirds[:, :, 0] + thirds[:, :, 1]) + thirds[:, :, 2]
     start = start.reshape(n_panel * sub_rows, rank)
 
-    near = jnp.where(live, along_z[:, :tok_rows], 0)
-    sums = jnp.einsum("ztf,pta->zfpa", near, across, preferred_element_type=F32)
-    sums = sums.reshape(n_zh, n_zl, n_x, sub_rows, n_y * n_c, width)
-    sums = sums.transpose(2, 4, 1, 0, 3, 5)
+    sums = tile(limit, along_z, across, n_zl, n_x, sub_rows)
     sums = sums.reshape(n_x * n_y * n_c, n_zl, n_zh, sub_rows, width)
     sums = exchange(sums, XYC).reshape(n_x, n_y * n_c, n_zl, n_zh, sub_rows, width)
     sums = jnp.sum(sums, axis=0).transpose(1, 0, 2, 3, 4)
@@ -135,7 +179,7 @@
     product = gather(product, DP).reshape(width, rank)
     product = jnp.dot(columns, product, precision=HIGH, preferred_element_type=F32)
     rows = jnp.sum(exchange(product.reshape(n_y * n_c, n_zh * sub_rows, rank), YC), axis=0)
-    rows = jnp.sum(gather(rows, ("zh",)), axis=0)
+    rows = jnp.sum(lax.all_gather(rows, "zh"), axis=0)
 
     gram = lax.dot_general(
         rows, rows, (((0,), (0,)), ((), ())), precision=HIGH, preferred_element_type=F32
@@ -143,8 +187,8 @@
     gram = jnp.sum(exchange(gram.reshape(n_x * n_y * n_c, -1, rank), XYC), axis=0)
     gram = jnp.sum(gather(gram, ("zl",)), axis=0)
     gram = gather(gram, XYC).reshape(rank, rank)
-    own = lax.dynamic_slice_in_dim(rows, lax.axis_index("zh") * sub_rows, sub_rows)
-    basis = math.sqrt(width * n_panel) * solve(gram, own)
+    place = lax.axis_index("zh").reshape(1)
+    basis = solve(gram, rows, place, sub_rows, math.sqrt(width * n_panel))
     return covariance, basis[None]
 
 

time: 228 us -> 223 us (0.978)
  Pallas kernels: 9.2 us -> 14.8 us
  blocking collectives: 120 us -> 115 us
  matrix products: 3.37 us -> 0.99 us
    all_to_all x6 -> x5, blocking collectives: 75.7 us -> 58.4 us  [exchange(): return lax.all_to_all(blocks, axes, 0, 0, tiled=True)]
    all_gather x0 -> x1, blocking collectives: none -> 14.9 us  [local(): rows = jnp.sum(lax.all_gather(rows, 'zh'), axis=0)]
    pallas_call x1 -> x2, Pallas kernels: 9.2 us -> 14.8 us  [the longest x1 9.23 us: solve(): pl.pallas_call(functools.partial(solve_kernel, scale_by=scale_by), out_sh...]
    dot_general x1 -> x0, matrix products: 2.39 us -> none  [local(): sums = jnp.einsum('ztf,pta->zfpa', near, across, preferred_element_type=F32)]
where the time goes in v5:
time: 223 us; the launch traced here: 222 us
  blocking collectives  115 us (52%)
  waiting for transfers between devices  47.1 us (21%)
  starting transfers between devices  19.3 us (9%)
  between operations  14.9 us (7%)
  Pallas kernels  14.8 us (7%)
  local copies, waits for them, and re-layouts  6.17 us (3%)
  other arithmetic  3.77 us (2%)
    all_to_all x5, blocking collectives, exchange(): return lax.all_to_all(blocks, axes, 0, 0, tiled=True)  58.4 us
    all_to_all x3, waiting for transfers between devices, exchange(): return lax.all_to_all(blocks, axes, 0, 0, tiled=True)  45.2 us
    all_gather x1, blocking collectives, local(): along_z = lax.all_gather(jnp.concatenate([features, extra]), 'zh')  42.1 us
    all_to_all x3, starting transfers between devices, exchange(): return lax.all_to_all(blocks, axes, 0, 0, tiled=True)  19.3 us
    all_gather x1, blocking collectives, local(): rows = jnp.sum(lax.all_gather(rows, 'zh'), axis=0)  14.9 us
    pallas_call x1, Pallas kernels, solve(): pl.pallas_call(functools.partial(solve_kernel, scale_by=scale_by), out_sh...  9.23 us
    pallas_call x1, Pallas kernels, tile(): pl.pallas_call(tile_kernel, grid=(panels // 2,), out_shape=jax.ShapeDtype...  5.61 us
  transfers between devices with their start and end apart: 5, of which 4 were waited for; matrix products, arithmetic and copies ran while one was open for 4% of the time, Pallas kernels for 0%

profile of v5, /device:TPU:1, one launch (start us, length us, event | category | flops | bytes accessed | tf_op | source)
XLA Modules:
  0.0 222.5 jit_solution(8476259403431473772)
XLA Ops:
  7.2 0.0 all-gather.7.cloned.1.call-start
  7.2 0.7 all-gather.7.cloned.1.call-update
  7.9 0.7 reduce-precision_convert_fusion.1
  8.6 1.2 dynamic_slice.3.limit_ref
  9.9 0.9 pad_maximum_fusion
  10.8 42.1 %all-gather = bf16[3264,128]{1,0:T(8,128)(2,1)} all-gather(bf16[816,128]{1,0:T(8,128)(2,1)S(1)} %pad_maximum_fusion), channel_id=2, replica_groups=mesh['zl'=4,'x'=4,'y'=4,'zh'=4,'c'=2] {'zh'}, dimensions={0}, use_global_device_ids=true | all-gather | bytes 1044480 | tf_op jit(solution)/shard_map/all_gather | solution.py:157
  52.9 0.0 all-gather.7.cloned.1.call-done
  52.9 5.6 %tile.1 = f32[4,8,4,4,8,128]{5,4,3,2,1,0:T(8,128)} custom-call(s32[1]{0:T(128)} %dynamic_slice.3.limit_ref, bf16[4,816,128]{2,1,0:T(8,128)(2,1)} %bitcast.42, bf16[8,768,128]{2,1,0:T(8,128)(2,1)} %bitcast.47), custom_call_target="tpu_custom_call" | custom-call | tf_op jit(solution)/shard_map/tile/pallas_call | solution.py:128
  58.5 10.9 %all-to-all-start = ((f32[32,4,4,8,128]{4,3,2,1,0:T(8,128)}), f32[32,4,4,8,128]{4,3,2,1,0:T(8,128)S(1)}, u32[]{:S(2)}, u32[]{:S(2)}) async-start(f32[32,4,4,8,128]{4,3,2,1,0:T(8,128)} %bitcast.40), calls=%async_computation | async-start | bytes 4194304 | tf_op jit(solution)/shard_map/all_to_all | solution.py:24
  69.5 0.0 all-gather.9.cloned.1.call-start
  69.5 0.8 slice.20
  70.3 0.7 pad.4
  71.0 0.0 all-gather.9.cloned.1.call-update
  71.0 26.8 %all-to-all-done = f32[32,4,4,8,128]{4,3,2,1,0:T(8,128)S(1)} async-done(((f32[32,4,4,8,128]{4,3,2,1,0:T(8,128)}), f32[32,4,4,8,128]{4,3,2,1,0:T(8,128)S(1)}, u32[]{:S(2)}, u32[]{:S(2)}) %all-to-all-start) | async-done | bytes 2097184 | tf_op jit(solution)/shard_map/all_to_all | solution.py:24
  97.8 0.0 copy-start.2
  97.8 0.2 reduce_sum.72
  98.0 0.8 copy.20
  98.9 3.5 %all-to-all-start.1 = ((f32[4,8,4,8,128]{4,3,2,1,0:T(8,128)}), f32[4,8,4,8,128]{4,3,2,1,0:T(8,128)S(1)}, u32[]{:S(2)}, u32[]{:S(2)}) async-start(f32[4,8,4,8,128]{4,3,2,1,0:T(8,128)} %copy.20), calls=%async_computation.1 | async-start | bytes 1048576 | tf_op jit(solution)/shard_map/all_to_all | solution.py:24
  102.4 0.0 copy-done.2
  102.4 0.6 reduce_sum.74
  103.6 1.3 all-gather.9.cloned.1.call-done
  104.9 1.0 slice_convert_fusion
  106.0 0.2 reshape.74
  106.2 0.1 slice_add_fusion
  106.2 10.1 %all-to-all-done.1 = f32[4,8,4,8,128]{4,3,2,1,0:T(8,128)S(1)} async-done(((f32[4,8,4,8,128]{4,3,2,1,0:T(8,128)}), f32[4,8,4,8,128]{4,3,2,1,0:T(8,128)S(1)}, u32[]{:S(2)}, u32[]{:S(2)}) %all-to-all-start.1) | async-done | bytes 524320 | tf_op jit(solution)/shard_map/all_to_all | solution.py:24
  116.4 0.1 copy.22
  116.5 0.3 fusion.4
  116.8 12.8 %all_to_all.40 = f32[16,8,256]{2,1,0:T(8,128)S(1)} all-to-all(f32[16,8,256]{2,1,0:T(8,128)S(1)} %fusion.4), channel_id=1, replica_groups=mesh['zl'=4,'x'=4,'y'=4,'zh'=4,'c'=2] {'zl','x'}, dimensions={0} | all-to-all | bytes 262144 | tf_op jit(solution)/shard_map/all_to_all | solution.py:24
  129.6 10.8 %all_to_all.41 = f32[16,8,256]{2,1,0:T(8,128)S(1)} all-to-all(f32[16,8,256]{2,1,0:T(8,128)S(1)} %broadcast_in_dim.8), channel_id=1, replica_groups=mesh['zl'=4,'x'=4,'y'=4,'zh'=4,'c'=2] {'zl','x'}, dimensions={0} | all-to-all | bytes 262144 | tf_op jit(solution)/shard_map/all_to_all | solution.py:24
  140.4 0.4 fusion
  140.8 11.9 %all_to_all.42 = f32[8,32,256]{2,1,0:T(8,128)S(1)} all-to-all(f32[8,32,256]{2,1,0:T(8,128)S(1)} %fusion), channel_id=1, replica_groups=mesh['zl'=4,'x'=4,'y'=4,'zh'=4,'c'=2] {'y','c'}, dimensions={0} | all-to-all | bytes 524288 | tf_op jit(solution)/shard_map/all_to_all | solution.py:24
  152.8 14.9 %all-gather.3 = f32[128,256]{1,0:T(8,128)S(1)} all-gather(f32[32,256]{1,0:T(8,128)S(1)} %reduce_sum.76), channel_id=5, replica_groups=mesh['zl'=4,'x'=4,'y'=4,'zh'=4,'c'=2] {'zh'}, dimensions={0}, use_global_device_ids=true | all-gather | bytes 163840 | tf_op jit(solution)/shard_map/all_gather | solution.py:182
  167.7 0.0 copy-start.1
  167.7 0.1 copy.23
  167.8 0.3 fusion.2
  168.1 16.0 %all_to_all.43 = f32[32,8,256]{2,1,0:T(8,128)S(1)} all-to-all(f32[32,8,256]{2,1,0:T(8,128)S(1)} %fusion.2), channel_id=1, replica_groups=mesh['zl'=4,'x'=4,'y'=4,'zh'=4,'c'=2] {'x','y','c'}, dimensions={0} | all-to-all | bytes 524288 | tf_op jit(solution)/shard_map/all_to_all | solution.py:24
  184.1 6.9 %all_to_all.44 = f32[4,8,256]{2,1,0:T(8,128)S(1)} all-to-all(f32[4,8,256]{2,1,0:T(8,128)S(1)} %broadcast_in_dim.9), channel_id=1, replica_groups=mesh['zl'=4,'x'=4,'y'=4,'zh'=4,'c'=2] {'zl'}, dimensions={0} | all-to-all | bytes 65536 | tf_op jit(solution)/shard_map/all_to_all | solution.py:24
  191.0 0.7 broadcast_in_dim.10
  191.7 4.9 %all-to-all-start.7 = ((f32[32,8,256]{2,1,0:T(8,128)}), f32[32,8,256]{2,1,0:T(8,128)S(1)}, u32[]{:S(2)}, u32[]{:S(2)}) async-start(f32[32,8,256]{2,1,0:T(8,128)} %broadcast_in_dim.10), calls=%async_computation.7 | async-start | bytes 524288 | tf_op jit(solution)/shard_map/all_to_all | solution.py:24
  196.6 0.8 copy.24
  197.4 8.3 %all-to-all-done.7 = f32[32,8,256]{2,1,0:T(8,128)S(1)} async-done(((f32[32,8,256]{2,1,0:T(8,128)}), f32[32,8,256]{2,1,0:T(8,128)S(1)}, u32[]{:S(2)}, u32[]{:S(2)}) %all-to-all-start.7) | async-done | bytes 262176 | tf_op jit(solution)/shard_map/all_to_all | solution.py:24
  205.7 0.0 copy-start
  205.7 0.0 copy-done.1
  205.7 0.7 copy-done
  206.4 9.2 %solve.1 = f32[8,256]{1,0:T(8,128)} custom-call(s32[1]{0:T(128)} %bitcast.8.place_ref, f32[256,256]{1,0:T(8,128)} %bitcast.48, f32[32,256]{1,0:T(8,128)} %copy-done.1), custom_call_target="tpu_custom_call" | custom-call | tf_op jit(solution)/shard_map/solve/pallas_call | solution.py:90
  (12 shorter events, 0.2 us)
Async XLA Ops:
  7.2 45.8 %all-gather.7.cloned.1.call-start = ((), (), s32[]{:S(2)}) async-start(), calls=%async_computation.8 | async-start | bytes 1769472 | tf_op jit(solution)/shard_map/all_gather | solution.py:156
  58.5 39.3 %all-to-all-start = ((f32[32,4,4,8,128]{4,3,2,1,0:T(8,128)}), f32[32,4,4,8,128]{4,3,2,1,0:T(8,128)S(1)}, u32[]{:S(2)}, u32[]{:S(2)}) async-start(f32[32,4,4,8,128]{4,3,2,1,0:T(8,128)} %bitcast.40), calls=%async_computation | async-start | bytes 4194304 | tf_op jit(solution)/shard_map/all_to_all | solution.py:24
  69.5 35.4 %all-gather.9.cloned.1.call-start = ((), (), s32[]{:S(2)}) async-start(), calls=%async_computation.9 | async-start | bytes 1179648 | tf_op jit(solution)/shard_map/all_gather | solution.py:159
  97.8 4.6 %copy-start.2 = (s32[16]{0:T(128)S(1)}, s32[16]{0:T(128)}, u32[]{:S(2)}) copy-start(s32[16]{0:T(128)} %param.5) | copy-start | bytes 196
  98.9 17.4 %all-to-all-start.1 = ((f32[4,8,4,8,128]{4,3,2,1,0:T(8,128)}), f32[4,8,4,8,128]{4,3,2,1,0:T(8,128)S(1)}, u32[]{:S(2)}, u32[]{:S(2)}) async-start(f32[4,8,4,8,128]{4,3,2,1,0:T(8,128)} %copy.20), calls=%async_computation.1 | async-start | bytes 1048576 | tf_op jit(solution)/shard_map/all_to_all | solution.py:24
  167.7 38.0 %copy-start.1 = (f32[32,256]{1,0:T(8,128)}, f32[32,256]{1,0:T(8,128)S(1)}, u32[]{:S(2)}) copy-start(f32[32,256]{1,0:T(8,128)S(1)} %reduce_sum.77.rows_ref) | copy-start | bytes 98308
  191.7 14.0 %all-to-all-start.7 = ((f32[32,8,256]{2,1,0:T(8,128)}), f32[32,8,256]{2,1,0:T(8,128)S(1)}, u32[]{:S(2)}, u32[]{:S(2)}) async-start(f32[32,8,256]{2,1,0:T(8,128)} %broadcast_in_dim.10), calls=%async_computation.7 | async-start | bytes 524288 | tf_op jit(solution)/shard_map/all_to_all | solution.py:24
  205.7 0.7 copy-start
Sparse Core Ops, SparseCore 0:
  10.1 37.6 all-gather.6
  73.1 31.7 all-gather.8

commit v6 on v5

--- a/solution.py
+++ b/solution.py
@@ -15,6 +15,7 @@
 PANEL = ("y", "zh", "c")
 YC = ("y", "c")
 XYC = ("x", "y", "c")
+RAISE = 256.0
 PANEL_STEP = 64
 BLOCK = 8
 PAD_ROWS = 512
@@ -34,9 +35,16 @@
     width = held_ref.shape[1]
     lanes = width - rank
     own = rows_ref[pl.ds(pl.multiple_of(place_ref[0] * count, count), count), :]
-    padded = jnp.concatenate([own, jnp.zeros((lanes - count, rank), F32)], axis=0)
-    held_ref[:, 0:rank] = gram_ref[...]
-    held_ref[:, rank:width] = padded.T
+    gram = gram_ref[...]
+    diagonal = lax.broadcasted_iota(jnp.int32, gram.shape, 0) == lax.broadcasted_iota(
+        jnp.int32, gram.shape, 1
+    )
+    kept = jnp.where(diagonal, gram, 0.0)
+    down = 1.0 / jnp.sqrt(jnp.sum(kept, axis=1, keepdims=True))
+    along = 1.0 / jnp.sqrt(jnp.sum(kept, axis=0, keepdims=True))
+    own = jnp.concatenate([own * along, jnp.zeros((lanes - count, rank), F32)], axis=0)
+    held_ref[:, 0:rank] = gram * down * along
+    held_ref[:, rank:width] = own.T
     for first in range(0, rank, PANEL_STEP):
         last = first + PANEL_STEP
         parts = {}
@@ -62,7 +70,10 @@
             rows = [{at: part[j : j + 1] for at, part in parts.items()} for j in range(BLOCK)]
             inverse = []
             for j in range(BLOCK):
-                inverse.append(1.0 / square[j][j])
+                if j % 2 == 0:
+                    top, cross, corner = square[j][j], square[j + 1][j], square[j + 1][j + 1]
+                    inverse.append(1.0 / top)
+                    inverse.append(top * (1.0 / (top * corner - cross * cross)))
                 for i in range(j + 1, BLOCK):
                     factor = square[i][j] * inverse[j]
                     for m in range(j + 1, i + 1):
@@ -97,32 +108,29 @@
     )(place, gram, rows)
 
 
-def tile_kernel(limit_ref, near_ref, across_ref, out_ref, turned_ref):
+def tile_kernel(place_ref, counts_ref, near_ref, across_ref, out_ref, turned_ref):
     n_zh, width = near_ref.shape[0], near_ref.shape[2]
     tok_rows = across_ref.shape[1]
     n_x, pair, n_zl, _, sub_rows, _ = out_ref.shape
 
     @pl.when(pl.program_id(0) == 0)
     def turn():
-        token = lax.broadcasted_iota(jnp.int32, (tok_rows, width), 0)
-        live = jnp.where(token < limit_ref[0], 1.0, 0.0)
+        token = lax.broadcasted_iota(jnp.int32, (width, tok_rows), 1)
+        live = jnp.where(token < counts_ref[place_ref[0]], 1.0, 0.0).astype(BF16)
         for z in range(n_zh):
-            kept = near_ref[z, 0:tok_rows, :].astype(F32) * live
-            turned_ref[z * width : (z + 1) * width, :] = kept.astype(BF16).T
+            turned_ref[z * width : (z + 1) * width, :] = near_ref[z, 0:tok_rows, :].T * live
 
     both = jnp.concatenate([across_ref[p] for p in range(pair)], axis=1)
+    product = jnp.dot(turned_ref[...], both, preferred_element_type=F32)
     for z in range(n_zh):
-        product = jnp.dot(
-            turned_ref[z * width : (z + 1) * width, :], both, preferred_element_type=F32
-        )
         for low in range(n_zl):
             for x in range(n_x):
-                row = (low * n_x + x) * sub_rows
+                row = ((z * n_zl + low) * n_x + x) * sub_rows
                 for p in range(pair):
                     out_ref[x, p, low, z] = product[row : row + sub_rows, p * width : (p + 1) * width]
 
 
-def tile(limit, near, across, n_zl, n_x, sub_rows):
+def tile(place, counts, near, across, n_zl, n_x, sub_rows):
     n_zh, near_rows, width = near.shape
     panels, tok_rows = across.shape[:2]
     return pl.pallas_call(
@@ -131,13 +139,14 @@
         out_shape=jax.ShapeDtypeStruct((n_x, panels, n_zl, n_zh, sub_rows, width), F32),
         in_specs=[
             pl.BlockSpec(memory_space=pltpu.SMEM),
+            pl.BlockSpec(memory_space=pltpu.SMEM),
             pl.BlockSpec((n_zh, near_rows, width), lambda q: (0, 0, 0)),
             pl.BlockSpec((2, tok_rows, width), lambda q: (q, 0, 0)),
         ],
         out_specs=pl.BlockSpec((n_x, 2, n_zl, n_zh, sub_rows, width), lambda q: (0, q, 0, 0, 0, 0)),
         scratch_shapes=[pltpu.VMEM((n_zh * width, tok_rows), BF16)],
         name="tile",
-    )(limit, near, across)
+    )(place, counts, near, across)
 
 
 def local(features, sketch, counts):
@@ -145,7 +154,6 @@
     sub_rows, rank = sketch.shape[1:]
     n_dp, n_panel = lax.axis_size(DP), lax.axis_size(PANEL)
     n_zl, n_x, n_y, n_zh, n_c = (lax.axis_size(name) for name in DP + PANEL)
-    limit = lax.dynamic_slice_in_dim(counts, lax.axis_index(DP), 1)
     token_total = jnp.sum(counts).astype(F32)
 
     high = lax.reduce_precision(sketch[0], 8, 7)
@@ -162,7 +170,7 @@
     start = (thirds[:, :, 0] + thirds[:, :, 1]) + thirds[:, :, 2]
     start = start.reshape(n_panel * sub_rows, rank)
 
-    sums = tile(limit, along_z, across, n_zl, n_x, sub_rows)
+    sums = tile(lax.axis_index(DP).reshape(1), counts, along_z, across, n_zl, n_x, sub_rows)
     sums = sums.reshape(n_x * n_y * n_c, n_zl, n_zh, sub_rows, width)
     sums = exchange(sums, XYC).reshape(n_x, n_y * n_c, n_zl, n_zh, sub_rows, width)
     sums = jnp.sum(sums, axis=0).transpose(1, 0, 2, 3, 4)
@@ -179,7 +187,7 @@
     product = gather(product, DP).reshape(width, rank)
     product = jnp.dot(columns, product, precision=HIGH, preferred_element_type=F32)
     rows = jnp.sum(exchange(product.reshape(n_y * n_c, n_zh * sub_rows, rank), YC), axis=0)
-    rows = jnp.sum(lax.all_gather(rows, "zh"), axis=0)
+    rows = RAISE * jnp.sum(lax.all_gather(rows, "zh"), axis=0)
 
     gram = lax.dot_general(
         rows, rows, (((0,), (0,)), ((), ())), precision=HIGH, preferred_element_type=F32

time: 223 us -> 221 us (level)
  transfers between devices with their start and end apart: 5 -> 5, of which waited for: 4 -> 4; matrix products, arithmetic and copies ran while one was open for 4% -> 3% of each run, Pallas kernels for 0% -> 0%
where the time goes in v6:
time: 221 us
  blocking collectives  115 us (52%)
  waiting for transfers between devices  46.5 us (21%)
  starting transfers between devices  19.3 us (9%)
  between operations  14.9 us (7%)
  Pallas kernels  14.2 us (6%)
  local copies, waits for them, and re-layouts  4.83 us (2%)
  other arithmetic  4.38 us (2%)
    all_to_all x5, blocking collectives, exchange(): return lax.all_to_all(blocks, axes, 0, 0, tiled=True)  58.4 us
    all_to_all x3, waiting for transfers between devices, exchange(): return lax.all_to_all(blocks, axes, 0, 0, tiled=True)  44.6 us
    all_gather x1, blocking collectives, local(): along_z = lax.all_gather(jnp.concatenate([features, extra]), 'zh')  42.1 us
    all_to_all x3, starting transfers between devices, exchange(): return lax.all_to_all(blocks, axes, 0, 0, tiled=True)  19.3 us
    all_gather x1, blocking collectives, local(): rows = RAISE * jnp.sum(lax.all_gather(rows, 'zh'), axis=0)  14.9 us
    pallas_call x1, Pallas kernels, solve(): pl.pallas_call(functools.partial(solve_kernel, scale_by=scale_by), out_sh...  9.26 us
    pallas_call x1, Pallas kernels, tile(): pl.pallas_call(tile_kernel, grid=(panels // 2,), out_shape=jax.ShapeDtype...  4.95 us
  transfers between devices with their start and end apart: 5, of which 4 were waited for; matrix products, arithmetic and copies ran while one was open for 3% of the time, Pallas kernels for 0%

profile of v6, /device:TPU:1, one launch (start us, length us, event | category | flops | bytes accessed | tf_op | source)
XLA Modules:
  0.0 220.5 jit_solution(3605937082639754392)
XLA Ops:
  7.2 0.0 all-gather.7.cloned.1.call-start
  7.2 0.7 all-gather.7.cloned.1.call-update
  7.9 0.7 reduce-precision_convert_fusion.1
  8.6 0.9 pad_maximum_fusion
  9.6 42.1 %all-gather = bf16[3264,128]{1,0:T(8,128)(2,1)} all-gather(bf16[816,128]{1,0:T(8,128)(2,1)S(1)} %pad_maximum_fusion), channel_id=2, replica_groups=mesh['zl'=4,'x'=4,'y'=4,'zh'=4,'c'=2] {'zh'}, dimensions={0}, use_global_device_ids=true | all-gather | bytes 1044480 | tf_op jit(solution)/shard_map/all_gather | solution.py:165
  51.7 0.0 all-gather.7.cloned.1.call-done
  51.7 4.9 %tile.1 = f32[4,8,4,4,8,128]{5,4,3,2,1,0:T(8,128)} custom-call(s32[1]{0:T(128)} %bitcast.place_ref, s32[16]{0:T(128)} %counts_ref.1, bf16[4,816,128]{2,1,0:T(8,128)(2,1)} %bitcast.38, bf16[8,768,128]{2,1,0:T(8,128)(2,1)} %bitcast.43), custom_call_target="tpu_custom_call" | custom-call | tf_op jit(solution)/shard_map/tile/pallas_call | solution.py:136
  56.6 10.9 %all-to-all-start = ((f32[32,4,4,8,128]{4,3,2,1,0:T(8,128)}), f32[32,4,4,8,128]{4,3,2,1,0:T(8,128)S(1)}, u32[]{:S(2)}, u32[]{:S(2)}) async-start(f32[32,4,4,8,128]{4,3,2,1,0:T(8,128)} %bitcast.36), calls=%async_computation | async-start | bytes 4194304 | tf_op jit(solution)/shard_map/all_to_all | solution.py:25
  67.6 0.0 all-gather.9.cloned.1.call-start
  67.6 0.8 slice.20
  68.4 0.7 pad.4
  69.1 0.0 all-gather.9.cloned.1.call-update
  69.1 26.8 %all-to-all-done = f32[32,4,4,8,128]{4,3,2,1,0:T(8,128)S(1)} async-done(((f32[32,4,4,8,128]{4,3,2,1,0:T(8,128)}), f32[32,4,4,8,128]{4,3,2,1,0:T(8,128)S(1)}, u32[]{:S(2)}, u32[]{:S(2)}) %all-to-all-start) | async-done | bytes 2097184 | tf_op jit(solution)/shard_map/all_to_all | solution.py:25
  95.9 0.0 copy-start.1
  95.9 0.2 reduce_sum.72
  96.1 0.8 copy.16
  97.0 3.5 %all-to-all-start.1 = ((f32[4,8,4,8,128]{4,3,2,1,0:T(8,128)}), f32[4,8,4,8,128]{4,3,2,1,0:T(8,128)S(1)}, u32[]{:S(2)}, u32[]{:S(2)}) async-start(f32[4,8,4,8,128]{4,3,2,1,0:T(8,128)} %copy.16), calls=%async_computation.1 | async-start | bytes 1048576 | tf_op jit(solution)/shard_map/all_to_all | solution.py:25
  100.5 0.0 copy-done.1
  100.5 0.6 reduce_sum.74
  101.8 1.3 all-gather.9.cloned.1.call-done
  103.0 1.0 slice_convert_fusion
  104.1 0.2 reshape.80
  104.3 0.1 slice_add_fusion
  104.3 10.1 %all-to-all-done.1 = f32[4,8,4,8,128]{4,3,2,1,0:T(8,128)S(1)} async-done(((f32[4,8,4,8,128]{4,3,2,1,0:T(8,128)}), f32[4,8,4,8,128]{4,3,2,1,0:T(8,128)S(1)}, u32[]{:S(2)}, u32[]{:S(2)}) %all-to-all-start.1) | async-done | bytes 524320 | tf_op jit(solution)/shard_map/all_to_all | solution.py:25
  114.5 0.1 copy.18
  114.6 0.3 fusion.2
  114.9 12.8 %all_to_all.40 = f32[16,8,256]{2,1,0:T(8,128)S(1)} all-to-all(f32[16,8,256]{2,1,0:T(8,128)S(1)} %fusion.2), channel_id=1, replica_groups=mesh['zl'=4,'x'=4,'y'=4,'zh'=4,'c'=2] {'zl','x'}, dimensions={0} | all-to-all | bytes 262144 | tf_op jit(solution)/shard_map/all_to_all | solution.py:25
  127.7 10.8 %all_to_all.41 = f32[16,8,256]{2,1,0:T(8,128)S(1)} all-to-all(f32[16,8,256]{2,1,0:T(8,128)S(1)} %broadcast_in_dim.8), channel_id=1, replica_groups=mesh['zl'=4,'x'=4,'y'=4,'zh'=4,'c'=2] {'zl','x'}, dimensions={0} | all-to-all | bytes 262144 | tf_op jit(solution)/shard_map/all_to_all | solution.py:25
  138.5 0.4 fusion
  138.9 11.9 %all_to_all.42 = f32[8,32,256]{2,1,0:T(8,128)S(1)} all-to-all(f32[8,32,256]{2,1,0:T(8,128)S(1)} %fusion), channel_id=1, replica_groups=mesh['zl'=4,'x'=4,'y'=4,'zh'=4,'c'=2] {'y','c'}, dimensions={0} | all-to-all | bytes 524288 | tf_op jit(solution)/shard_map/all_to_all | solution.py:25
  150.9 14.9 %all-gather.3 = f32[128,256]{1,0:T(8,128)S(1)} all-gather(f32[32,256]{1,0:T(8,128)S(1)} %reduce_sum.76), channel_id=5, replica_groups=mesh['zl'=4,'x'=4,'y'=4,'zh'=4,'c'=2] {'zh'}, dimensions={0}, use_global_device_ids=true | all-gather | bytes 163840 | tf_op jit(solution)/shard_map/all_gather | solution.py:190
  165.7 0.4 convolution_bitcast_fusion
  166.2 16.0 %all_to_all.43 = f32[32,8,256]{2,1,0:T(8,128)S(1)} all-to-all(f32[32,8,256]{2,1,0:T(8,128)S(1)} %convolution_bitcast_fusion), channel_id=1, replica_groups=mesh['zl'=4,'x'=4,'y'=4,'zh'=4,'c'=2] {'x','y','c'}, dimensions={0} | all-to-all | bytes 524288 | tf_op jit(solution)/shard_map/all_to_all | solution.py:25
  182.2 6.9 %all_to_all.44 = f32[4,8,256]{2,1,0:T(8,128)S(1)} all-to-all(f32[4,8,256]{2,1,0:T(8,128)S(1)} %broadcast_in_dim.9), channel_id=1, replica_groups=mesh['zl'=4,'x'=4,'y'=4,'zh'=4,'c'=2] {'zl'}, dimensions={0} | all-to-all | bytes 65536 | tf_op jit(solution)/shard_map/all_to_all | solution.py:25
  189.1 0.7 broadcast_in_dim.10
  189.8 4.9 %all-to-all-start.7 = ((f32[32,8,256]{2,1,0:T(8,128)}), f32[32,8,256]{2,1,0:T(8,128)S(1)}, u32[]{:S(2)}, u32[]{:S(2)}) async-start(f32[32,8,256]{2,1,0:T(8,128)} %broadcast_in_dim.10), calls=%async_computation.7 | async-start | bytes 524288 | tf_op jit(solution)/shard_map/all_to_all | solution.py:25
  194.7 0.8 copy.19
  195.4 0.6 broadcast_multiply_fusion.rows_ref
  196.0 7.7 %all-to-all-done.7 = f32[32,8,256]{2,1,0:T(8,128)S(1)} async-done(((f32[32,8,256]{2,1,0:T(8,128)}), f32[32,8,256]{2,1,0:T(8,128)S(1)}, u32[]{:S(2)}, u32[]{:S(2)}) %all-to-all-start.7) | async-done | bytes 262176 | tf_op jit(solution)/shard_map/all_to_all | solution.py:25
  203.8 0.0 copy-start
  203.8 0.7 copy-done
  204.4 9.3 %solve.1 = f32[8,256]{1,0:T(8,128)} custom-call(s32[1]{0:T(128)} %bitcast.9.place_ref, f32[256,256]{1,0:T(8,128)} %bitcast.44, f32[32,256]{1,0:T(8,128)} %broadcast_multiply_fusion.rows_ref), custom_call_target="tpu_custom_call" | custom-call | tf_op jit(solution)/shard_map/solve/pallas_call | solution.py:101
  (12 shorter events, 0.2 us)
Async XLA Ops:
  7.2 44.5 %all-gather.7.cloned.1.call-start = ((), (), s32[]{:S(2)}) async-start(), calls=%async_computation.8 | async-start | bytes 1769472 | tf_op jit(solution)/shard_map/all_gather | solution.py:164
  56.6 39.3 %all-to-all-start = ((f32[32,4,4,8,128]{4,3,2,1,0:T(8,128)}), f32[32,4,4,8,128]{4,3,2,1,0:T(8,128)S(1)}, u32[]{:S(2)}, u32[]{:S(2)}) async-start(f32[32,4,4,8,128]{4,3,2,1,0:T(8,128)} %bitcast.36), calls=%async_computation | async-start | bytes 4194304 | tf_op jit(solution)/shard_map/all_to_all | solution.py:25
  67.6 35.4 %all-gather.9.cloned.1.call-start = ((), (), s32[]{:S(2)}) async-start(), calls=%async_computation.9 | async-start | bytes 1179648 | tf_op jit(solution)/shard_map/all_gather | solution.py:167
  95.9 4.6 %copy-start.1 = (s32[16]{0:T(128)S(1)}, s32[16]{0:T(128)}, u32[]{:S(2)}) copy-start(s32[16]{0:T(128)} %counts_ref.1) | copy-start | bytes 196
  97.0 17.4 %all-to-all-start.1 = ((f32[4,8,4,8,128]{4,3,2,1,0:T(8,128)}), f32[4,8,4,8,128]{4,3,2,1,0:T(8,128)S(1)}, u32[]{:S(2)}, u32[]{:S(2)}) async-start(f32[4,8,4,8,128]{4,3,2,1,0:T(8,128)} %copy.16), calls=%async_computation.1 | async-start | bytes 1048576 | tf_op jit(solution)/shard_map/all_to_all | solution.py:25
  189.8 14.0 %all-to-all-start.7 = ((f32[32,8,256]{2,1,0:T(8,128)}), f32[32,8,256]{2,1,0:T(8,128)S(1)}, u32[]{:S(2)}, u32[]{:S(2)}) async-start(f32[32,8,256]{2,1,0:T(8,128)} %broadcast_in_dim.10), calls=%async_computation.7 | async-start | bytes 524288 | tf_op jit(solution)/shard_map/all_to_all | solution.py:25
  203.8 0.7 copy-start
Sparse Core Ops, SparseCore 0:
  10.1 37.6 all-gather.6
  71.2 31.7 all-gather.8

commit v7 on v6

--- a/solution.py
+++ b/solution.py
@@ -16,6 +16,7 @@
 YC = ("y", "c")
 XYC = ("x", "y", "c")
 RAISE = 256.0
+KERNEL_VMEM = 16 * 2**20
 PANEL_STEP = 64
 BLOCK = 8
 PAD_ROWS = 512
@@ -104,6 +105,7 @@
         in_specs=[pl.BlockSpec(memory_space=pltpu.SMEM), vmem, vmem],
         out_specs=vmem,
         scratch_shapes=[pltpu.VMEM((rank, rank + 128), F32)],
+        compiler_params=pltpu.CompilerParams(vmem_limit_bytes=KERNEL_VMEM),
         name="solve",
     )(place, gram, rows)
 
@@ -111,40 +113,33 @@
 def tile_kernel(place_ref, counts_ref, near_ref, across_ref, out_ref, turned_ref):
     n_zh, width = near_ref.shape[0], near_ref.shape[2]
     tok_rows = across_ref.shape[1]
-    n_x, pair, n_zl, _, sub_rows, _ = out_ref.shape
-
-    @pl.when(pl.program_id(0) == 0)
-    def turn():
-        token = lax.broadcasted_iota(jnp.int32, (width, tok_rows), 1)
-        live = jnp.where(token < counts_ref[place_ref[0]], 1.0, 0.0).astype(BF16)
-        for z in range(n_zh):
-            turned_ref[z * width : (z + 1) * width, :] = near_ref[z, 0:tok_rows, :].T * live
-
-    both = jnp.concatenate([across_ref[p] for p in range(pair)], axis=1)
-    product = jnp.dot(turned_ref[...], both, preferred_element_type=F32)
+    n_x, panels, n_zl, _, sub_rows, _ = out_ref.shape
+    token = lax.broadcasted_iota(jnp.int32, (width, tok_rows), 1)
+    live = jnp.where(token < counts_ref[place_ref[0]], 1.0, 0.0).astype(BF16)
+    for z in range(n_zh):
+        turned_ref[z * width : (z + 1) * width, :] = near_ref[z, 0:tok_rows, :].T * live
+    beside = jnp.concatenate([across_ref[p] for p in range(panels)], axis=1)
+    product = jnp.dot(turned_ref[...], beside, preferred_element_type=F32)
     for z in range(n_zh):
         for low in range(n_zl):
             for x in range(n_x):
                 row = ((z * n_zl + low) * n_x + x) * sub_rows
-                for p in range(pair):
+                for p in range(panels):
                     out_ref[x, p, low, z] = product[row : row + sub_rows, p * width : (p + 1) * width]
 
 
 def tile(place, counts, near, across, n_zl, n_x, sub_rows):
-    n_zh, near_rows, width = near.shape
+    n_zh, width = near.shape[0], near.shape[2]
     panels, tok_rows = across.shape[:2]
+    smem = pl.BlockSpec(memory_space=pltpu.SMEM)
+    vmem = pl.BlockSpec(memory_space=pltpu.VMEM)
     return pl.pallas_call(
         tile_kernel,
-        grid=(panels // 2,),
         out_shape=jax.ShapeDtypeStruct((n_x, panels, n_zl, n_zh, sub_rows, width), F32),
-        in_specs=[
-            pl.BlockSpec(memory_space=pltpu.SMEM),
-            pl.BlockSpec(memory_space=pltpu.SMEM),
-            pl.BlockSpec((n_zh, near_rows, width), lambda q: (0, 0, 0)),
-            pl.BlockSpec((2, tok_rows, width), lambda q: (q, 0, 0)),
-        ],
-        out_specs=pl.BlockSpec((n_x, 2, n_zl, n_zh, sub_rows, width), lambda q: (0, q, 0, 0, 0, 0)),
+        in_specs=[smem, smem, vmem, vmem],
+        out_specs=vmem,
         scratch_shapes=[pltpu.VMEM((n_zh * width, tok_rows), BF16)],
+        compiler_params=pltpu.CompilerParams(vmem_limit_bytes=KERNEL_VMEM),
         name="tile",
     )(place, counts, near, across)
 

time: 221 us -> 221 us (level)
  Pallas kernels: 14.2 us -> 11.2 us
  blocking collectives: 115 us -> 118 us
where the time goes in v7:
time: 221 us; the launch traced here: 220 us
  blocking collectives  118 us (53%)
  waiting for transfers between devices  47.9 us (22%)
  starting transfers between devices  18.5 us (8%)
  between operations  14.9 us (7%)
  Pallas kernels  11.2 us (5%)
  local copies, waits for them, and re-layouts  5.4 us (2%)
  other arithmetic  3.8 us (2%)
    all_to_all x5, blocking collectives, exchange(): return lax.all_to_all(blocks, axes, 0, 0, tiled=True)  58.5 us
    all_to_all x3, waiting for transfers between devices, exchange(): return lax.all_to_all(blocks, axes, 0, 0, tiled=True)  46 us
    all_gather x1, blocking collectives, local(): along_z = lax.all_gather(jnp.concatenate([features, extra]), 'zh')  44.2 us
    all_to_all x3, starting transfers between devices, exchange(): return lax.all_to_all(blocks, axes, 0, 0, tiled=True)  18.4 us
    all_gather x1, blocking collectives, local(): rows = RAISE * jnp.sum(lax.all_gather(rows, 'zh'), axis=0)  14.8 us
    pallas_call x1, Pallas kernels, solve(): pl.pallas_call(functools.partial(solve_kernel, scale_by=scale_by), out_sh...  8.31 us
  transfers between devices with their start and end apart: 5, of which 4 were waited for; matrix products, arithmetic and copies ran while one was open for 3% of the time, Pallas kernels for 0%

profile of v7, /device:TPU:1, one launch (start us, length us, event | category | flops | bytes accessed | tf_op | source)
XLA Modules:
  0.0 220.3 jit_solution(17195981550353559373)
XLA Ops:
  7.2 0.0 all-gather.7.cloned.1.call-start
  7.2 0.7 all-gather.7.cloned.1.call-update
  7.9 0.7 reduce-precision_convert_fusion.1
  8.6 0.9 pad_maximum_fusion
  9.6 44.2 %all-gather = bf16[3264,128]{1,0:T(8,128)(2,1)S(1)} all-gather(bf16[816,128]{1,0:T(8,128)(2,1)S(1)} %pad_maximum_fusion), channel_id=2, replica_groups=mesh['zl'=4,'x'=4,'y'=4,'zh'=4,'c'=2] {'zh'}, dimensions={0}, use_global_device_ids=true | all-gather | bytes 1044480 | tf_op jit(solution)/shard_map/all_gather | solution.py:160
  53.8 0.0 all-gather.7.cloned.1.call-done
  53.8 0.0 copy-start
  53.8 1.4 copy-done
  55.2 0.0 copy-start.1
  55.2 0.7 copy-done.1
  55.9 2.9 %tile.1 = f32[4,8,4,4,8,128]{5,4,3,2,1,0:T(8,128)} custom-call(s32[1]{0:T(128)} %bitcast.place_ref, s32[16]{0:T(128)S(1)} %copy-done.1, bf16[4,816,128]{2,1,0:T(8,128)(2,1)S(1)} %bitcast.36, bf16[8,768,128]{2,1,0:T(8,128)(2,1)S(1)} %bitcast.38), custom_call_target="tpu_custom_call" | custom-call | tf_op jit(solution)/shard_map/tile/pallas_call | solution.py:136
  58.8 10.1 %all-to-all-start = ((f32[32,4,4,8,128]{4,3,2,1,0:T(8,128)}), f32[32,4,4,8,128]{4,3,2,1,0:T(8,128)S(1)}, u32[]{:S(2)}, u32[]{:S(2)}) async-start(f32[32,4,4,8,128]{4,3,2,1,0:T(8,128)} %bitcast.3), calls=%async_computation | async-start | bytes 4194304 | tf_op jit(solution)/shard_map/all_to_all | solution.py:26
  68.9 0.0 all-gather.9.cloned.1.call-start
  69.0 0.7 pad.4
  69.6 0.0 all-gather.9.cloned.1.call-update
  69.7 27.6 %all-to-all-done = f32[32,4,4,8,128]{4,3,2,1,0:T(8,128)S(1)} async-done(((f32[32,4,4,8,128]{4,3,2,1,0:T(8,128)}), f32[32,4,4,8,128]{4,3,2,1,0:T(8,128)S(1)}, u32[]{:S(2)}, u32[]{:S(2)}) %all-to-all-start) | async-done | bytes 2097184 | tf_op jit(solution)/shard_map/all_to_all | solution.py:26
  97.2 0.0 copy-start.2
  97.2 0.3 reduce_sum.72
  97.5 0.8 copy.16
  98.3 3.5 %all-to-all-start.1 = ((f32[4,8,4,8,128]{4,3,2,1,0:T(8,128)}), f32[4,8,4,8,128]{4,3,2,1,0:T(8,128)S(1)}, u32[]{:S(2)}, u32[]{:S(2)}) async-start(f32[4,8,4,8,128]{4,3,2,1,0:T(8,128)} %copy.16), calls=%async_computation.1 | async-start | bytes 1048576 | tf_op jit(solution)/shard_map/all_to_all | solution.py:26
  101.8 0.0 copy-done.2
  101.8 0.6 reduce_sum.74
  103.1 1.2 all-gather.9.cloned.1.call-done
  104.3 1.0 slice_convert_fusion
  105.4 0.2 reshape.80
  105.6 0.1 slice_add_fusion
  105.7 10.1 %all-to-all-done.1 = f32[4,8,4,8,128]{4,3,2,1,0:T(8,128)S(1)} async-done(((f32[4,8,4,8,128]{4,3,2,1,0:T(8,128)}), f32[4,8,4,8,128]{4,3,2,1,0:T(8,128)S(1)}, u32[]{:S(2)}, u32[]{:S(2)}) %all-to-all-start.1) | async-done | bytes 524320 | tf_op jit(solution)/shard_map/all_to_all | solution.py:26
  115.8 0.1 copy.18
  115.9 0.3 fusion.2
  116.2 12.9 %all_to_all.40 = f32[16,8,256]{2,1,0:T(8,128)S(1)} all-to-all(f32[16,8,256]{2,1,0:T(8,128)S(1)} %fusion.2), channel_id=1, replica_groups=mesh['zl'=4,'x'=4,'y'=4,'zh'=4,'c'=2] {'zl','x'}, dimensions={0} | all-to-all | bytes 262144 | tf_op jit(solution)/shard_map/all_to_all | solution.py:26
  129.2 11.3 %all_to_all.41 = f32[16,8,256]{2,1,0:T(8,128)S(1)} all-to-all(f32[16,8,256]{2,1,0:T(8,128)S(1)} %broadcast_in_dim.8), channel_id=1, replica_groups=mesh['zl'=4,'x'=4,'y'=4,'zh'=4,'c'=2] {'zl','x'}, dimensions={0} | all-to-all | bytes 262144 | tf_op jit(solution)/shard_map/all_to_all | solution.py:26
  140.5 0.4 fusion
  140.9 11.3 %all_to_all.42 = f32[8,32,256]{2,1,0:T(8,128)S(1)} all-to-all(f32[8,32,256]{2,1,0:T(8,128)S(1)} %fusion), channel_id=1, replica_groups=mesh['zl'=4,'x'=4,'y'=4,'zh'=4,'c'=2] {'y','c'}, dimensions={0} | all-to-all | bytes 524288 | tf_op jit(solution)/shard_map/all_to_all | solution.py:26
  152.2 14.8 %all-gather.3 = f32[128,256]{1,0:T(8,128)S(1)} all-gather(f32[32,256]{1,0:T(8,128)S(1)} %reduce_sum.76), channel_id=5, replica_groups=mesh['zl'=4,'x'=4,'y'=4,'zh'=4,'c'=2] {'zh'}, dimensions={0}, use_global_device_ids=true | all-gather | bytes 163840 | tf_op jit(solution)/shard_map/all_gather | solution.py:185
  167.1 0.4 convolution_bitcast_fusion
  167.5 16.1 %all_to_all.43 = f32[32,8,256]{2,1,0:T(8,128)S(1)} all-to-all(f32[32,8,256]{2,1,0:T(8,128)S(1)} %convolution_bitcast_fusion), channel_id=1, replica_groups=mesh['zl'=4,'x'=4,'y'=4,'zh'=4,'c'=2] {'x','y','c'}, dimensions={0} | all-to-all | bytes 524288 | tf_op jit(solution)/shard_map/all_to_all | solution.py:26
  183.6 6.9 %all_to_all.44 = f32[4,8,256]{2,1,0:T(8,128)S(1)} all-to-all(f32[4,8,256]{2,1,0:T(8,128)S(1)} %broadcast_in_dim.9), channel_id=1, replica_groups=mesh['zl'=4,'x'=4,'y'=4,'zh'=4,'c'=2] {'zl'}, dimensions={0} | all-to-all | bytes 65536 | tf_op jit(solution)/shard_map/all_to_all | solution.py:26
  190.5 0.7 broadcast_in_dim.10
  191.2 4.9 %all-to-all-start.7 = ((f32[32,8,256]{2,1,0:T(8,128)}), f32[32,8,256]{2,1,0:T(8,128)S(1)}, u32[]{:S(2)}, u32[]{:S(2)}) async-start(f32[32,8,256]{2,1,0:T(8,128)} %broadcast_in_dim.10), calls=%async_computation.7 | async-start | bytes 524288 | tf_op jit(solution)/shard_map/all_to_all | solution.py:26
  196.1 0.8 copy.19
  196.8 8.3 %all-to-all-done.7 = f32[32,8,256]{2,1,0:T(8,128)S(1)} async-done(((f32[32,8,256]{2,1,0:T(8,128)}), f32[32,8,256]{2,1,0:T(8,128)S(1)}, u32[]{:S(2)}, u32[]{:S(2)}) %all-to-all-start.7) | async-done | bytes 262176 | tf_op jit(solution)/shard_map/all_to_all | solution.py:26
  205.2 8.3 %solve.1 = f32[8,256]{1,0:T(8,128)} custom-call(s32[1]{0:T(128)} %bitcast.9.place_ref, f32[256,256]{1,0:T(8,128)S(1)} %bitcast.39, f32[32,256]{1,0:T(8,128)S(1)} %broadcast_multiply_fusion.rows_ref), custom_call_target="tpu_custom_call" | custom-call | tf_op jit(solution)/shard_map/solve/pallas_call | solution.py:102
  (14 shorter events, 0.2 us)
Async XLA Ops:
  7.2 46.7 %all-gather.7.cloned.1.call-start = ((), (), s32[]{:S(2)}) async-start(), calls=%async_computation.8 | async-start | bytes 1769472 | tf_op jit(solution)/shard_map/all_gather | solution.py:159
  53.8 1.4 copy-start
  55.2 0.7 copy-start.1
  58.8 38.4 %all-to-all-start = ((f32[32,4,4,8,128]{4,3,2,1,0:T(8,128)}), f32[32,4,4,8,128]{4,3,2,1,0:T(8,128)S(1)}, u32[]{:S(2)}, u32[]{:S(2)}) async-start(f32[32,4,4,8,128]{4,3,2,1,0:T(8,128)} %bitcast.3), calls=%async_computation | async-start | bytes 4194304 | tf_op jit(solution)/shard_map/all_to_all | solution.py:26
  68.9 35.4 %all-gather.9.cloned.1.call-start = ((), (), s32[]{:S(2)}) async-start(), calls=%async_computation.9 | async-start | bytes 1179648 | tf_op jit(solution)/shard_map/all_gather | solution.py:162
  97.2 4.6 %copy-start.2 = (s32[16]{0:T(128)S(1)}, s32[16]{0:T(128)}, u32[]{:S(2)}) copy-start(s32[16]{0:T(128)} %counts_ref.1) | copy-start | bytes 196
  98.3 17.4 %all-to-all-start.1 = ((f32[4,8,4,8,128]{4,3,2,1,0:T(8,128)}), f32[4,8,4,8,128]{4,3,2,1,0:T(8,128)S(1)}, u32[]{:S(2)}, u32[]{:S(2)}) async-start(f32[4,8,4,8,128]{4,3,2,1,0:T(8,128)} %copy.16), calls=%async_computation.1 | async-start | bytes 1048576 | tf_op jit(solution)/shard_map/all_to_all | solution.py:26
  191.2 14.0 %all-to-all-start.7 = ((f32[32,8,256]{2,1,0:T(8,128)}), f32[32,8,256]{2,1,0:T(8,128)S(1)}, u32[]{:S(2)}, u32[]{:S(2)}) async-start(f32[32,8,256]{2,1,0:T(8,128)} %broadcast_in_dim.10), calls=%async_computation.7 | async-start | bytes 524288 | tf_op jit(solution)/shard_map/all_to_all | solution.py:26
Sparse Core Ops, SparseCore 0:
  10.1 37.9 all-gather.6
  72.5 31.7 all-gather.8

commit v8 on v7

--- a/solution.py
+++ b/solution.py
@@ -110,36 +110,73 @@
     )(place, gram, rows)
 
 
-def tile_kernel(place_ref, counts_ref, near_ref, across_ref, out_ref, turned_ref):
-    n_zh, width = near_ref.shape[0], near_ref.shape[2]
-    tok_rows = across_ref.shape[1]
-    n_x, panels, n_zl, _, sub_rows, _ = out_ref.shape
+def tile_kernel(
+    place_ref, counts_ref, near_any, across_any, out_any,
+    near_ref, across_ref, out_ref, turned_ref, near_sem, across_sem, out_sem,
+):
+    n_zh, tok_rows, width = near_ref.shape
+    halves, panels = across_ref.shape[:2]
+    n_x, n_zl, sub_rows = out_ref.shape[1], out_ref.shape[3], out_ref.shape[5]
+    near_copies = [
+        pltpu.make_async_copy(near_any.at[z, 0:tok_rows], near_ref.at[z], near_sem.at[z])
+        for z in range(n_zh)
+    ]
+    across_copies = [
+        pltpu.make_async_copy(
+            across_any.at[h * panels : (h + 1) * panels], across_ref.at[h], across_sem.at[h]
+        )
+        for h in range(halves)
+    ]
+    out_copies = [
+        pltpu.make_async_copy(
+            out_ref.at[h], out_any.at[:, h * panels : (h + 1) * panels], out_sem.at[h]
+        )
+        for h in range(halves)
+    ]
+    for copy in near_copies + across_copies:
+        copy.start()
     token = lax.broadcasted_iota(jnp.int32, (width, tok_rows), 1)
     live = jnp.where(token < counts_ref[place_ref[0]], 1.0, 0.0).astype(BF16)
     for z in range(n_zh):
-        turned_ref[z * width : (z + 1) * width, :] = near_ref[z, 0:tok_rows, :].T * live
-    beside = jnp.concatenate([across_ref[p] for p in range(panels)], axis=1)
-    product = jnp.dot(turned_ref[...], beside, preferred_element_type=F32)
-    for z in range(n_zh):
-        for low in range(n_zl):
-            for x in range(n_x):
-                row = ((z * n_zl + low) * n_x + x) * sub_rows
-                for p in range(panels):
-                    out_ref[x, p, low, z] = product[row : row + sub_rows, p * width : (p + 1) * width]
+        near_copies[z].wait()
+        turned_ref[z * width : (z + 1) * width, :] = near_ref[z].T * live
+    for h in range(halves):
+        across_copies[h].wait()
+        beside = jnp.concatenate([across_ref[h, p] for p in range(panels)], axis=1)
+        product = jnp.dot(turned_ref[...], beside, preferred_element_type=F32)
+        for z in range(n_zh):
+            for low in range(n_zl):
+                for x in range(n_x):
+                    row = ((z * n_zl + low) * n_x + x) * sub_rows
+                    for p in range(panels):
+                        out_ref[h, x, p, low, z] = product[
+                            row : row + sub_rows, p * width : (p + 1) * width
+                        ]
+        out_copies[h].start()
+    for copy in out_copies:
+        copy.wait()
 
 
 def tile(place, counts, near, across, n_zl, n_x, sub_rows):
     n_zh, width = near.shape[0], near.shape[2]
     panels, tok_rows = across.shape[:2]
+    half = panels // 2
     smem = pl.BlockSpec(memory_space=pltpu.SMEM)
-    vmem = pl.BlockSpec(memory_space=pltpu.VMEM)
+    anywhere = pl.BlockSpec(memory_space=pl.ANY)
     return pl.pallas_call(
         tile_kernel,
         out_shape=jax.ShapeDtypeStruct((n_x, panels, n_zl, n_zh, sub_rows, width), F32),
-        in_specs=[smem, smem, vmem, vmem],
-        out_specs=vmem,
-        scratch_shapes=[pltpu.VMEM((n_zh * width, tok_rows), BF16)],
-        compiler_params=pltpu.CompilerParams(vmem_limit_bytes=KERNEL_VMEM),
+        in_specs=[smem, smem, anywhere, anywhere],
+        out_specs=anywhere,
+        scratch_shapes=[
+            pltpu.VMEM((n_zh, tok_rows, width), BF16),
+            pltpu.VMEM((2, half, tok_rows, width), BF16),
+            pltpu.VMEM((2, n_x, half, n_zl, n_zh, sub_rows, width), F32),
+            pltpu.VMEM((n_zh * width, tok_rows), BF16),
+            pltpu.SemaphoreType.DMA((n_zh,)),
+            pltpu.SemaphoreType.DMA((2,)),
+            pltpu.SemaphoreType.DMA((2,)),
+        ],
         name="tile",
     )(place, counts, near, across)
 

time: 221 us -> 219 us (level)
  blocking collectives: 118 us -> 115 us
where the time goes in v8:
time: 219 us; the launch traced here: 218 us
  blocking collectives  115 us (53%)
  waiting for transfers between devices  47.1 us (22%)
  starting transfers between devices  19.4 us (9%)
  between operations  14.9 us (7%)
  Pallas kernels  12.8 us (6%)
  local copies, waits for them, and re-layouts  4.14 us (2%)
  other arithmetic  3.78 us (2%)
    all_to_all x5, blocking collectives, exchange(): return lax.all_to_all(blocks, axes, 0, 0, tiled=True)  58.4 us
    all_to_all x3, waiting for transfers between devices, exchange(): return lax.all_to_all(blocks, axes, 0, 0, tiled=True)  45.1 us
    all_gather x1, blocking collectives, local(): along_z = lax.all_gather(jnp.concatenate([features, extra]), 'zh')  42.1 us
    all_to_all x3, starting transfers between devices, exchange(): return lax.all_to_all(blocks, axes, 0, 0, tiled=True)  19.3 us
    all_gather x1, blocking collectives, local(): rows = RAISE * jnp.sum(lax.all_gather(rows, 'zh'), axis=0)  14.9 us
    pallas_call x1, Pallas kernels, solve(): pl.pallas_call(functools.partial(solve_kernel, scale_by=scale_by), out_sh...  8.31 us
    pallas_call x1, Pallas kernels, tile(): pl.pallas_call(tile_kernel, out_shape=jax.ShapeDtypeStruct((n_x, panels,...  4.46 us
  transfers between devices with their start and end apart: 5, of which 4 were waited for; matrix products, arithmetic and copies ran while one was open for 3% of the time, Pallas kernels for 0%

profile of v8, /device:TPU:1, one launch (start us, length us, event | category | flops | bytes accessed | tf_op | source)
XLA Modules:
  0.0 218.4 jit_solution(10667960984134255301)
XLA Ops:
  7.2 0.0 all-gather.7.cloned.1.call-start
  7.2 0.7 all-gather.7.cloned.1.call-update
  7.9 0.7 reduce-precision_convert_fusion.1
  8.6 0.9 pad_maximum_fusion
  9.6 42.1 %all-gather = bf16[3264,128]{1,0:T(8,128)(2,1)} all-gather(bf16[816,128]{1,0:T(8,128)(2,1)S(1)} %pad_maximum_fusion), channel_id=2, replica_groups=mesh['zl'=4,'x'=4,'y'=4,'zh'=4,'c'=2] {'zh'}, dimensions={0}, use_global_device_ids=true | all-gather | bytes 1044480 | tf_op jit(solution)/shard_map/all_gather | solution.py:197
  51.7 0.0 all-gather.7.cloned.1.call-done
  51.7 4.5 %tile.1 = f32[4,8,4,4,8,128]{5,4,3,2,1,0:T(8,128)} custom-call(s32[1]{0:T(128)} %bitcast.place_ref, s32[16]{0:T(128)} %counts_ref.1, bf16[4,816,128]{2,1,0:T(8,128)(2,1)} %bitcast.39, bf16[8,768,128]{2,1,0:T(8,128)(2,1)} %bitcast.44), custom_call_target="tpu_custom_call" | custom-call | tf_op jit(solution)/shard_map/tile/pallas_call | solution.py:166
  56.2 10.9 %all-to-all-start = ((f32[32,4,4,8,128]{4,3,2,1,0:T(8,128)}), f32[32,4,4,8,128]{4,3,2,1,0:T(8,128)S(1)}, u32[]{:S(2)}, u32[]{:S(2)}) async-start(f32[32,4,4,8,128]{4,3,2,1,0:T(8,128)} %bitcast.37), calls=%async_computation | async-start | bytes 4194304 | tf_op jit(solution)/shard_map/all_to_all | solution.py:26
  67.1 0.0 all-gather.9.cloned.1.call-start
  67.2 0.8 slice.20
  68.0 0.7 pad.4
  68.6 0.0 all-gather.9.cloned.1.call-update
  68.7 26.8 %all-to-all-done = f32[32,4,4,8,128]{4,3,2,1,0:T(8,128)S(1)} async-done(((f32[32,4,4,8,128]{4,3,2,1,0:T(8,128)}), f32[32,4,4,8,128]{4,3,2,1,0:T(8,128)S(1)}, u32[]{:S(2)}, u32[]{:S(2)}) %all-to-all-start) | async-done | bytes 2097184 | tf_op jit(solution)/shard_map/all_to_all | solution.py:26
  95.4 0.0 copy-start
  95.4 0.2 reduce_sum.72
  95.7 0.8 copy.16
  96.5 3.5 %all-to-all-start.1 = ((f32[4,8,4,8,128]{4,3,2,1,0:T(8,128)}), f32[4,8,4,8,128]{4,3,2,1,0:T(8,128)S(1)}, u32[]{:S(2)}, u32[]{:S(2)}) async-start(f32[4,8,4,8,128]{4,3,2,1,0:T(8,128)} %copy.16), calls=%async_computation.1 | async-start | bytes 1048576 | tf_op jit(solution)/shard_map/all_to_all | solution.py:26
  100.0 0.0 copy-done
  100.0 0.6 reduce_sum.74
  101.3 1.3 all-gather.9.cloned.1.call-done
  102.5 1.0 slice_convert_fusion
  103.6 0.2 reshape.80
  103.8 0.1 slice_add_fusion
  103.9 10.1 %all-to-all-done.1 = f32[4,8,4,8,128]{4,3,2,1,0:T(8,128)S(1)} async-done(((f32[4,8,4,8,128]{4,3,2,1,0:T(8,128)}), f32[4,8,4,8,128]{4,3,2,1,0:T(8,128)S(1)}, u32[]{:S(2)}, u32[]{:S(2)}) %all-to-all-start.1) | async-done | bytes 524320 | tf_op jit(solution)/shard_map/all_to_all | solution.py:26
  114.0 0.1 copy.18
  114.1 0.3 fusion.2
  114.4 12.8 %all_to_all.40 = f32[16,8,256]{2,1,0:T(8,128)S(1)} all-to-all(f32[16,8,256]{2,1,0:T(8,128)S(1)} %fusion.2), channel_id=1, replica_groups=mesh['zl'=4,'x'=4,'y'=4,'zh'=4,'c'=2] {'zl','x'}, dimensions={0} | all-to-all | bytes 262144 | tf_op jit(solution)/shard_map/all_to_all | solution.py:26
  127.2 10.8 %all_to_all.41 = f32[16,8,256]{2,1,0:T(8,128)S(1)} all-to-all(f32[16,8,256]{2,1,0:T(8,128)S(1)} %broadcast_in_dim.8), channel_id=1, replica_groups=mesh['zl'=4,'x'=4,'y'=4,'zh'=4,'c'=2] {'zl','x'}, dimensions={0} | all-to-all | bytes 262144 | tf_op jit(solution)/shard_map/all_to_all | solution.py:26
  138.0 0.4 fusion
  138.4 12.0 %all_to_all.42 = f32[8,32,256]{2,1,0:T(8,128)S(1)} all-to-all(f32[8,32,256]{2,1,0:T(8,128)S(1)} %fusion), channel_id=1, replica_groups=mesh['zl'=4,'x'=4,'y'=4,'zh'=4,'c'=2] {'y','c'}, dimensions={0} | all-to-all | bytes 524288 | tf_op jit(solution)/shard_map/all_to_all | solution.py:26
  150.4 14.9 %all-gather.3 = f32[128,256]{1,0:T(8,128)S(1)} all-gather(f32[32,256]{1,0:T(8,128)S(1)} %reduce_sum.76), channel_id=5, replica_groups=mesh['zl'=4,'x'=4,'y'=4,'zh'=4,'c'=2] {'zh'}, dimensions={0}, use_global_device_ids=true | all-gather | bytes 163840 | tf_op jit(solution)/shard_map/all_gather | solution.py:222
  165.3 0.4 convolution_bitcast_fusion
  165.7 16.0 %all_to_all.43 = f32[32,8,256]{2,1,0:T(8,128)S(1)} all-to-all(f32[32,8,256]{2,1,0:T(8,128)S(1)} %convolution_bitcast_fusion), channel_id=1, replica_groups=mesh['zl'=4,'x'=4,'y'=4,'zh'=4,'c'=2] {'x','y','c'}, dimensions={0} | all-to-all | bytes 524288 | tf_op jit(solution)/shard_map/all_to_all | solution.py:26
  181.7 6.9 %all_to_all.44 = f32[4,8,256]{2,1,0:T(8,128)S(1)} all-to-all(f32[4,8,256]{2,1,0:T(8,128)S(1)} %broadcast_in_dim.9), channel_id=1, replica_groups=mesh['zl'=4,'x'=4,'y'=4,'zh'=4,'c'=2] {'zl'}, dimensions={0} | all-to-all | bytes 65536 | tf_op jit(solution)/shard_map/all_to_all | solution.py:26
  188.6 0.7 broadcast_in_dim.10
  189.3 4.9 %all-to-all-start.7 = ((f32[32,8,256]{2,1,0:T(8,128)}), f32[32,8,256]{2,1,0:T(8,128)S(1)}, u32[]{:S(2)}, u32[]{:S(2)}) async-start(f32[32,8,256]{2,1,0:T(8,128)} %broadcast_in_dim.10), calls=%async_computation.7 | async-start | bytes 524288 | tf_op jit(solution)/shard_map/all_to_all | solution.py:26
  194.2 0.8 copy.19
  195.0 8.3 %all-to-all-done.7 = f32[32,8,256]{2,1,0:T(8,128)S(1)} async-done(((f32[32,8,256]{2,1,0:T(8,128)}), f32[32,8,256]{2,1,0:T(8,128)S(1)}, u32[]{:S(2)}, u32[]{:S(2)}) %all-to-all-start.7) | async-done | bytes 262176 | tf_op jit(solution)/shard_map/all_to_all | solution.py:26
  203.3 8.3 %solve.1 = f32[8,256]{1,0:T(8,128)} custom-call(s32[1]{0:T(128)} %bitcast.9.place_ref, f32[256,256]{1,0:T(8,128)S(1)} %bitcast.36, f32[32,256]{1,0:T(8,128)S(1)} %broadcast_multiply_fusion.rows_ref), custom_call_target="tpu_custom_call" | custom-call | tf_op jit(solution)/shard_map/solve/pallas_call | solution.py:102
  (13 shorter events, 0.2 us)
Async XLA Ops:
  7.2 44.5 %all-gather.7.cloned.1.call-start = ((), (), s32[]{:S(2)}) async-start(), calls=%async_computation.8 | async-start | bytes 1769472 | tf_op jit(solution)/shard_map/all_gather | solution.py:196
  56.2 39.3 %all-to-all-start = ((f32[32,4,4,8,128]{4,3,2,1,0:T(8,128)}), f32[32,4,4,8,128]{4,3,2,1,0:T(8,128)S(1)}, u32[]{:S(2)}, u32[]{:S(2)}) async-start(f32[32,4,4,8,128]{4,3,2,1,0:T(8,128)} %bitcast.37), calls=%async_computation | async-start | bytes 4194304 | tf_op jit(solution)/shard_map/all_to_all | solution.py:26
  67.1 35.4 %all-gather.9.cloned.1.call-start = ((), (), s32[]{:S(2)}) async-start(), calls=%async_computation.9 | async-start | bytes 1179648 | tf_op jit(solution)/shard_map/all_gather | solution.py:199
  95.4 4.6 %copy-start = (s32[16]{0:T(128)S(1)}, s32[16]{0:T(128)}, u32[]{:S(2)}) copy-start(s32[16]{0:T(128)} %counts_ref.1) | copy-start | bytes 196
  96.5 17.4 %all-to-all-start.1 = ((f32[4,8,4,8,128]{4,3,2,1,0:T(8,128)}), f32[4,8,4,8,128]{4,3,2,1,0:T(8,128)S(1)}, u32[]{:S(2)}, u32[]{:S(2)}) async-start(f32[4,8,4,8,128]{4,3,2,1,0:T(8,128)} %copy.16), calls=%async_computation.1 | async-start | bytes 1048576 | tf_op jit(solution)/shard_map/all_to_all | solution.py:26
  189.3 14.0 %all-to-all-start.7 = ((f32[32,8,256]{2,1,0:T(8,128)}), f32[32,8,256]{2,1,0:T(8,128)S(1)}, u32[]{:S(2)}, u32[]{:S(2)}) async-start(f32[32,8,256]{2,1,0:T(8,128)} %broadcast_in_dim.10), calls=%async_computation.7 | async-start | bytes 524288 | tf_op jit(solution)/shard_map/all_to_all | solution.py:26
Sparse Core Ops, SparseCore 0:
  10.1 37.6 all-gather.6
  70.7 31.7 all-gather.8

commit v9 on v8

--- a/solution.py
+++ b/solution.py
@@ -31,11 +31,11 @@
     return exchange(jnp.broadcast_to(block[None], (size,) + block.shape), axes)
 
 
-def solve_kernel(place_ref, gram_ref, rows_ref, out_ref, held_ref, *, scale_by):
+def solve_kernel(gram_ref, rows_ref, out_ref, held_ref, *, scale_by):
     count, rank = out_ref.shape
     width = held_ref.shape[1]
     lanes = width - rank
-    own = rows_ref[pl.ds(pl.multiple_of(place_ref[0] * count, count), count), :]
+    own = rows_ref[pl.ds(pl.multiple_of(lax.axis_index("zh") * count, count), count), :]
     gram = gram_ref[...]
     diagonal = lax.broadcasted_iota(jnp.int32, gram.shape, 0) == lax.broadcasted_iota(
         jnp.int32, gram.shape, 1
@@ -96,23 +96,23 @@
     out_ref[...] = held_ref[:, rank:width].T[0:count] * scale_by
 
 
-def solve(gram, rows, place, count, scale_by):
+def solve(gram, rows, count, scale_by):
     rank = rows.shape[1]
     vmem = pl.BlockSpec(memory_space=pltpu.VMEM)
     return pl.pallas_call(
         functools.partial(solve_kernel, scale_by=scale_by),
         out_shape=jax.ShapeDtypeStruct((count, rank), F32),
-        in_specs=[pl.BlockSpec(memory_space=pltpu.SMEM), vmem, vmem],
+        in_specs=[vmem, vmem],
         out_specs=vmem,
         scratch_shapes=[pltpu.VMEM((rank, rank + 128), F32)],
         compiler_params=pltpu.CompilerParams(vmem_limit_bytes=KERNEL_VMEM),
         name="solve",
-    )(place, gram, rows)
+    )(gram, rows)
 
 
 def tile_kernel(
-    place_ref, counts_ref, near_any, across_any, out_any,
-    near_ref, across_ref, out_ref, turned_ref, near_sem, across_sem, out_sem,
+    counts_any, near_any, across_any, out_any,
+    counts_ref, near_ref, across_ref, out_ref, turned_ref, counts_sem, near_sem, across_sem, out_sem,
 ):
     n_zh, tok_rows, width = near_ref.shape
     halves, panels = across_ref.shape[:2]
@@ -133,10 +133,12 @@
         )
         for h in range(halves)
     ]
-    for copy in near_copies + across_copies:
+    counts_copy = pltpu.make_async_copy(counts_any, counts_ref, counts_sem)
+    for copy in [counts_copy] + near_copies + across_copies:
         copy.start()
+    counts_copy.wait()
     token = lax.broadcasted_iota(jnp.int32, (width, tok_rows), 1)
-    live = jnp.where(token < counts_ref[place_ref[0]], 1.0, 0.0).astype(BF16)
+    live = jnp.where(token < counts_ref[lax.axis_index(DP)], 1.0, 0.0).astype(BF16)
     for z in range(n_zh):
         near_copies[z].wait()
         turned_ref[z * width : (z + 1) * width, :] = near_ref[z].T * live
@@ -157,28 +159,29 @@
         copy.wait()
 
 
-def tile(place, counts, near, across, n_zl, n_x, sub_rows):
+def tile(counts, near, across, n_zl, n_x, sub_rows):
     n_zh, width = near.shape[0], near.shape[2]
     panels, tok_rows = across.shape[:2]
     half = panels // 2
-    smem = pl.BlockSpec(memory_space=pltpu.SMEM)
     anywhere = pl.BlockSpec(memory_space=pl.ANY)
     return pl.pallas_call(
         tile_kernel,
         out_shape=jax.ShapeDtypeStruct((n_x, panels, n_zl, n_zh, sub_rows, width), F32),
-        in_specs=[smem, smem, anywhere, anywhere],
+        in_specs=[anywhere, anywhere, anywhere],
         out_specs=anywhere,
         scratch_shapes=[
+            pltpu.SMEM(counts.shape, jnp.int32),
             pltpu.VMEM((n_zh, tok_rows, width), BF16),
             pltpu.VMEM((2, half, tok_rows, width), BF16),
             pltpu.VMEM((2, n_x, half, n_zl, n_zh, sub_rows, width), F32),
             pltpu.VMEM((n_zh * width, tok_rows), BF16),
+            pltpu.SemaphoreType.DMA,
             pltpu.SemaphoreType.DMA((n_zh,)),
             pltpu.SemaphoreType.DMA((2,)),
             pltpu.SemaphoreType.DMA((2,)),
         ],
         name="tile",
-    )(place, counts, near, across)
+    )(counts, near, across)
 
 
 def local(features, sketch, counts):
@@ -202,7 +205,7 @@
     start = (thirds[:, :, 0] + thirds[:, :, 1]) + thirds[:, :, 2]
     start = start.reshape(n_panel * sub_rows, rank)
 
-    sums = tile(lax.axis_index(DP).reshape(1), counts, along_z, across, n_zl, n_x, sub_rows)
+    sums = tile(counts, along_z, across, n_zl, n_x, sub_rows)
     sums = sums.reshape(n_x * n_y * n_c, n_zl, n_zh, sub_rows, width)
     sums = exchange(sums, XYC).reshape(n_x, n_y * n_c, n_zl, n_zh, sub_rows, width)
     sums = jnp.sum(sums, axis=0).transpose(1, 0, 2, 3, 4)
@@ -227,8 +230,7 @@
     gram = jnp.sum(exchange(gram.reshape(n_x * n_y * n_c, -1, rank), XYC), axis=0)
     gram = jnp.sum(gather(gram, ("zl",)), axis=0)
     gram = gather(gram, XYC).reshape(rank, rank)
-    place = lax.axis_index("zh").reshape(1)
-    basis = solve(gram, rows, place, sub_rows, math.sqrt(width * n_panel))
+    basis = solve(gram, rows, sub_rows, math.sqrt(width * n_panel))
     return covariance, basis[None]
 
 

time: 219 us -> 218 us (level)
  no operation moved by 1% of the time
where the time goes in v9:
time: 218 us
  blocking collectives  115 us (53%)
  waiting for transfers between devices  47.1 us (22%)
  starting transfers between devices  19.4 us (9%)
  between operations  14.8 us (7%)
  Pallas kernels  12.1 us (6%)
  local copies, waits for them, and re-layouts  4.14 us (2%)
  other arithmetic  3.78 us (2%)
    all_to_all x5, blocking collectives, exchange(): return lax.all_to_all(blocks, axes, 0, 0, tiled=True)  58.4 us
    all_to_all x3, waiting for transfers between devices, exchange(): return lax.all_to_all(blocks, axes, 0, 0, tiled=True)  45.1 us
    all_gather x1, blocking collectives, local(): along_z = lax.all_gather(jnp.concatenate([features, extra]), 'zh')  42.1 us
    all_to_all x3, starting transfers between devices, exchange(): return lax.all_to_all(blocks, axes, 0, 0, tiled=True)  19.3 us
    all_gather x1, blocking collectives, local(): rows = RAISE * jnp.sum(lax.all_gather(rows, 'zh'), axis=0)  14.9 us
    pallas_call x1, Pallas kernels, solve(): pl.pallas_call(functools.partial(solve_kernel, scale_by=scale_by), out_sh...  8.31 us
  transfers between devices with their start and end apart: 5, of which 4 were waited for; matrix products, arithmetic and copies ran while one was open for 3% of the time, Pallas kernels for 0%

profile of v9, /device:TPU:1, one launch (start us, length us, event | category | flops | bytes accessed | tf_op | source)
XLA Modules:
  0.0 217.8 jit_solution(9153123467941897851)
XLA Ops:
  7.2 0.0 all-gather.7.cloned.1.call-start
  7.2 0.7 all-gather.7.cloned.1.call-update
  7.9 0.7 reduce-precision_convert_fusion.1
  8.6 0.9 pad_maximum_fusion
  9.6 42.1 %all-gather = bf16[3264,128]{1,0:T(8,128)(2,1)} all-gather(bf16[816,128]{1,0:T(8,128)(2,1)S(1)} %pad_maximum_fusion), channel_id=2, replica_groups=mesh['zl'=4,'x'=4,'y'=4,'zh'=4,'c'=2] {'zh'}, dimensions={0}, use_global_device_ids=true | all-gather | bytes 1044480 | tf_op jit(solution)/shard_map/all_gather | solution.py:200
  51.7 0.0 all-gather.7.cloned.1.call-done
  51.7 3.8 %tile.1 = f32[4,8,4,4,8,128]{5,4,3,2,1,0:T(8,128)} custom-call(s32[16]{0:T(128)} %counts_any.1, bf16[4,816,128]{2,1,0:T(8,128)(2,1)} %bitcast.37, bf16[8,768,128]{2,1,0:T(8,128)(2,1)} %bitcast.42), custom_call_target="tpu_custom_call" | custom-call | tf_op jit(solution)/shard_map/tile/pallas_call | solution.py:167
  55.5 10.9 %all-to-all-start = ((f32[32,4,4,8,128]{4,3,2,1,0:T(8,128)}), f32[32,4,4,8,128]{4,3,2,1,0:T(8,128)S(1)}, u32[]{:S(2)}, u32[]{:S(2)}) async-start(f32[32,4,4,8,128]{4,3,2,1,0:T(8,128)} %bitcast.35), calls=%async_computation | async-start | bytes 4194304 | tf_op jit(solution)/shard_map/all_to_all | solution.py:26
  66.5 0.0 all-gather.9.cloned.1.call-start
  66.5 0.8 slice.20
  67.3 0.7 pad.4
  68.0 0.0 all-gather.9.cloned.1.call-update
  68.0 26.8 %all-to-all-done = f32[32,4,4,8,128]{4,3,2,1,0:T(8,128)S(1)} async-done(((f32[32,4,4,8,128]{4,3,2,1,0:T(8,128)}), f32[32,4,4,8,128]{4,3,2,1,0:T(8,128)S(1)}, u32[]{:S(2)}, u32[]{:S(2)}) %all-to-all-start) | async-done | bytes 2097184 | tf_op jit(solution)/shard_map/all_to_all | solution.py:26
  94.8 0.0 copy-start
  94.8 0.2 reduce_sum.72
  95.0 0.8 copy.16
  95.8 3.5 %all-to-all-start.1 = ((f32[4,8,4,8,128]{4,3,2,1,0:T(8,128)}), f32[4,8,4,8,128]{4,3,2,1,0:T(8,128)S(1)}, u32[]{:S(2)}, u32[]{:S(2)}) async-start(f32[4,8,4,8,128]{4,3,2,1,0:T(8,128)} %copy.16), calls=%async_computation.1 | async-start | bytes 1048576 | tf_op jit(solution)/shard_map/all_to_all | solution.py:26
  99.3 0.0 copy-done
  99.3 0.6 reduce_sum.74
  100.6 1.3 all-gather.9.cloned.1.call-done
  101.9 1.0 slice_convert_fusion
  102.9 0.2 reshape.72
  103.1 0.1 slice_add_fusion
  103.2 10.1 %all-to-all-done.1 = f32[4,8,4,8,128]{4,3,2,1,0:T(8,128)S(1)} async-done(((f32[4,8,4,8,128]{4,3,2,1,0:T(8,128)}), f32[4,8,4,8,128]{4,3,2,1,0:T(8,128)S(1)}, u32[]{:S(2)}, u32[]{:S(2)}) %all-to-all-start.1) | async-done | bytes 524320 | tf_op jit(solution)/shard_map/all_to_all | solution.py:26
  113.4 0.1 copy.18
  113.5 0.3 fusion.2
  113.7 12.8 %all_to_all.40 = f32[16,8,256]{2,1,0:T(8,128)S(1)} all-to-all(f32[16,8,256]{2,1,0:T(8,128)S(1)} %fusion.2), channel_id=1, replica_groups=mesh['zl'=4,'x'=4,'y'=4,'zh'=4,'c'=2] {'zl','x'}, dimensions={0} | all-to-all | bytes 262144 | tf_op jit(solution)/shard_map/all_to_all | solution.py:26
  126.5 10.8 %all_to_all.41 = f32[16,8,256]{2,1,0:T(8,128)S(1)} all-to-all(f32[16,8,256]{2,1,0:T(8,128)S(1)} %broadcast_in_dim.8), channel_id=1, replica_groups=mesh['zl'=4,'x'=4,'y'=4,'zh'=4,'c'=2] {'zl','x'}, dimensions={0} | all-to-all | bytes 262144 | tf_op jit(solution)/shard_map/all_to_all | solution.py:26
  137.4 0.4 fusion
  137.7 12.0 %all_to_all.42 = f32[8,32,256]{2,1,0:T(8,128)S(1)} all-to-all(f32[8,32,256]{2,1,0:T(8,128)S(1)} %fusion), channel_id=1, replica_groups=mesh['zl'=4,'x'=4,'y'=4,'zh'=4,'c'=2] {'y','c'}, dimensions={0} | all-to-all | bytes 524288 | tf_op jit(solution)/shard_map/all_to_all | solution.py:26
  149.7 14.9 %all-gather.3 = f32[128,256]{1,0:T(8,128)S(1)} all-gather(f32[32,256]{1,0:T(8,128)S(1)} %reduce_sum.76), channel_id=5, replica_groups=mesh['zl'=4,'x'=4,'y'=4,'zh'=4,'c'=2] {'zh'}, dimensions={0}, use_global_device_ids=true | all-gather | bytes 163840 | tf_op jit(solution)/shard_map/all_gather | solution.py:225
  164.6 0.4 convolution_bitcast_fusion
  165.0 16.0 %all_to_all.43 = f32[32,8,256]{2,1,0:T(8,128)S(1)} all-to-all(f32[32,8,256]{2,1,0:T(8,128)S(1)} %convolution_bitcast_fusion), channel_id=1, replica_groups=mesh['zl'=4,'x'=4,'y'=4,'zh'=4,'c'=2] {'x','y','c'}, dimensions={0} | all-to-all | bytes 524288 | tf_op jit(solution)/shard_map/all_to_all | solution.py:26
  181.1 6.9 %all_to_all.44 = f32[4,8,256]{2,1,0:T(8,128)S(1)} all-to-all(f32[4,8,256]{2,1,0:T(8,128)S(1)} %broadcast_in_dim.9), channel_id=1, replica_groups=mesh['zl'=4,'x'=4,'y'=4,'zh'=4,'c'=2] {'zl'}, dimensions={0} | all-to-all | bytes 65536 | tf_op jit(solution)/shard_map/all_to_all | solution.py:26
  187.9 0.7 broadcast_in_dim.10
  188.7 4.9 %all-to-all-start.7 = ((f32[32,8,256]{2,1,0:T(8,128)}), f32[32,8,256]{2,1,0:T(8,128)S(1)}, u32[]{:S(2)}, u32[]{:S(2)}) async-start(f32[32,8,256]{2,1,0:T(8,128)} %broadcast_in_dim.10), calls=%async_computation.7 | async-start | bytes 524288 | tf_op jit(solution)/shard_map/all_to_all | solution.py:26
  193.5 0.8 copy.19
  194.3 8.3 %all-to-all-done.7 = f32[32,8,256]{2,1,0:T(8,128)S(1)} async-done(((f32[32,8,256]{2,1,0:T(8,128)}), f32[32,8,256]{2,1,0:T(8,128)S(1)}, u32[]{:S(2)}, u32[]{:S(2)}) %all-to-all-start.7) | async-done | bytes 262176 | tf_op jit(solution)/shard_map/all_to_all | solution.py:26
  202.6 8.3 %solve.1 = f32[8,256]{1,0:T(8,128)} custom-call(f32[256,256]{1,0:T(8,128)S(1)} %bitcast.34, f32[32,256]{1,0:T(8,128)S(1)} %broadcast_multiply_fusion.rows_ref), custom_call_target="tpu_custom_call" | custom-call | tf_op jit(solution)/shard_map/solve/pallas_call | solution.py:102
  (13 shorter events, 0.2 us)
Async XLA Ops:
  7.2 44.5 %all-gather.7.cloned.1.call-start = ((), (), s32[]{:S(2)}) async-start(), calls=%async_computation.8 | async-start | bytes 1769472 | tf_op jit(solution)/shard_map/all_gather | solution.py:199
  55.5 39.3 %all-to-all-start = ((f32[32,4,4,8,128]{4,3,2,1,0:T(8,128)}), f32[32,4,4,8,128]{4,3,2,1,0:T(8,128)S(1)}, u32[]{:S(2)}, u32[]{:S(2)}) async-start(f32[32,4,4,8,128]{4,3,2,1,0:T(8,128)} %bitcast.35), calls=%async_computation | async-start | bytes 4194304 | tf_op jit(solution)/shard_map/all_to_all | solution.py:26
  66.5 35.4 %all-gather.9.cloned.1.call-start = ((), (), s32[]{:S(2)}) async-start(), calls=%async_computation.9 | async-start | bytes 1179648 | tf_op jit(solution)/shard_map/all_gather | solution.py:202
  94.8 4.6 %copy-start = (s32[16]{0:T(128)S(1)}, s32[16]{0:T(128)}, u32[]{:S(2)}) copy-start(s32[16]{0:T(128)} %counts_any.1) | copy-start | bytes 196
  95.8 17.4 %all-to-all-start.1 = ((f32[4,8,4,8,128]{4,3,2,1,0:T(8,128)}), f32[4,8,4,8,128]{4,3,2,1,0:T(8,128)S(1)}, u32[]{:S(2)}, u32[]{:S(2)}) async-start(f32[4,8,4,8,128]{4,3,2,1,0:T(8,128)} %copy.16), calls=%async_computation.1 | async-start | bytes 1048576 | tf_op jit(solution)/shard_map/all_to_all | solution.py:26
  188.7 14.0 %all-to-all-start.7 = ((f32[32,8,256]{2,1,0:T(8,128)}), f32[32,8,256]{2,1,0:T(8,128)S(1)}, u32[]{:S(2)}, u32[]{:S(2)}) async-start(f32[32,8,256]{2,1,0:T(8,128)} %broadcast_in_dim.10), calls=%async_computation.7 | async-start | bytes 524288 | tf_op jit(solution)/shard_map/all_to_all | solution.py:26
Sparse Core Ops, SparseCore 0:
  10.1 37.6 all-gather.6
  70.0 31.7 all-gather.8

commit v10 on v9

--- a/solution.py
+++ b/solution.py
@@ -13,8 +13,8 @@
 HIGH = lax.Precision.HIGHEST
 DP = ("zl", "x")
 PANEL = ("y", "zh", "c")
-YC = ("y", "c")
-XYC = ("x", "y", "c")
+CY = ("c", "y")
+XCY = ("x", "c", "y")
 RAISE = 256.0
 KERNEL_VMEM = 16 * 2**20
 PANEL_STEP = 64
@@ -196,10 +196,10 @@
     middle = lax.reduce_precision(rest, 8, 7)
     extra = jnp.stack([high, middle, rest - middle]).astype(BF16).reshape(-1, width)
 
-    across = lax.all_gather(features, YC)
+    across = lax.all_gather(features, CY)
     along_z = lax.all_gather(jnp.concatenate([features, extra]), "zh")
     thirds = along_z[:, tok_rows:].reshape(-1, width)
-    thirds = lax.all_gather(jnp.pad(thirds, ((0, PAD_ROWS - thirds.shape[0]), (0, 0))), YC)
+    thirds = lax.all_gather(jnp.pad(thirds, ((0, PAD_ROWS - thirds.shape[0]), (0, 0))), CY)
     thirds = thirds[:, 0 : n_zh * extra.shape[0]].astype(F32)
     thirds = thirds.reshape(n_y * n_c, n_zh, 3, sub_rows, rank)
     start = (thirds[:, :, 0] + thirds[:, :, 1]) + thirds[:, :, 2]
@@ -207,13 +207,13 @@
 
     sums = tile(counts, along_z, across, n_zl, n_x, sub_rows)
     sums = sums.reshape(n_x * n_y * n_c, n_zl, n_zh, sub_rows, width)
-    sums = exchange(sums, XYC).reshape(n_x, n_y * n_c, n_zl, n_zh, sub_rows, width)
+    sums = exchange(sums, XCY).reshape(n_x, n_y * n_c, n_zl, n_zh, sub_rows, width)
     sums = jnp.sum(sums, axis=0).transpose(1, 0, 2, 3, 4)
     sums = jnp.sum(exchange(sums, ("zl",)), axis=0) / token_total
 
     columns = sums.reshape(n_panel * sub_rows, width)
-    covariance = sums.reshape(n_y, n_c, n_zh, sub_rows, width)
-    covariance = covariance.transpose(4, 0, 2, 1, 3).reshape(width, 1, n_panel * sub_rows)
+    covariance = sums.reshape(n_c, n_y, n_zh, sub_rows, width)
+    covariance = covariance.transpose(4, 1, 2, 0, 3).reshape(width, 1, n_panel * sub_rows)
 
     product = lax.dot_general(
         columns, start, (((0,), (0,)), ((), ())), precision=HIGH, preferred_element_type=F32
@@ -221,15 +221,15 @@
     product = jnp.sum(exchange(product.reshape(n_dp, sub_rows, rank), DP), axis=0)
     product = gather(product, DP).reshape(width, rank)
     product = jnp.dot(columns, product, precision=HIGH, preferred_element_type=F32)
-    rows = jnp.sum(exchange(product.reshape(n_y * n_c, n_zh * sub_rows, rank), YC), axis=0)
+    rows = jnp.sum(exchange(product.reshape(n_y * n_c, n_zh * sub_rows, rank), CY), axis=0)
     rows = RAISE * jnp.sum(lax.all_gather(rows, "zh"), axis=0)
 
     gram = lax.dot_general(
         rows, rows, (((0,), (0,)), ((), ())), precision=HIGH, preferred_element_type=F32
     )
-    gram = jnp.sum(exchange(gram.reshape(n_x * n_y * n_c, -1, rank), XYC), axis=0)
+    gram = jnp.sum(exchange(gram.reshape(n_x * n_y * n_c, -1, rank), XCY), axis=0)
     gram = jnp.sum(gather(gram, ("zl",)), axis=0)
-    gram = gather(gram, XYC).reshape(rank, rank)
+    gram = gather(gram, XCY).reshape(rank, rank)
     basis = solve(gram, rows, sub_rows, math.sqrt(width * n_panel))
     return covariance, basis[None]
 

time: 218 us -> 217 us (level)
    all_to_all x3, waiting for transfers between devices: 45.1 us -> 41.5 us  [exchange(): return lax.all_to_all(blocks, axes, 0, 0, tiled=True)]
    all_gather x1, waiting for transfers between devices: 1.26 us -> 4.02 us  [local(): lax.all_gather(jnp.pad(thirds, ((0, PAD_ROWS - thirds.shape[0]), (0, 0)))...]
where the time goes in v10:
time: 217 us
  blocking collectives  115 us (53%)
  waiting for transfers between devices  46.3 us (21%)
  starting transfers between devices  19.9 us (9%)
  between operations  14.8 us (7%)
  Pallas kernels  12.1 us (6%)
  local copies, waits for them, and re-layouts  4.14 us (2%)
  other arithmetic  3.78 us (2%)
    all_to_all x5, blocking collectives, exchange(): return lax.all_to_all(blocks, axes, 0, 0, tiled=True)  57.5 us
    all_gather x1, blocking collectives, local(): along_z = lax.all_gather(jnp.concatenate([features, extra]), 'zh')  42.1 us
    all_to_all x3, waiting for transfers between devices, exchange(): return lax.all_to_all(blocks, axes, 0, 0, tiled=True)  41.5 us
    all_to_all x3, starting transfers between devices, exchange(): return lax.all_to_all(blocks, axes, 0, 0, tiled=True)  19.9 us
    all_gather x1, blocking collectives, local(): rows = RAISE * jnp.sum(lax.all_gather(rows, 'zh'), axis=0)  15 us
    pallas_call x1, Pallas kernels, solve(): pl.pallas_call(functools.partial(solve_kernel, scale_by=scale_by), out_sh...  8.31 us
  transfers between devices with their start and end apart: 5, of which 4 were waited for; matrix products, arithmetic and copies ran while one was open for 3% of the time, Pallas kernels for 0%

profile of v10, /device:TPU:1, one launch (start us, length us, event | category | flops | bytes accessed | tf_op | source)
XLA Modules:
  0.0 216.7 jit_solution(3122309319474909679)
XLA Ops:
  7.2 0.0 all-gather.7.cloned.1.call-start
  7.2 0.7 all-gather.7.cloned.1.call-update
  7.9 0.7 reduce-precision_convert_fusion.1
  8.6 0.9 pad_maximum_fusion
  9.6 42.1 %all-gather = bf16[3264,128]{1,0:T(8,128)(2,1)} all-gather(bf16[816,128]{1,0:T(8,128)(2,1)S(1)} %pad_maximum_fusion), channel_id=2, replica_groups=mesh['zl'=4,'x'=4,'y'=4,'zh'=4,'c'=2] {'zh'}, dimensions={0}, use_global_device_ids=true | all-gather | bytes 1044480 | tf_op jit(solution)/shard_map/all_gather | solution.py:200
  51.7 0.0 all-gather.7.cloned.1.call-done
  51.7 3.8 %tile.1 = f32[4,8,4,4,8,128]{5,4,3,2,1,0:T(8,128)} custom-call(s32[16]{0:T(128)} %counts_any.1, bf16[4,816,128]{2,1,0:T(8,128)(2,1)} %bitcast.37, bf16[8,768,128]{2,1,0:T(8,128)(2,1)} %bitcast.42), custom_call_target="tpu_custom_call" | custom-call | tf_op jit(solution)/shard_map/tile/pallas_call | solution.py:167
  55.5 10.9 %all-to-all-start = ((f32[32,4,4,8,128]{4,3,2,1,0:T(8,128)}), f32[32,4,4,8,128]{4,3,2,1,0:T(8,128)S(1)}, u32[]{:S(2)}, u32[]{:S(2)}) async-start(f32[32,4,4,8,128]{4,3,2,1,0:T(8,128)} %bitcast.35), calls=%async_computation | async-start | bytes 4194304 | tf_op jit(solution)/shard_map/all_to_all | solution.py:26
  66.5 0.0 all-gather.9.cloned.1.call-start
  66.5 0.8 slice.20
  67.3 0.7 pad.4
  68.0 0.0 all-gather.9.cloned.1.call-update
  68.0 26.1 %all-to-all-done = f32[32,4,4,8,128]{4,3,2,1,0:T(8,128)S(1)} async-done(((f32[32,4,4,8,128]{4,3,2,1,0:T(8,128)}), f32[32,4,4,8,128]{4,3,2,1,0:T(8,128)S(1)}, u32[]{:S(2)}, u32[]{:S(2)}) %all-to-all-start) | async-done | bytes 2097184 | tf_op jit(solution)/shard_map/all_to_all | solution.py:26
  94.1 0.0 copy-start
  94.1 0.2 reduce_sum.72
  94.4 0.8 copy.16
  95.2 3.5 %all-to-all-start.1 = ((f32[4,8,4,8,128]{4,3,2,1,0:T(8,128)}), f32[4,8,4,8,128]{4,3,2,1,0:T(8,128)S(1)}, u32[]{:S(2)}, u32[]{:S(2)}) async-start(f32[4,8,4,8,128]{4,3,2,1,0:T(8,128)} %copy.16), calls=%async_computation.1 | async-start | bytes 1048576 | tf_op jit(solution)/shard_map/all_to_all | solution.py:26
  98.7 0.0 copy-done
  98.7 0.6 reduce_sum.74
  100.0 4.0 %all-gather.9.cloned.1.call-done = bf16[4096,128]{1,0:T(8,128)(2,1)} async-done(((bf16[512,128]{1,0:T(8,128)(2,1)}), bf16[4096,128]{1,0:T(8,128)(2,1)}) %all-gather.9.cloned.1.call-update) | async-done | bytes 1048592 | tf_op jit(solution)/shard_map/all_gather | solution.py:202
  104.0 1.0 slice_convert_fusion
  105.1 0.2 reshape.72
  105.3 0.1 slice_add_fusion
  105.4 7.3 %all-to-all-done.1 = f32[4,8,4,8,128]{4,3,2,1,0:T(8,128)S(1)} async-done(((f32[4,8,4,8,128]{4,3,2,1,0:T(8,128)}), f32[4,8,4,8,128]{4,3,2,1,0:T(8,128)S(1)}, u32[]{:S(2)}, u32[]{:S(2)}) %all-to-all-start.1) | async-done | bytes 524320 | tf_op jit(solution)/shard_map/all_to_all | solution.py:26
  112.7 0.1 copy.18
  112.8 0.3 fusion.2
  113.1 11.8 %all_to_all.40 = f32[16,8,256]{2,1,0:T(8,128)S(1)} all-to-all(f32[16,8,256]{2,1,0:T(8,128)S(1)} %fusion.2), channel_id=1, replica_groups=mesh['zl'=4,'x'=4,'y'=4,'zh'=4,'c'=2] {'zl','x'}, dimensions={0} | all-to-all | bytes 262144 | tf_op jit(solution)/shard_map/all_to_all | solution.py:26
  125.0 10.4 %all_to_all.41 = f32[16,8,256]{2,1,0:T(8,128)S(1)} all-to-all(f32[16,8,256]{2,1,0:T(8,128)S(1)} %broadcast_in_dim.8), channel_id=1, replica_groups=mesh['zl'=4,'x'=4,'y'=4,'zh'=4,'c'=2] {'zl','x'}, dimensions={0} | all-to-all | bytes 262144 | tf_op jit(solution)/shard_map/all_to_all | solution.py:26
  135.4 0.4 fusion
  135.8 13.6 %all_to_all.42 = f32[8,32,256]{2,1,0:T(8,128)S(1)} all-to-all(f32[8,32,256]{2,1,0:T(8,128)S(1)} %fusion), channel_id=1, replica_groups=mesh['zl'=4,'x'=4,'y'=4,'zh'=4,'c'=2] {'c','y'}, dimensions={0} | all-to-all | bytes 524288 | tf_op jit(solution)/shard_map/all_to_all | solution.py:26
  149.4 15.0 %all-gather.3 = f32[128,256]{1,0:T(8,128)S(1)} all-gather(f32[32,256]{1,0:T(8,128)S(1)} %reduce_sum.76), channel_id=5, replica_groups=mesh['zl'=4,'x'=4,'y'=4,'zh'=4,'c'=2] {'zh'}, dimensions={0}, use_global_device_ids=true | all-gather | bytes 163840 | tf_op jit(solution)/shard_map/all_gather | solution.py:225
  164.4 0.4 convolution_bitcast_fusion
  164.8 14.8 %all_to_all.43 = f32[32,8,256]{2,1,0:T(8,128)S(1)} all-to-all(f32[32,8,256]{2,1,0:T(8,128)S(1)} %convolution_bitcast_fusion), channel_id=1, replica_groups=mesh['zl'=4,'x'=4,'y'=4,'zh'=4,'c'=2] {'x','c','y'}, dimensions={0} | all-to-all | bytes 524288 | tf_op jit(solution)/shard_map/all_to_all | solution.py:26
  179.7 6.9 %all_to_all.44 = f32[4,8,256]{2,1,0:T(8,128)S(1)} all-to-all(f32[4,8,256]{2,1,0:T(8,128)S(1)} %broadcast_in_dim.9), channel_id=1, replica_groups=mesh['zl'=4,'x'=4,'y'=4,'zh'=4,'c'=2] {'zl'}, dimensions={0} | all-to-all | bytes 65536 | tf_op jit(solution)/shard_map/all_to_all | solution.py:26
  186.5 0.7 broadcast_in_dim.10
  187.2 5.4 %all-to-all-start.7 = ((f32[32,8,256]{2,1,0:T(8,128)}), f32[32,8,256]{2,1,0:T(8,128)S(1)}, u32[]{:S(2)}, u32[]{:S(2)}) async-start(f32[32,8,256]{2,1,0:T(8,128)} %broadcast_in_dim.10), calls=%async_computation.7 | async-start | bytes 524288 | tf_op jit(solution)/shard_map/all_to_all | solution.py:26
  192.7 0.8 copy.19
  193.5 8.1 %all-to-all-done.7 = f32[32,8,256]{2,1,0:T(8,128)S(1)} async-done(((f32[32,8,256]{2,1,0:T(8,128)}), f32[32,8,256]{2,1,0:T(8,128)S(1)}, u32[]{:S(2)}, u32[]{:S(2)}) %all-to-all-start.7) | async-done | bytes 262176 | tf_op jit(solution)/shard_map/all_to_all | solution.py:26
  201.6 8.3 %solve.1 = f32[8,256]{1,0:T(8,128)} custom-call(f32[256,256]{1,0:T(8,128)S(1)} %bitcast.34, f32[32,256]{1,0:T(8,128)S(1)} %broadcast_multiply_fusion.rows_ref), custom_call_target="tpu_custom_call" | custom-call | tf_op jit(solution)/shard_map/solve/pallas_call | solution.py:102
  (13 shorter events, 0.2 us)
Async XLA Ops:
  7.2 44.5 %all-gather.7.cloned.1.call-start = ((), (), s32[]{:S(2)}) async-start(), calls=%async_computation.8 | async-start | bytes 1769472 | tf_op jit(solution)/shard_map/all_gather | solution.py:199
  55.5 38.6 %all-to-all-start = ((f32[32,4,4,8,128]{4,3,2,1,0:T(8,128)}), f32[32,4,4,8,128]{4,3,2,1,0:T(8,128)S(1)}, u32[]{:S(2)}, u32[]{:S(2)}) async-start(f32[32,4,4,8,128]{4,3,2,1,0:T(8,128)} %bitcast.35), calls=%async_computation | async-start | bytes 4194304 | tf_op jit(solution)/shard_map/all_to_all | solution.py:26
  66.5 37.6 %all-gather.9.cloned.1.call-start = ((), (), s32[]{:S(2)}) async-start(), calls=%async_computation.9 | async-start | bytes 1179648 | tf_op jit(solution)/shard_map/all_gather | solution.py:202
  94.1 4.6 %copy-start = (s32[16]{0:T(128)S(1)}, s32[16]{0:T(128)}, u32[]{:S(2)}) copy-start(s32[16]{0:T(128)} %counts_any.1) | copy-start | bytes 196
  95.2 17.4 %all-to-all-start.1 = ((f32[4,8,4,8,128]{4,3,2,1,0:T(8,128)}), f32[4,8,4,8,128]{4,3,2,1,0:T(8,128)S(1)}, u32[]{:S(2)}, u32[]{:S(2)}) async-start(f32[4,8,4,8,128]{4,3,2,1,0:T(8,128)} %copy.16), calls=%async_computation.1 | async-start | bytes 1048576 | tf_op jit(solution)/shard_map/all_to_all | solution.py:26
  187.2 14.3 %all-to-all-start.7 = ((f32[32,8,256]{2,1,0:T(8,128)}), f32[32,8,256]{2,1,0:T(8,128)S(1)}, u32[]{:S(2)}, u32[]{:S(2)}) async-start(f32[32,8,256]{2,1,0:T(8,128)} %broadcast_in_dim.10), calls=%async_computation.7 | async-start | bytes 524288 | tf_op jit(solution)/shard_map/all_to_all | solution.py:26
Sparse Core Ops, SparseCore 0:
  10.1 37.6 all-gather.6
  70.0 33.9 all-gather.8

commit v11 on v10

--- a/solution.py
+++ b/solution.py
@@ -14,6 +14,7 @@
 DP = ("zl", "x")
 PANEL = ("y", "zh", "c")
 CY = ("c", "y")
+XZ = ("x", "zl")
 XCY = ("x", "c", "y")
 RAISE = 256.0
 KERNEL_VMEM = 16 * 2**20
@@ -218,8 +219,10 @@
     product = lax.dot_general(
         columns, start, (((0,), (0,)), ((), ())), precision=HIGH, preferred_element_type=F32
     )
-    product = jnp.sum(exchange(product.reshape(n_dp, sub_rows, rank), DP), axis=0)
-    product = gather(product, DP).reshape(width, rank)
+    product = product.reshape(n_zl, n_x, sub_rows, rank).transpose(1, 0, 2, 3)
+    product = jnp.sum(exchange(product.reshape(n_dp, sub_rows, rank), XZ), axis=0)
+    product = gather(product, XZ).reshape(n_x, n_zl, sub_rows, rank).transpose(1, 0, 2, 3)
+    product = product.reshape(width, rank)
     product = jnp.dot(columns, product, precision=HIGH, preferred_element_type=F32)
     rows = jnp.sum(exchange(product.reshape(n_y * n_c, n_zh * sub_rows, rank), CY), axis=0)
     rows = RAISE * jnp.sum(lax.all_gather(rows, "zh"), axis=0)

time: 217 us -> 217 us (level)
  no operation moved by 1% of the time
where the time goes in v11:
time: 217 us
  blocking collectives  115 us (53%)
  waiting for transfers between devices  46.3 us (21%)
  starting transfers between devices  19.8 us (9%)
  between operations  14.9 us (7%)
  Pallas kernels  12.1 us (6%)
  local copies, waits for them, and re-layouts  4.16 us (2%)
  other arithmetic  3.78 us (2%)
    all_to_all x5, blocking collectives, exchange(): return lax.all_to_all(blocks, axes, 0, 0, tiled=True)  58 us
    all_gather x1, blocking collectives, local(): along_z = lax.all_gather(jnp.concatenate([features, extra]), 'zh')  42.1 us
    all_to_all x3, waiting for transfers between devices, exchange(): return lax.all_to_all(blocks, axes, 0, 0, tiled=True)  41.5 us
    all_to_all x3, starting transfers between devices, exchange(): return lax.all_to_all(blocks, axes, 0, 0, tiled=True)  19.7 us
    all_gather x1, blocking collectives, local(): rows = RAISE * jnp.sum(lax.all_gather(rows, 'zh'), axis=0)  14.7 us
    pallas_call x1, Pallas kernels, solve(): pl.pallas_call(functools.partial(solve_kernel, scale_by=scale_by), out_sh...  8.31 us
  transfers between devices with their start and end apart: 5, of which 4 were waited for; matrix products, arithmetic and copies ran while one was open for 3% of the time, Pallas kernels for 0%

profile of v11, /device:TPU:1, one launch (start us, length us, event | category | flops | bytes accessed | tf_op | source)
XLA Modules:
  0.0 216.8 jit_solution(8903391845164878603)
XLA Ops:
  7.2 0.0 all-gather.7.cloned.1.call-start
  7.2 0.7 all-gather.7.cloned.1.call-update
  7.9 0.7 reduce-precision_convert_fusion.1
  8.6 0.9 pad_maximum_fusion
  9.6 42.1 %all-gather = bf16[3264,128]{1,0:T(8,128)(2,1)} all-gather(bf16[816,128]{1,0:T(8,128)(2,1)S(1)} %pad_maximum_fusion), channel_id=2, replica_groups=mesh['zl'=4,'x'=4,'y'=4,'zh'=4,'c'=2] {'zh'}, dimensions={0}, use_global_device_ids=true | all-gather | bytes 1044480 | tf_op jit(solution)/shard_map/all_gather | solution.py:201
  51.7 0.0 all-gather.7.cloned.1.call-done
  51.7 3.8 %tile.1 = f32[4,8,4,4,8,128]{5,4,3,2,1,0:T(8,128)} custom-call(s32[16]{0:T(128)} %counts_any.1, bf16[4,816,128]{2,1,0:T(8,128)(2,1)} %bitcast.43, bf16[8,768,128]{2,1,0:T(8,128)(2,1)} %bitcast.48), custom_call_target="tpu_custom_call" | custom-call | tf_op jit(solution)/shard_map/tile/pallas_call | solution.py:168
  55.5 10.9 %all-to-all-start = ((f32[32,4,4,8,128]{4,3,2,1,0:T(8,128)}), f32[32,4,4,8,128]{4,3,2,1,0:T(8,128)S(1)}, u32[]{:S(2)}, u32[]{:S(2)}) async-start(f32[32,4,4,8,128]{4,3,2,1,0:T(8,128)} %bitcast.41), calls=%async_computation | async-start | bytes 4194304 | tf_op jit(solution)/shard_map/all_to_all | solution.py:27
  66.5 0.0 all-gather.9.cloned.1.call-start
  66.5 0.8 slice.20
  67.3 0.7 pad.4
  68.0 0.0 all-gather.9.cloned.1.call-update
  68.0 26.1 %all-to-all-done = f32[32,4,4,8,128]{4,3,2,1,0:T(8,128)S(1)} async-done(((f32[32,4,4,8,128]{4,3,2,1,0:T(8,128)}), f32[32,4,4,8,128]{4,3,2,1,0:T(8,128)S(1)}, u32[]{:S(2)}, u32[]{:S(2)}) %all-to-all-start) | async-done | bytes 2097184 | tf_op jit(solution)/shard_map/all_to_all | solution.py:27
  94.1 0.0 copy-start
  94.1 0.2 reduce_sum.72
  94.4 0.8 copy.22
  95.2 3.5 %all-to-all-start.1 = ((f32[4,8,4,8,128]{4,3,2,1,0:T(8,128)}), f32[4,8,4,8,128]{4,3,2,1,0:T(8,128)S(1)}, u32[]{:S(2)}, u32[]{:S(2)}) async-start(f32[4,8,4,8,128]{4,3,2,1,0:T(8,128)} %copy.22), calls=%async_computation.1 | async-start | bytes 1048576 | tf_op jit(solution)/shard_map/all_to_all | solution.py:27
  98.7 0.0 copy-done
  98.7 0.6 reduce_sum.74
  100.0 4.0 %all-gather.9.cloned.1.call-done = bf16[4096,128]{1,0:T(8,128)(2,1)} async-done(((bf16[512,128]{1,0:T(8,128)(2,1)}), bf16[4096,128]{1,0:T(8,128)(2,1)}) %all-gather.9.cloned.1.call-update) | async-done | bytes 1048592 | tf_op jit(solution)/shard_map/all_gather | solution.py:203
  104.0 1.0 slice_convert_fusion
  105.1 0.2 reshape.80
  105.3 0.1 slice_add_fusion
  105.4 7.3 %all-to-all-done.1 = f32[4,8,4,8,128]{4,3,2,1,0:T(8,128)S(1)} async-done(((f32[4,8,4,8,128]{4,3,2,1,0:T(8,128)}), f32[4,8,4,8,128]{4,3,2,1,0:T(8,128)S(1)}, u32[]{:S(2)}, u32[]{:S(2)}) %all-to-all-start.1) | async-done | bytes 524320 | tf_op jit(solution)/shard_map/all_to_all | solution.py:27
  112.7 0.1 copy.24
  112.8 0.3 convolution_bitcast_fusion.1
  113.1 11.3 %all_to_all.40 = f32[16,8,256]{2,1,0:T(8,128)S(1)} all-to-all(f32[16,8,256]{2,1,0:T(8,128)S(1)} %bitcast.51), channel_id=1, replica_groups=mesh['zl'=4,'x'=4,'y'=4,'zh'=4,'c'=2] {'x','zl'}, dimensions={0} | all-to-all | bytes 262144 | tf_op jit(solution)/shard_map/all_to_all | solution.py:27
  124.5 10.0 %all_to_all.41 = f32[16,8,256]{2,1,0:T(8,128)S(1)} all-to-all(f32[16,8,256]{2,1,0:T(8,128)S(1)} %broadcast_in_dim.8), channel_id=1, replica_groups=mesh['zl'=4,'x'=4,'y'=4,'zh'=4,'c'=2] {'x','zl'}, dimensions={0} | all-to-all | bytes 262144 | tf_op jit(solution)/shard_map/all_to_all | solution.py:27
  134.5 0.4 fusion
  134.8 13.7 %all_to_all.42 = f32[8,32,256]{2,1,0:T(8,128)S(1)} all-to-all(f32[8,32,256]{2,1,0:T(8,128)S(1)} %fusion), channel_id=1, replica_groups=mesh['zl'=4,'x'=4,'y'=4,'zh'=4,'c'=2] {'c','y'}, dimensions={0} | all-to-all | bytes 524288 | tf_op jit(solution)/shard_map/all_to_all | solution.py:27
  148.6 14.7 %all-gather.3 = f32[128,256]{1,0:T(8,128)S(1)} all-gather(f32[32,256]{1,0:T(8,128)S(1)} %reduce_sum.76), channel_id=5, replica_groups=mesh['zl'=4,'x'=4,'y'=4,'zh'=4,'c'=2] {'zh'}, dimensions={0}, use_global_device_ids=true | all-gather | bytes 163840 | tf_op jit(solution)/shard_map/all_gather | solution.py:228
  163.2 0.4 convolution_bitcast_fusion
  163.7 16.2 %all_to_all.43 = f32[32,8,256]{2,1,0:T(8,128)S(1)} all-to-all(f32[32,8,256]{2,1,0:T(8,128)S(1)} %convolution_bitcast_fusion), channel_id=1, replica_groups=mesh['zl'=4,'x'=4,'y'=4,'zh'=4,'c'=2] {'x','c','y'}, dimensions={0} | all-to-all | bytes 524288 | tf_op jit(solution)/shard_map/all_to_all | solution.py:27
  179.9 6.9 %all_to_all.44 = f32[4,8,256]{2,1,0:T(8,128)S(1)} all-to-all(f32[4,8,256]{2,1,0:T(8,128)S(1)} %broadcast_in_dim.9), channel_id=1, replica_groups=mesh['zl'=4,'x'=4,'y'=4,'zh'=4,'c'=2] {'zl'}, dimensions={0} | all-to-all | bytes 65536 | tf_op jit(solution)/shard_map/all_to_all | solution.py:27
  186.7 0.7 broadcast_in_dim.10
  187.4 5.3 %all-to-all-start.7 = ((f32[32,8,256]{2,1,0:T(8,128)}), f32[32,8,256]{2,1,0:T(8,128)S(1)}, u32[]{:S(2)}, u32[]{:S(2)}) async-start(f32[32,8,256]{2,1,0:T(8,128)} %broadcast_in_dim.10), calls=%async_computation.7 | async-start | bytes 524288 | tf_op jit(solution)/shard_map/all_to_all | solution.py:27
  192.7 0.8 copy.27
  193.5 8.1 %all-to-all-done.7 = f32[32,8,256]{2,1,0:T(8,128)S(1)} async-done(((f32[32,8,256]{2,1,0:T(8,128)}), f32[32,8,256]{2,1,0:T(8,128)S(1)}, u32[]{:S(2)}, u32[]{:S(2)}) %all-to-all-start.7) | async-done | bytes 262176 | tf_op jit(solution)/shard_map/all_to_all | solution.py:27
  201.6 8.3 %solve.1 = f32[8,256]{1,0:T(8,128)} custom-call(f32[256,256]{1,0:T(8,128)S(1)} %bitcast.40, f32[32,256]{1,0:T(8,128)S(1)} %broadcast_multiply_fusion.rows_ref), custom_call_target="tpu_custom_call" | custom-call | tf_op jit(solution)/shard_map/solve/pallas_call | solution.py:103
  (15 shorter events, 0.2 us)
Async XLA Ops:
  7.2 44.5 %all-gather.7.cloned.1.call-start = ((), (), s32[]{:S(2)}) async-start(), calls=%async_computation.8 | async-start | bytes 1769472 | tf_op jit(solution)/shard_map/all_gather | solution.py:200
  55.5 38.6 %all-to-all-start = ((f32[32,4,4,8,128]{4,3,2,1,0:T(8,128)}), f32[32,4,4,8,128]{4,3,2,1,0:T(8,128)S(1)}, u32[]{:S(2)}, u32[]{:S(2)}) async-start(f32[32,4,4,8,128]{4,3,2,1,0:T(8,128)} %bitcast.41), calls=%async_computation | async-start | bytes 4194304 | tf_op jit(solution)/shard_map/all_to_all | solution.py:27
  66.5 37.6 %all-gather.9.cloned.1.call-start = ((), (), s32[]{:S(2)}) async-start(), calls=%async_computation.9 | async-start | bytes 1179648 | tf_op jit(solution)/shard_map/all_gather | solution.py:203
  94.1 4.6 %copy-start = (s32[16]{0:T(128)S(1)}, s32[16]{0:T(128)}, u32[]{:S(2)}) copy-start(s32[16]{0:T(128)} %counts_any.1) | copy-start | bytes 196
  95.2 17.4 %all-to-all-start.1 = ((f32[4,8,4,8,128]{4,3,2,1,0:T(8,128)}), f32[4,8,4,8,128]{4,3,2,1,0:T(8,128)S(1)}, u32[]{:S(2)}, u32[]{:S(2)}) async-start(f32[4,8,4,8,128]{4,3,2,1,0:T(8,128)} %copy.22), calls=%async_computation.1 | async-start | bytes 1048576 | tf_op jit(solution)/shard_map/all_to_all | solution.py:27
  187.4 14.2 %all-to-all-start.7 = ((f32[32,8,256]{2,1,0:T(8,128)}), f32[32,8,256]{2,1,0:T(8,128)S(1)}, u32[]{:S(2)}, u32[]{:S(2)}) async-start(f32[32,8,256]{2,1,0:T(8,128)} %broadcast_in_dim.10), calls=%async_computation.7 | async-start | bytes 524288 | tf_op jit(solution)/shard_map/all_to_all | solution.py:27
Sparse Core Ops, SparseCore 0:
  10.1 37.6 all-gather.6
  70.0 33.9 all-gather.8
